TPU v7x, 32 devices: a whole 2x2x4 slice. The times are simulated.
32 devices in a mesh: ctx: 8 (over y, x, core), fsdp: 4 (over z).
Axes of the slice: x: 2, y: 2, z: 4, core: 2. Of those that a mesh axis runs over, the one named last changes fastest.
Arguments:
- tokens: bfloat16 [8, 2, 256, 768], P('ctx', None, 'fsdp'), may hold values from -6 to 6
- block_owner: int32 [8, 2], replicated, may hold values from 0 to 15, as said below
- first_gain: bfloat16 [768], P('fsdp'), may hold values from 0.099609375 to 1.8984375
- first_shift: bfloat16 [768], P('fsdp'), may hold values from -3 to 3
- mixer_in: bfloat16 [768, 2304], P('fsdp'), may hold values from -0.21875 to 0.21875
- mixer_out: bfloat16 [768, 768], P('fsdp'), may hold values from -3.5 to 3.5
- mixer_bias: bfloat16 [768], P('fsdp'), may hold values from -2 to 2
- second_gain: bfloat16 [768], P('fsdp'), may hold values from 0.099609375 to 1.8984375
- second_shift: bfloat16 [768], P('fsdp'), may hold values from -3 to 3
- up_weight: bfloat16 [3072, 768], P('fsdp'), may hold values from -0.21875 to 0.21875
- up_bias: bfloat16 [3072], P('fsdp'), may hold values from -3 to 3
- down_weight: bfloat16 [3072, 768], P('fsdp'), may hold values from -0.109375 to 0.109375
- down_bias: bfloat16 [768], P('fsdp'), may hold values from -2 to 2
- out_grad: bfloat16 [8, 2, 256, 768], P('ctx', None, 'fsdp'), may hold values from -6 to 6
Outputs:
- block_out: bfloat16 [8, 2, 256, 768], P('ctx', None, 'fsdp')
- tokens_grad: float32 [8, 2, 256, 768], P('ctx', None, 'fsdp')
- first_gain_grad: float32 [768], P('fsdp')
- first_shift_grad: float32 [768], P('fsdp')
- mixer_in_grad: float32 [768, 2304], P('fsdp')
- mixer_out_grad: float32 [768, 768], P('fsdp')
- mixer_bias_grad: float32 [768], P('fsdp')
- second_gain_grad: float32 [768], P('fsdp')
- second_shift_grad: float32 [768], P('fsdp')
- up_weight_grad: float32 [3072, 768], P('fsdp')
- up_bias_grad: float32 [3072], P('fsdp')
- down_weight_grad: float32 [3072, 768], P('fsdp')
- down_bias_grad: float32 [768], P('fsdp')
Inputs may be any that keep to these rules, and one draw needn't show every extreme that they name: `block_owner`: row c holds a block number b < 8 and 15 - b; every block number appears exactly once.
All inputs are finite; a program needn't handle non-finite values.
Results may differ from a plain program's by a relative error of at most 0.028.
Values may be sent and summed in bfloat16 or wider, within the bound.
No kernel may reach another device: no remote copies, remote signals or barrier semaphores. Data moves between devices by JAX's collectives and lax.ppermute only.
A program may use at most 256 MiB of HBM per device.

v0:
```python
import functools

import jax
import jax.numpy as jnp
from jax import lax
from jax.experimental import pallas as pl
from jax.experimental.pallas import tpu as pltpu
from jax.sharding import PartitionSpec as P

HEADS = 12
HEAD_DIM = 64

EPS = 1e-05
MASKED = -1e30
F32 = jnp.float32
BF16 = jnp.bfloat16
VMEM_LIMIT = 56 * 1024 * 1024


def swap(x, axis, mask):
    return lax.ppermute(x, axis, [(i, i ^ mask) for i in range(lax.axis_size(axis))])


def add16(left, right):
    return (left.astype(F32) + right.astype(F32)).astype(BF16)


def z_gather(x):
    return [x] + [swap(x, "fsdp", r) for r in range(1, lax.axis_size("fsdp"))]


def z_exchange(pieces):
    return [pieces[0]] + [swap(pieces[r], "fsdp", r) for r in range(1, len(pieces))]


def z_sum(pieces):
    return sum(piece.astype(F32) for piece in z_exchange(pieces))


def chip_spread(x, chips):
    return [x] + [swap(x, "ctx", 2 * r) for r in range(1, chips)]


def ctx_spread(x):
    held = chip_spread(x, lax.axis_size("ctx") // 2)
    return held + [swap(piece, "ctx", 1) for piece in held]


def ctx_collect(keep, send):
    came = swap(send, "ctx", 1)
    pieces = [add16(keep[r], came[r]) for r in range(keep.shape[0])]
    return sum(
        piece.astype(F32)
        for piece in [pieces[0]] + [swap(pieces[r], "ctx", 2 * r) for r in range(1, len(pieces))]
    )


def pick(stacked, index):
    return lax.dynamic_index_in_dim(stacked, index, 0, keepdims=False)


def shuffle_kernel(table, x_ref, out_ref):
    width = x_ref.shape[2]
    extra = out_ref.shape[2] - width
    for i in range(out_ref.shape[0]):
        out_ref[i, :, :width] = x_ref[table[i]].astype(out_ref.dtype)
        if extra:
            out_ref[i, :, width:] = jnp.zeros((x_ref.shape[1], extra), out_ref.dtype)


def shuffle(x, table, kind, width=None):
    shape = (table.shape[0], x.shape[1], width or x.shape[2])
    return pl.pallas_call(
        shuffle_kernel,
        grid_spec=pltpu.PrefetchScalarGridSpec(
            num_scalar_prefetch=1,
            grid=(),
            in_specs=[pl.BlockSpec(memory_space=pltpu.VMEM)],
            out_specs=pl.BlockSpec(memory_space=pltpu.VMEM),
        ),
        out_shape=jax.ShapeDtypeStruct(shape, kind),
        compiler_params=pltpu.CompilerParams(vmem_limit_bytes=VMEM_LIMIT),
    )(table, x)


def mm(left, right):
    return jnp.dot(left, right, preferred_element_type=F32)


def contract_rows(left, right):
    return lax.dot_general(left, right, (((0,), (0,)), ((), ())), preferred_element_type=F32)


def contract_cols(left, right):
    return lax.dot_general(left, right, (((1,), (1,)), ((), ())), preferred_element_type=F32)


def head_rows(values, at, heads):
    rows = lax.broadcasted_iota(jnp.int32, values.shape, 0) - at
    return [
        jnp.where((rows >= h * HEAD_DIM) & (rows < (h + 1) * HEAD_DIM), values, 0.0).astype(BF16)
        for h in range(heads)
    ]


def head_cols(values, at, heads):
    cols = lax.broadcasted_iota(jnp.int32, values.shape, 1) - at
    return [
        jnp.where((cols >= h * HEAD_DIM) & (cols < (h + 1) * HEAD_DIM), values, 0.0).astype(BF16)
        for h in range(heads)
    ]


def causal_mask(size, flip):
    keys = lax.broadcasted_iota(jnp.int32, (size, size), 0) ^ flip
    queries = lax.broadcasted_iota(jnp.int32, (size, size), 1) ^ flip
    return keys <= queries


def load_pieces(pieces, kv_ref, sems):
    copies = [
        pltpu.make_async_copy(piece, kv_ref.at[pl.ds(2 * i, 2)], sems.at[i])
        for i, piece in enumerate(pieces)
    ]
    for copy in copies:
        copy.start()
    return copies


def attend_kernel(meta, *refs, heads, pieces, groups):
    q_ref = refs[0]
    piece_refs = refs[1 : 1 + pieces]
    outs = refs[1 + pieces : 1 + pieces + groups]
    sum_ref, lse_ref, kv_ref, sems = refs[1 + pieces + groups :]
    size, wide = q_ref.shape[1:]
    slot = size // groups
    count = 2 * pieces
    width = heads * HEAD_DIM
    scale = HEAD_DIM ** (-0.5)
    copies = load_pieces(piece_refs, kv_ref, sems)
    for copy in copies:
        copy.wait()
    for j in range(2):
        block = meta[count + j]
        turned = head_rows(jnp.transpose(q_ref[j].astype(F32)) * scale, 0, heads)

        def visit(place, carry, diagonal):
            keys = kv_ref[place, :, :wide]
            values = jnp.transpose(kv_ref[place, :, 2 * width - wide :].astype(F32)).astype(BF16)
            later = []
            for h in range(heads):
                score = mm(keys, turned[h])
                if diagonal:
                    score = jnp.where(causal_mask(size, meta[count + 2]), score, MASKED)
                top = jnp.max(score, axis=0, keepdims=True)
                if not diagonal:
                    top = jnp.maximum(top, carry[2 * h])
                weight = jnp.exp(score - top)
                total = jnp.sum(weight, axis=0, keepdims=True)
                at = wide - width + h * HEAD_DIM
                gain = mm(values[at : at + HEAD_DIM], weight.astype(BF16))
                spot = slice(h * HEAD_DIM, (h + 1) * HEAD_DIM)
                if not diagonal:
                    fade = jnp.exp(carry[2 * h] - top)
                    total = total + carry[2 * h + 1] * fade
                    gain = gain + sum_ref[j, spot] * fade
                sum_ref[j, spot] = gain
                later += [top, total]
            return tuple(later)

        carry = visit(j, None, True)
        carry = lax.fori_loop(0, block, lambda n, c: visit(meta[n], c, False), carry)
        for h in range(heads):
            spot = slice(h * HEAD_DIM, (h + 1) * HEAD_DIM)
            sum_ref[j, spot] = sum_ref[j, spot] / carry[2 * h + 1]
            lse_ref[j, h : h + 1] = carry[2 * h] + jnp.log(carry[2 * h + 1])
        result = jnp.transpose(sum_ref[j]).astype(BF16)
        for r in range(groups):
            outs[r][j] = result[r * slot : (r + 1) * slot]


def attend_back_kernel(meta, *refs, heads, pieces, groups):
    q_ref = refs[0]
    piece_refs = refs[1 : 1 + pieces]
    grad_refs = refs[1 + pieces : 1 + pieces + groups]
    sum_ref, lse_ref, dq_ref, keep_ref, send_ref, kv_ref, sems, acc_ref, dq_acc = refs[
        1 + pieces + groups :
    ]
    size, wide = q_ref.shape[1:]
    count = 2 * pieces
    width = heads * HEAD_DIM
    pad = wide - width
    scale = HEAD_DIM ** (-0.5)
    copies = load_pieces(piece_refs, kv_ref, sems)
    acc_ref[...] = jnp.zeros_like(acc_ref)
    for copy in copies:
        copy.wait()
    for j in range(2):
        block = meta[count + j]
        query = q_ref[j].astype(F32) * scale
        plain = head_cols(query, 0, heads)
        turned = head_rows(jnp.transpose(query), 0, heads)
        grad = jnp.concatenate([grad_refs[r][j] for r in range(groups)], axis=0)
        grad_turned = jnp.transpose(grad.astype(F32))
        dots = [
            jnp.sum(
                grad_turned[h * HEAD_DIM : (h + 1) * HEAD_DIM]
                * sum_ref[j, h * HEAD_DIM : (h + 1) * HEAD_DIM],
                axis=0,
                keepdims=True,
            )
            for h in range(heads)
        ]
        if pad:
            grad_turned = jnp.concatenate([jnp.zeros((pad, size), F32), grad_turned], axis=0)
        grads = head_cols(jnp.transpose(grad_turned), pad, heads)
        grads_turned = head_rows(grad_turned, pad, heads)
        dq_acc[...] = jnp.zeros_like(dq_acc)

        def visit(place, diagonal):
            keys = kv_ref[place, :, :wide]
            values = kv_ref[place, :, 2 * width - wide :]
            keys_turned = jnp.transpose(keys.astype(F32)).astype(BF16)
            key_grad = jnp.zeros((size, wide), F32)
            value_grad = jnp.zeros((size, wide), F32)
            for h in range(heads):
                score = mm(keys, turned[h])
                if diagonal:
                    score = jnp.where(causal_mask(size, meta[count + 2]), score, MASKED)
                prob = jnp.exp(score - lse_ref[j, h : h + 1])
                prob_grad = mm(values, grads_turned[h])
                score_grad = (prob * (prob_grad - dots[h])).astype(BF16)
                value_grad += mm(prob.astype(BF16), grads[h])
                key_grad += mm(score_grad, plain[h])
                spot = slice(h * HEAD_DIM, (h + 1) * HEAD_DIM)
                dq_acc[spot] += mm(keys_turned[spot], score_grad)
            acc_ref[place, :, :wide] += key_grad
            acc_ref[place, :, 2 * width - wide :] += value_grad

        visit(j, True)

        def step(n, carry):
            visit(meta[n], False)
            return carry

        lax.fori_loop(0, block, step, 0)
        dq_ref[j] = jnp.transpose(dq_acc[...] * scale).astype(BF16)
    for i in range(pieces):
        to_ref = keep_ref if i < pieces // 2 else send_ref
        to_ref[i % (pieces // 2)] = acc_ref[2 * i : 2 * i + 2].astype(BF16)


def in_grad_kernel(meta, normed_ref, grad_ref, late_ref, keep_ref, send_ref, term_ref, *, cut, share):
    term_ref[...] = contract_rows(normed_ref[...], grad_ref[...])
    here, member = meta[0], meta[1]
    fetch, groups, tall, wide = keep_ref.shape
    for core, to_ref in enumerate((keep_ref, send_ref)):
        for r in range(fetch):
            for z in range(groups):
                owner = member ^ z
                start = owner * share + ((here ^ (2 * r + core)) & (2 * fetch - 1)) * cut
                rows = term_ref[pl.ds(pl.multiple_of(start, 8), cut)]
                to_ref[r, z] = jnp.concatenate([rows, late_ref[owner]], axis=0).astype(BF16)


def in_home_kernel(meta, *refs, cut, fetch, part, width):
    pieces, out_ref, late_ref = refs[:-2], refs[-2], refs[-1]
    here, member = meta[0], meta[1]
    groups = pieces[0].shape[0]
    for i, piece in enumerate(pieces):
        r = 2 * (i % fetch) + i // fetch
        start = pl.multiple_of(((here ^ r) & (2 * fetch - 1)) * cut, 8)
        held = [piece[z ^ member].astype(F32) for z in range(groups)]
        for k, home in enumerate((width, 2 * width, 0)):
            whole = jnp.concatenate([h[:cut, k * part : (k + 1) * part] for h in held], axis=1)
            out_ref[pl.ds(start, cut), home : home + width] = whole[:, :width]
        if i == 0:
            late_ref[...] = sum(h[cut:] for h in held)


def in_vmem(kernel, meta, arrays, outs, scratch=(), flops=0, there=()):
    vmem = pl.BlockSpec(memory_space=pltpu.VMEM)
    anywhere = pl.BlockSpec(memory_space=pl.ANY)
    return pl.pallas_call(
        kernel,
        grid_spec=pltpu.PrefetchScalarGridSpec(
            num_scalar_prefetch=1,
            grid=(),
            in_specs=[anywhere if i in there else vmem for i in range(len(arrays))],
            out_specs=[vmem] * len(outs),
            scratch_shapes=list(scratch),
        ),
        out_shape=outs,
        compiler_params=pltpu.CompilerParams(vmem_limit_bytes=VMEM_LIMIT),
        cost_estimate=pl.CostEstimate(flops=flops, bytes_accessed=1 << 20, transcendentals=0),
    )(meta, *arrays)


def norm_parts(values):
    center = values - jnp.mean(values, axis=-1, keepdims=True)
    rate = lax.rsqrt(jnp.mean(center * center, axis=-1, keepdims=True) + EPS)
    return center * rate, rate


def norm_back(unit, rate, gain, grad):
    e = gain * grad
    return rate * (
        e
        - jnp.mean(e, axis=-1, keepdims=True)
        - unit * jnp.mean(e * unit, axis=-1, keepdims=True)
    )


def after(x, *others):
    return lax.optimization_barrier((x,) + others)[0]


def per_device(
    tokens,
    block_owner,
    first_gain,
    first_shift,
    mixer_in,
    mixer_out,
    mixer_bias,
    second_gain,
    second_shift,
    up_weight,
    up_bias,
    down_weight,
    down_bias,
    out_grad,
):
    groups = lax.axis_size("fsdp")
    member = lax.axis_index("fsdp")
    n_ctx = lax.axis_size("ctx")
    here = lax.axis_index("ctx")
    slot, width = tokens.shape[2:]
    block_len = slot * groups
    local_rows = 2 * slot
    count_rows = 2 * block_len
    blocks = 2 * n_ctx
    share = width // groups
    hidden = up_weight.shape[0]
    hidden_cut = hidden // n_ctx
    heads = -(-HEADS // groups)
    part = heads * HEAD_DIM
    wide = -(-part // 128) * 128
    chips = n_ctx // 2
    fetch = max(f for f in (1, 2, 4, 8, 16) if f <= chips and share % (16 * f) == 0)
    fold = max(f for f in (1, 2, 4, 8, 16) if f <= chips and share % (16 * f) == 0)
    chip = (here // 2) % fetch
    cut = share // (2 * fold)
    spread_f = jnp.arange(groups, dtype=jnp.int32)
    spread_c = jnp.arange(n_ctx, dtype=jnp.int32)
    spread_h = jnp.arange(fetch, dtype=jnp.int32)

    own = tokens.reshape(2, slot, width)
    rows = own.reshape(local_rows, width).astype(F32)
    grad16 = out_grad.reshape(2, slot, width)
    place_index = jnp.stack([here, member]).astype(jnp.int32)

    group_tokens = jnp.stack(z_gather(own), axis=1).reshape(count_rows, width)
    in_cut = lax.dynamic_slice_in_dim(mixer_in, chip * (share // fetch), share // fetch, 0)
    in_cut = in_cut.reshape(-1, 3, width)
    in_cut = jnp.pad(in_cut, ((0, 0), (0, 0), (0, groups * part - width)))
    in_cut = in_cut.reshape(-1, 3, groups, part)
    in_cut = jnp.stack([in_cut[:, 1], in_cut[:, 2], in_cut[:, 0]], axis=2)
    in_cut = in_cut.transpose(1, 0, 2, 3).reshape(groups, share // fetch, 3 * part)
    norm_row = jnp.pad(jnp.concatenate([first_gain, first_shift]), (0, 3 * part - 2 * share))
    norm_rows = jnp.broadcast_to(norm_row, (groups, 16, 3 * part))
    in_cut = jnp.concatenate([in_cut, norm_rows], axis=1)
    in_pieces = jnp.stack(z_exchange([pick(in_cut, member ^ r) for r in range(groups)]))
    norm_nat = jnp.concatenate(
        [pick(in_pieces[:, share // fetch], member ^ r)[None] for r in range(groups)]
    ).astype(F32)
    gain_one = norm_nat[:, :share].reshape(width)
    shift_one = norm_nat[:, share : 2 * share].reshape(width)
    in_parts = jnp.stack(chip_spread(in_pieces[:, : share // fetch], fetch))
    fetch_table = (
        (spread_h[None, :] ^ chip) * groups + (spread_f[:, None] ^ member)
    ).reshape(-1)
    proj_in = shuffle(
        in_parts.reshape(fetch * groups, share // fetch, 3 * part),
        fetch_table,
        BF16,
        2 * part + wide,
    ).reshape(width, 2 * part + wide)

    unit_one, _ = norm_parts(group_tokens.astype(F32))
    normed16 = (unit_one * gain_one + shift_one).astype(BF16)
    mixed = mm(normed16, proj_in).astype(BF16)
    keyval = mixed[:, : 2 * part].reshape(2, block_len, 2 * part)
    query = mixed[:, 2 * part :].reshape(2, block_len, wide)
    keyvals = ctx_spread(keyval)

    owners = block_owner.reshape(-1)
    numbers = jnp.arange(blocks, dtype=jnp.int32)
    places = jnp.sum(jnp.where(owners[None, :] == numbers[:, None], numbers[None, :], 0), axis=1)
    offset = (places // 2) ^ here
    places = (offset % 2) * n_ctx + (offset // 2) * 2 + places % 2
    meta = jnp.concatenate(
        [
            places,
            lax.dynamic_index_in_dim(block_owner, here, 0, keepdims=False),
            (member * slot)[None],
        ]
    ).astype(jnp.int32)

    grads_all = lax.all_gather(grad16.reshape(local_rows, width), "ctx", axis=0, tiled=True)
    order = jnp.concatenate([spread_c[0::2], spread_c[1::2]]) ^ here
    grads_all = shuffle(grads_all.reshape(n_ctx, local_rows, width), order, BF16)
    grads_all = grads_all.reshape(n_ctx * local_rows, width)
    extra = jnp.concatenate([mixer_bias, second_gain, second_shift, down_bias]).reshape(1, 4 * share)
    extra = jnp.concatenate([extra, jnp.pad(up_bias, (0, 4 * share - hidden))[None]])
    extra = jnp.pad(extra, ((0, 14), (0, width - 4 * share)))
    out_pack = after(jnp.concatenate([mixer_out, extra]), group_tokens)
    out_pack = lax.all_gather(out_pack, "fsdp", axis=0, tiled=True)
    out_pack = out_pack.reshape(groups, share + 16, width)
    proj_out = out_pack[:, :share].reshape(width, width)
    mix_bias, gain_two, shift_two, bias_down = (
        out_pack[:, share, i * share : (i + 1) * share].reshape(width).astype(F32)
        for i in range(4)
    )
    up_bias_part = lax.dynamic_slice_in_dim(
        out_pack[:, share + 1], here * hidden_cut, hidden_cut, 1
    ).reshape(groups * hidden_cut)
    ffn_cut = jnp.concatenate(
        [
            lax.dynamic_slice_in_dim(up_weight, here * hidden_cut, hidden_cut, 0),
            lax.dynamic_slice_in_dim(down_weight, here * hidden_cut, hidden_cut, 0),
        ]
    )
    ffn_parts = lax.all_gather(after(ffn_cut, group_tokens), "fsdp", axis=0, tiled=True)
    ffn_parts = ffn_parts.reshape(groups, 2, hidden_cut, width)
    up_part = ffn_parts[:, 0].reshape(groups * hidden_cut, width)
    down_part = ffn_parts[:, 1].reshape(groups * hidden_cut, width)

    attend_flops = 10 * blocks * block_len * block_len * wide * heads
    pair = jax.ShapeDtypeStruct((2, slot, part), BF16)
    results = in_vmem(
        functools.partial(attend_kernel, heads=heads, pieces=n_ctx, groups=groups),
        meta,
        [query] + keyvals,
        [pair] * groups
        + [
            jax.ShapeDtypeStruct((2, part, block_len), F32),
            jax.ShapeDtypeStruct((2, heads, block_len), F32),
        ],
        [
            pltpu.VMEM((blocks, block_len, 2 * part), BF16),
            pltpu.SemaphoreType.DMA((n_ctx,)),
        ],
        attend_flops,
        range(1, 1 + n_ctx),
    )
    sums, lse = results[groups:]
    attended = jnp.stack(z_exchange(results[:groups])).reshape(groups, local_rows, part)
    attend16 = jnp.concatenate([pick(attended, member ^ i) for i in range(groups)], axis=1)
    attend16 = attend16[:, :width]

    resid = rows + (mm(attend16, proj_out) + mix_bias)
    unit_two, rate_two = norm_parts(resid)
    second16 = (unit_two * gain_two + shift_two).astype(BF16)

    second_all = jnp.concatenate(ctx_spread(second16))
    pre = contract_cols(second_all, up_part) + up_bias_part.astype(F32)
    act, gate_pull = jax.vjp(functools.partial(jax.nn.gelu, approximate=True), pre)
    act16 = act.astype(BF16)
    pre_grad = gate_pull(contract_cols(grads_all, down_part))[0].astype(BF16)
    second_part = mm(pre_grad, up_part).astype(BF16).reshape(2, chips, local_rows, width)
    second_grad = ctx_collect(second_part[0], second_part[1])
    resid_grad = grad16.reshape(local_rows, width).astype(F32) + norm_back(
        unit_two, rate_two, gain_two, second_grad
    )
    branch_grad16 = resid_grad.astype(BF16)
    attend_grad = contract_cols(branch_grad16, proj_out).astype(BF16)
    attend_grad = jnp.pad(attend_grad, ((0, 0), (0, groups * part - width)))
    attend_grad = attend_grad.reshape(2, slot, groups, part).transpose(2, 0, 1, 3)
    attend_grads = z_exchange([pick(attend_grad, member ^ r) for r in range(groups)])

    half = jax.ShapeDtypeStruct((chips, 2, block_len, 2 * part), BF16)
    query_grad, keyval_keep, keyval_send = in_vmem(
        functools.partial(attend_back_kernel, heads=heads, pieces=n_ctx, groups=groups),
        meta,
        [query] + keyvals + attend_grads + [sums, lse],
        [jax.ShapeDtypeStruct((2, block_len, part), BF16), half, half],
        [
            pltpu.VMEM((blocks, block_len, 2 * part), BF16),
            pltpu.SemaphoreType.DMA((n_ctx,)),
            pltpu.VMEM((blocks, block_len, 2 * part), F32),
            pltpu.VMEM((part, block_len), F32),
        ],
        attend_flops,
        range(1, 1 + n_ctx),
    )
    keyval_grad = ctx_collect(keyval_keep, keyval_send).astype(BF16)
    mixed_grad = jnp.concatenate(
        [keyval_grad.reshape(count_rows, 2 * part), query_grad.reshape(count_rows, part)], axis=1
    )
    normed_part = contract_cols(mixed_grad, proj_in[:, : 3 * part])
    normed_pieces = normed_part.astype(BF16).reshape(2, groups, slot, width)
    normed_grad = z_sum([normed_pieces[:, r] for r in range(groups)]).reshape(local_rows, width)
    unit_own, rate_own = norm_parts(rows)
    tokens_grad = resid_grad + norm_back(unit_own, rate_own, gain_one, normed_grad)

    late = jnp.stack([jnp.sum(normed_part * unit_one, axis=0), jnp.sum(normed_part, axis=0)])
    late = late.reshape(2, groups, share).transpose(1, 0, 2).reshape(groups, 1, 2 * share)
    late = jnp.pad(late, ((0, 0), (0, 7), (0, 3 * part - 2 * share)))
    tall = cut + 8
    half = jax.ShapeDtypeStruct((fold, groups, tall, 3 * part), BF16)
    in_keep, in_send = in_vmem(
        functools.partial(in_grad_kernel, cut=cut, share=share),
        place_index,
        [normed16, mixed_grad, late],
        [half, half],
        [pltpu.VMEM((width, 3 * part), F32)],
    )
    in_came = swap(in_send, "ctx", 1)
    in_sums = [add16(in_keep[r], in_came[r]) for r in range(fold)]
    in_term = sum(
        piece.astype(F32)
        for piece in [in_sums[0]] + [swap(in_sums[r], "ctx", 2 * r) for r in range(1, fold)]
    ).astype(BF16)
    mask = 2 * fold
    while mask < n_ctx:
        in_term = add16(in_term, swap(in_term, "ctx", mask))
        mask *= 2
    in_term = jnp.stack(z_exchange([in_term[r] for r in range(groups)]))
    in_held = chip_spread(in_term, fold)
    in_held = in_held + [swap(piece, "ctx", 1) for piece in in_held]
    mixer_in_grad, late = in_vmem(
        functools.partial(in_home_kernel, cut=cut, fetch=fold, part=part, width=width),
        place_index,
        in_held,
        [
            jax.ShapeDtypeStruct((share, 3 * width), F32),
            jax.ShapeDtypeStruct((8, 3 * part), F32),
        ],
    )

    ffn_terms = jnp.concatenate(
        [
            contract_rows(pre_grad, second_all).astype(BF16).reshape(groups, hidden_cut, width),
            contract_rows(act16, grads_all).astype(BF16).reshape(groups, hidden_cut, width),
        ],
        axis=1,
    ).reshape(groups * 2 * hidden_cut, width)
    ffn_term = lax.psum_scatter(ffn_terms, "fsdp", scatter_dimension=0, tiled=True)
    ffn_grads = lax.all_gather(ffn_term, "ctx", axis=0, tiled=True)
    ffn_grads = ffn_grads.reshape(n_ctx, 2, hidden_cut, width).astype(F32)

    feed_part = mm(act16, down_part).astype(BF16).reshape(2, chips, local_rows, width)
    feed_part = after(feed_part, branch_grad16)
    feed = ctx_collect(feed_part[0], feed_part[1])
    block_out = (resid + feed + bias_down).astype(BF16)

    early = jnp.stack(
        [
            jnp.sum(branch_grad16.astype(F32), axis=0),
            jnp.sum(second_grad * unit_two, axis=0),
            jnp.sum(second_grad, axis=0),
            jnp.sum(grad16.reshape(local_rows, width).astype(F32), axis=0),
        ]
    )
    early = early.reshape(4, groups, share).transpose(1, 0, 2).reshape(groups, 1, 4 * share)
    up_bias_terms = jnp.sum(pre_grad.astype(F32), axis=0).reshape(groups, 1, hidden_cut)
    up_bias_terms = lax.dynamic_update_slice(
        jnp.zeros((groups, 1, width), F32), up_bias_terms, (0, 0, here * hidden_cut)
    )
    early = jnp.pad(early, ((0, 0), (0, 0), (0, width - 4 * share)))
    early = jnp.concatenate([early, up_bias_terms, jnp.zeros((groups, 14, width), F32)], axis=1)
    out_term = contract_rows(attend16, branch_grad16).reshape(groups, share, width)
    out_term = jnp.concatenate([out_term, early], axis=1).astype(BF16)
    out_term = out_term.reshape(groups * (share + 16), width)
    out_term = lax.psum_scatter(out_term, "fsdp", scatter_dimension=0, tiled=True)
    out_term = lax.psum(out_term, "ctx").astype(F32)

    return (
        block_out.reshape(1, 2, slot, width),
        tokens_grad.reshape(1, 2, slot, width),
        late[0, :share],
        late[0, share : 2 * share],
        mixer_in_grad,
        out_term[:share],
        out_term[share, :share],
        out_term[share, share : 2 * share],
        out_term[share, 2 * share : 3 * share],
        ffn_grads[:, 0].reshape(hidden, width),
        out_term[share + 1, :hidden],
        ffn_grads[:, 1].reshape(hidden, width),
        out_term[share, 3 * share : 4 * share],
    )


def solution(mesh):
    in_specs = (
        P("ctx", None, "fsdp", None),
        P(),
        P("fsdp"),
        P("fsdp"),
        P("fsdp", None),
        P("fsdp", None),
        P("fsdp"),
        P("fsdp"),
        P("fsdp"),
        P("fsdp", None),
        P("fsdp"),
        P("fsdp", None),
        P("fsdp"),
        P("ctx", None, "fsdp", None),
    )
    out_specs = (
        P("ctx", None, "fsdp", None),
        P("ctx", None, "fsdp", None),
        P("fsdp"),
        P("fsdp"),
        P("fsdp", None),
        P("fsdp", None),
        P("fsdp"),
        P("fsdp"),
        P("fsdp"),
        P("fsdp", None),
        P("fsdp"),
        P("fsdp", None),
        P("fsdp"),
    )
    return jax.shard_map(
        per_device, mesh=mesh, in_specs=in_specs, out_specs=out_specs, check_vma=False
    )
```

profile of v0, /device:TPU:0, one launch (start us, length us, event | category | flops | bytes accessed | tf_op | source)
XLA Modules:
  0.0 345.2 jit_solution(6707338214770180959)
XLA Ops:
  7.2 5.1 %collective-permute-start.2 = (bf16[2,64,768]{2,1,0:T(8,128)(2,1)}, bf16[2,64,768]{2,1,0:T(8,128)(2,1)S(1)}, u32[]{:S(2)}, u32[]{:S(2)}) collective-permute-start(bf16[2,64,768]{2,1,0:T(8,128)(2,1)} %bitcast.258), channel_id=1, source_target_pairs={{0,3},{1,2},{2,1},{3,0},{4,7},{5,6},{6,5},{7,4},{8,11},{9,10},{10,... | collective-permute-start | bytes 589832 | tf_op jit(solution)/shard_map/ppermute | solution.py:21
  16.2 2.2 collective-permute-done.2
  18.4 10.8 %collective-permute-done.1 = bf16[2,64,768]{2,1,0:T(8,128)(2,1)S(1)} collective-permute-done((bf16[2,64,768]{2,1,0:T(8,128)(2,1)}, bf16[2,64,768]{2,1,0:T(8,128)(2,1)S(1)}, u32[]{:S(2)}, u32[]{:S(2)}) %collective-permute-start.1) | collective-permute-done | bytes 196640 | tf_op jit(solution)/shard_map/ppermute | solution.py:21
  32.0 3.0 collective-permute-start.4
  46.2 3.9 %collective-permute-done.6 = bf16[4,48,576]{2,1,0:T(8,128)(2,1)S(1)} collective-permute-done((bf16[4,48,576]{2,1,0:T(8,128)(2,1)S(1)}, bf16[4,48,576]{2,1,0:T(8,128)(2,1)S(1)}, u32[]{:S(2)}, u32[]{:S(2)}) %collective-permute-start.6) | collective-permute-done | bytes 221216 | tf_op jit(solution)/shard_map/ppermute | solution.py:21
  50.0 3.8 %collective-permute-done.7 = bf16[4,48,576]{2,1,0:T(8,128)(2,1)S(1)} collective-permute-done((bf16[4,48,576]{2,1,0:T(8,128)(2,1)S(1)}, bf16[4,48,576]{2,1,0:T(8,128)(2,1)S(1)}, u32[]{:S(2)}, u32[]{:S(2)}) %collective-permute-start.7) | collective-permute-done | bytes 221216 | tf_op jit(solution)/shard_map/ppermute | solution.py:21
  55.0 3.0 shard_map.237
  58.0 2.0 convolution_convert_fusion.3
  64.3 8.8 %collective-permute-done.11.refs_4_ = bf16[2,256,384]{2,1,0:T(8,128)(2,1)S(1)} collective-permute-done((bf16[2,256,384]{2,1,0:T(8,128)(2,1)S(1)}, bf16[2,256,384]{2,1,0:T(8,128)(2,1)S(1)}, u32[]{:S(2)}, u32[]{:S(2)}) %collective-permute-start.11) | collective-permute-done | bytes 393248 | tf_op jit(solution)/shard_map/ppermute | solution.py:21
  73.1 4.3 %collective-permute-done.10.refs_3_ = bf16[2,256,384]{2,1,0:T(8,128)(2,1)S(1)} collective-permute-done((bf16[2,256,384]{2,1,0:T(8,128)(2,1)S(1)}, bf16[2,256,384]{2,1,0:T(8,128)(2,1)S(1)}, u32[]{:S(2)}, u32[]{:S(2)}) %collective-permute-start.10) | collective-permute-done | bytes 393248 | tf_op jit(solution)/shard_map/ppermute | solution.py:21
  80.5 20.4 %shard_map.238 = (bf16[2,64,192]{2,1,0:T(8,128)(2,1)}, bf16[2,64,192]{2,1,0:T(8,128)(2,1)}, bf16[2,64,192]{2,1,0:T(8,128)(2,1)}, bf16[2,64,192]{2,1,0:T(8,128)(2...) custom-call(s32[19]{0:T(128)} %pad_add_fusion.meta, bf16[2,256,256]{2,1,0:T(8,128)(2,1)} %bitcast.311, ...), custom_call_target="tpu_custom_call" | custom-call | flops 8053063680 | bytes 1048576 | tf_op jit(solution)/shard_map/pallas_call | solution.py:284
  101.3 4.2 %collective-permute-start.18 = (bf16[2,64,192]{2,1,0:T(8,128)(2,1)}, bf16[2,64,192]{2,1,0:T(8,128)(2,1)S(1)}, u32[]{:S(2)}, u32[]{:S(2)}) collective-permute-start(bf16[2,64,192]{2,1,0:T(8,128)(2,1)} %get-tuple-element.32), channel_id=1, source_target_pairs={{0,3},{1,2},{2,1},{3,0},{4,7},{5,6},{6,5},{7,4},{8,11},{9,10},{10,... | collective-permute-start | bytes 147464 | tf_op jit(solution)/shard_map/ppermute | solution.py:21
  106.4 3.4 collective-permute-done.17
  121.1 5.3 %collective-permute-done.21 = bf16[128,768]{1,0:T(8,128)(2,1)S(1)} collective-permute-done((bf16[128,768]{1,0:T(8,128)(2,1)}, bf16[128,768]{1,0:T(8,128)(2,1)S(1)}, u32[]{:S(2)}, u32[]{:S(2)}) %collective-permute-start.21) | collective-permute-done | bytes 196640 | tf_op jit(solution)/shard_map/ppermute | solution.py:21
  126.4 2.4 collective-permute-done.20
  135.1 3.3 shard_map.239
  138.4 2.5 fusion.85
  141.0 3.1 convert_reduce_fusion.1
  144.0 2.3 convolution_convert_fusion
  146.5 2.3 collective-permute-done.26
  154.5 4.0 %collective-permute-done.27 = bf16[128,768]{1,0:T(8,128)(2,1)} collective-permute-done((bf16[128,768]{1,0:T(8,128)(2,1)}, bf16[128,768]{1,0:T(8,128)(2,1)}, u32[]{:S(2)}, u32[]{:S(2)}) %collective-permute-start.27) | collective-permute-done | bytes 196640 | tf_op jit(solution)/shard_map/ppermute | solution.py:21
  158.6 3.8 %collective-permute-done.29 = bf16[128,768]{1,0:T(8,128)(2,1)} collective-permute-done((bf16[128,768]{1,0:T(8,128)(2,1)}, bf16[128,768]{1,0:T(8,128)(2,1)}, u32[]{:S(2)}, u32[]{:S(2)}) %collective-permute-start.29) | collective-permute-done | bytes 196640 | tf_op jit(solution)/shard_map/ppermute | solution.py:21
  163.6 2.2 multiply_reduce_fusion.1
  166.0 1.9 fusion.76
  171.1 2.6 convolution_convert_fusion.5
  173.7 2.4 convolution_convert_fusion.4
  179.2 2.1 collective-permute-start.34
  184.3 3.6 %collective-permute-done.34.refs_10_ = bf16[2,64,192]{2,1,0:T(8,128)(2,1)S(1)} collective-permute-done((bf16[2,64,192]{2,1,0:T(8,128)(2,1)S(1)}, bf16[2,64,192]{2,1,0:T(8,128)(2,1)S(1)}, u32[]{:S(2)}, u32[]{:S(2)}) %collective-permute-start.34) | collective-permute-done | bytes 49184 | tf_op jit(solution)/shard_map/ppermute | solution.py:21
  187.9 5.2 %collective-permute-done.35.refs_11_ = bf16[2,64,192]{2,1,0:T(8,128)(2,1)S(1)} collective-permute-done((bf16[2,64,192]{2,1,0:T(8,128)(2,1)S(1)}, bf16[2,64,192]{2,1,0:T(8,128)(2,1)S(1)}, u32[]{:S(2)}, u32[]{:S(2)}) %collective-permute-start.35) | collective-permute-done | bytes 49184 | tf_op jit(solution)/shard_map/ppermute | solution.py:21
  193.8 20.4 %shard_map.240 = (bf16[2,256,192]{2,1,0:T(8,128)(2,1)}, bf16[4,2,256,384]{3,2,1,0:T(8,128)(2,1)}, bf16[4,2,256,384]{3,2,1,0:T(8,128)(2,1)}) custom-call(s32[19]{0:T(128)} %pad_add_fusion.meta, bf16[2,256,256]{2,1,0:T(8,128)(2,1)} %bitcast.312, bf16[2,256,384]{2,1,0:T(8,128)(2,1)} %bitcast.307, bf16[2,256,384]{2,1,0:T(8,128)(2,1)} %copy-done.36, ...), custom_call_target="tpu_custom_call" | custom-call | flops 8053063680 | bytes 1048576 | tf_op jit(solution)/shard_map/pallas_call | solution.py:284
  218.7 17.8 %reduce-scatter.5.cloned.1.call-done = bf16[192,768]{1,0:T(8,128)(2,1)} async-done(((bf16[768,768]{1,0:T(8,128)(2,1)}), bf16[192,768]{1,0:T(8,128)(2,1)}) %reduce-scatter.5.cloned.1.call-update) | async-done | bytes 294928 | tf_op jit(solution)/shard_map/reduce_scatter | solution.py:549
  236.5 2.4 fusion.20
  243.4 2.2 fusion.27
  248.6 3.7 %collective-permute-done.38 = bf16[2,256,384]{2,1,0:T(8,128)(2,1)} collective-permute-done((bf16[2,256,384]{2,1,0:T(8,128)(2,1)}, bf16[2,256,384]{2,1,0:T(8,128)(2,1)}, u32[]{:S(2)}, u32[]{:S(2)}) %collective-permute-start.38) | collective-permute-done | bytes 393248 | tf_op jit(solution)/shard_map/ppermute | solution.py:21
  253.9 8.0 %collective-permute-done.40 = bf16[2,256,384]{2,1,0:T(8,128)(2,1)} collective-permute-done((bf16[2,256,384]{2,1,0:T(8,128)(2,1)}, bf16[2,256,384]{2,1,0:T(8,128)(2,1)}, u32[]{:S(2)}, u32[]{:S(2)}) %collective-permute-start.40) | collective-permute-done | bytes 393248 | tf_op jit(solution)/shard_map/ppermute | solution.py:21
  261.9 2.4 collective-permute-done.39
  270.7 3.9 %shard_map.241 = (bf16[4,4,32,576]{3,2,1,0:T(8,128)(2,1)}, bf16[4,4,32,576]{3,2,1,0:T(8,128)(2,1)}) custom-call(s32[2]{0:T(128)} %pad_add_fusion.1.meta, bf16[512,768]{1,0:T(8,128)(2,1)} %get-tuple-element.85.normed_ref, bf16[512,576]{1,0:T(8,128)(2,1)} %pad_maximum_fusion.3.grad_ref, f32[4,8,576]{2,1,0:T(8,128)} %pad.14.late_ref), custom_call_target="tpu_custom_call" | custom-call | bytes 1048576 | tf_op jit(solution)/shard_map/pallas_call | solution.py:284
  276.2 3.0 collective-permute-start.43
  279.2 2.0 add_convert_fusion.5
  281.2 4.4 %collective-permute-done.41 = bf16[2,64,768]{2,1,0:T(8,128)(2,1)S(1)} collective-permute-done((bf16[2,64,768]{2,1,0:T(8,128)(2,1)S(1)}, bf16[2,64,768]{2,1,0:T(8,128)(2,1)S(1)}, u32[]{:S(2)}, u32[]{:S(2)}) %collective-permute-start.41) | collective-permute-done | bytes 196640 | tf_op jit(solution)/shard_map/ppermute | solution.py:21
  285.6 6.3 %collective-permute-done.42 = bf16[2,64,768]{2,1,0:T(8,128)(2,1)S(1)} collective-permute-done((bf16[2,64,768]{2,1,0:T(8,128)(2,1)S(1)}, bf16[2,64,768]{2,1,0:T(8,128)(2,1)S(1)}, u32[]{:S(2)}, u32[]{:S(2)}) %collective-permute-start.42) | collective-permute-done | bytes 196640 | tf_op jit(solution)/shard_map/ppermute | solution.py:21
  295.9 3.7 %collective-permute-done.45 = bf16[4,32,576]{2,1,0:T(8,128)(2,1)S(1)} collective-permute-done((bf16[4,32,576]{2,1,0:T(8,128)(2,1)S(1)}, bf16[4,32,576]{2,1,0:T(8,128)(2,1)S(1)}, u32[]{:S(2)}, u32[]{:S(2)}) %collective-permute-start.45) | collective-permute-done | bytes 147488 | tf_op jit(solution)/shard_map/ppermute | solution.py:21
  304.9 4.3 %collective-permute-start.49 = (bf16[32,576]{1,0:T(8,128)(2,1)S(1)}, bf16[32,576]{1,0:T(8,128)(2,1)S(1)}, u32[]{:S(2)}, u32[]{:S(2)}) collective-permute-start(bf16[32,576]{1,0:T(8,128)(2,1)S(1)} %get-tuple-element.110), channel_id=1, source_target_pairs={{0,2},{1,3},{2,0},{3,1},{4,6},{5,7},{6,4},{7,5},{8,10},{9,11},{10,... | collective-permute-start | bytes 110600 | tf_op jit(solution)/shard_map/ppermute | solution.py:21
  309.4 2.2 collective-permute-done.49
  313.3 2.7 collective-permute-start.53
  317.8 2.8 collective-permute-done.53.refs_3_
  329.1 3.5 %shard_map.242 = (f32[192,2304]{1,0:T(8,128)}, f32[8,576]{1,0:T(8,128)}) custom-call(s32[2]{0:T(128)} %pad_add_fusion.1.meta, bf16[4,32,576]{2,1,0:T(8,128)(2,1)} %copy-done.17, bf16[4,32,576]{2,1,0:T(8,128)(2,1)} %copy-done.26, bf16[4,32,576]{2,1,0:T(8,128)(2,1)} %copy-done.25, bf16[4,32,576]{2,1,0:T(8,128)(2,1)} %copy-done.24, ...), custom_call_target="tpu_custom_call" | custom-call | bytes 1048576 | tf_op jit(solution)/shard_map/pallas_call | solution.py:284
  334.0 4.4 %fusion.79 = (f32[8,1,96,768]{3,2,1,0:T(8,128)}, f32[8,1,96,768]{3,2,1,0:T(8,128)}) fusion(bf16[8,2,96,768]{3,2,1,0:T(8,128)(2,1)} %bitcast.254), kind=kLoop, calls=%fused_computation.242 | loop fusion | bytes 9437184 | tf_op jit(solution)/shard_map/slice | solution.py:591
  (328 shorter events, 105.9 us)
Async XLA Ops:
  7.2 103.6 %all-gather.5.cloned.1.call-start = ((), (), s32[]{:S(2)}) async-start(), calls=%async_computation.2 | async-start | bytes 1597440 | tf_op jit(solution)/shard_map/all_gather | solution.py:418
  7.2 11.2 %collective-permute-start.2 = (bf16[2,64,768]{2,1,0:T(8,128)(2,1)}, bf16[2,64,768]{2,1,0:T(8,128)(2,1)S(1)}, u32[]{:S(2)}, u32[]{:S(2)}) collective-permute-start(bf16[2,64,768]{2,1,0:T(8,128)(2,1)} %bitcast.258), channel_id=1, source_target_pairs={{0,3},{1,2},{2,1},{3,0},{4,7},{5,6},{6,5},{7,4},{8,11},{9,10},{10,... | collective-permute-start | bytes 589832 | tf_op jit(solution)/shard_map/ppermute | solution.py:21
  12.4 16.9 %collective-permute-start.1 = (bf16[2,64,768]{2,1,0:T(8,128)(2,1)}, bf16[2,64,768]{2,1,0:T(8,128)(2,1)S(1)}, u32[]{:S(2)}, u32[]{:S(2)}) collective-permute-start(bf16[2,64,768]{2,1,0:T(8,128)(2,1)} %bitcast.259), channel_id=1, source_target_pairs={{0,2},{1,3},{2,0},{3,1},{4,6},{5,7},{6,4},{7,5},{8,10},{9,11},{10,... | collective-permute-start | bytes 589832 | tf_op jit(solution)/shard_map/ppermute | solution.py:21
  12.4 16.9 %collective-permute-start = (bf16[2,64,768]{2,1,0:T(8,128)(2,1)}, bf16[2,64,768]{2,1,0:T(8,128)(2,1)S(1)}, u32[]{:S(2)}, u32[]{:S(2)}) collective-permute-start(bf16[2,64,768]{2,1,0:T(8,128)(2,1)} %bitcast.260), channel_id=1, source_target_pairs={{0,1},{1,0},{2,3},{3,2},{4,5},{5,4},{6,7},{7,6},{8,9},{9,8},{10,11... | collective-permute-start | bytes 589832 | tf_op jit(solution)/shard_map/ppermute | solution.py:21
  30.4 88.2 %all-gather.7.cloned.1.call-start = ((), (), s32[]{:S(2)}) async-start(), calls=%async_computation.3 | async-start | bytes 1474560 | tf_op jit(solution)/shard_map/all_gather | solution.py:434
  32.0 8.2 %collective-permute-start.4 = (bf16[64,576]{1,0:T(8,128)(2,1)S(1)}, bf16[64,576]{1,0:T(8,128)(2,1)S(1)}, u32[]{:S(2)}, u32[]{:S(2)}) collective-permute-start(bf16[64,576]{1,0:T(8,128)(2,1)S(1)} %get-tuple-element.91), channel_id=1, source_target_pairs={{0,2},{1,3},{2,0},{3,1},{4,6},{5,7},{6,4},{7,5},{8,10},{9,11},{10,... | collective-permute-start | bytes 221192 | tf_op jit(solution)/shard_map/ppermute | solution.py:21
  41.5 8.5 %collective-permute-start.6 = (bf16[4,48,576]{2,1,0:T(8,128)(2,1)S(1)}, bf16[4,48,576]{2,1,0:T(8,128)(2,1)S(1)}, u32[]{:S(2)}, u32[]{:S(2)}) collective-permute-start(bf16[4,48,576]{2,1,0:T(8,128)(2,1)S(1)} %pad_maximum_fusion.7), channel_id=1, source_target_pairs={{0,8},{4,12},{8,0},{12,4},{16,24},{20,28},{24,16},{28,20},{1,9},{5... | collective-permute-start | bytes 663560 | tf_op jit(solution)/shard_map/ppermute | solution.py:21
  43.0 10.8 %collective-permute-start.7 = (bf16[4,48,576]{2,1,0:T(8,128)(2,1)S(1)}, bf16[4,48,576]{2,1,0:T(8,128)(2,1)S(1)}, u32[]{:S(2)}, u32[]{:S(2)}) collective-permute-start(bf16[4,48,576]{2,1,0:T(8,128)(2,1)S(1)} %pad_maximum_fusion.7), channel_id=1, source_target_pairs={{0,16},{4,20},{8,24},{12,28},{16,0},{20,4},{24,8},{28,12},{1,17},{... | collective-permute-start | bytes 663560 | tf_op jit(solution)/shard_map/ppermute | solution.py:21
  44.6 9.3 %collective-permute-start.8 = (bf16[4,48,576]{2,1,0:T(8,128)(2,1)S(1)}, bf16[4,48,576]{2,1,0:T(8,128)(2,1)S(1)}, u32[]{:S(2)}, u32[]{:S(2)}) collective-permute-start(bf16[4,48,576]{2,1,0:T(8,128)(2,1)S(1)} %pad_maximum_fusion.7), channel_id=1, source_target_pairs={{0,24},{4,28},{8,16},{12,20},{16,8},{20,12},{24,0},{28,4},{1,25},{... | collective-permute-start | bytes 663560 | tf_op jit(solution)/shard_map/ppermute | solution.py:21
  45.3 89.8 %all-gather.9.cloned.1.call-start = ((), (), s32[]{:S(2)}) async-start(), calls=%async_computation.4 | async-start | bytes 1769472 | tf_op jit(solution)/shard_map/all_gather | solution.py:410
  60.1 13.0 %collective-permute-start.11 = (bf16[2,256,384]{2,1,0:T(8,128)(2,1)S(1)}, bf16[2,256,384]{2,1,0:T(8,128)(2,1)S(1)}, u32[]{:S(2)}, u32[]{:S(2)}) collective-permute-start(bf16[2,256,384]{2,1,0:T(8,128)(2,1)S(1)} %bitcast.302), channel_id=1, source_target_pairs={{0,24},{4,28},{8,16},{12,20},{16,8},{20,12},{24,0},{28,4},{1,25},{... | collective-permute-start | bytes 1179656 | tf_op jit(solution)/shard_map/ppermute | solution.py:21
  61.7 15.8 %collective-permute-start.10 = (bf16[2,256,384]{2,1,0:T(8,128)(2,1)S(1)}, bf16[2,256,384]{2,1,0:T(8,128)(2,1)S(1)}, u32[]{:S(2)}, u32[]{:S(2)}) collective-permute-start(bf16[2,256,384]{2,1,0:T(8,128)(2,1)S(1)} %bitcast.303), channel_id=1, source_target_pairs={{0,16},{4,20},{8,24},{12,28},{16,0},{20,4},{24,8},{28,12},{1,17},{... | collective-permute-start | bytes 1179656 | tf_op jit(solution)/shard_map/ppermute | solution.py:21
  62.9 14.6 %collective-permute-start.9 = (bf16[2,256,384]{2,1,0:T(8,128)(2,1)S(1)}, bf16[2,256,384]{2,1,0:T(8,128)(2,1)S(1)}, u32[]{:S(2)}, u32[]{:S(2)}) collective-permute-start(bf16[2,256,384]{2,1,0:T(8,128)(2,1)S(1)} %bitcast.304), channel_id=1, source_target_pairs={{0,8},{4,12},{8,0},{12,4},{16,24},{20,28},{24,16},{28,20},{1,9},{5... | collective-permute-start | bytes 1179656 | tf_op jit(solution)/shard_map/ppermute | solution.py:21
  63.7 154.5 %reduce-scatter.3.cloned.1.call-start = ((), (), s32[]{:S(2)}) async-start(), calls=%async_computation.5 | async-start | bytes 1597440 | tf_op jit(solution)/shard_map/reduce_scatter | solution.py:576
  64.3 15.1 %collective-permute-start.12 = (bf16[2,256,384]{2,1,0:T(8,128)(2,1)S(1)}, bf16[2,256,384]{2,1,0:T(8,128)(2,1)S(1)}, u32[]{:S(2)}, u32[]{:S(2)}) collective-permute-start(bf16[2,256,384]{2,1,0:T(8,128)(2,1)S(1)} %bitcast.305), channel_id=1, source_target_pairs={{0,4},{4,0},{8,12},{12,8},{16,20},{20,16},{24,28},{28,24},{1,5},{5... | collective-permute-start | bytes 1179656 | tf_op jit(solution)/shard_map/ppermute | solution.py:21
  101.0 8.8 %collective-permute-start.17 = (bf16[2,64,192]{2,1,0:T(8,128)(2,1)}, bf16[2,64,192]{2,1,0:T(8,128)(2,1)S(1)}, u32[]{:S(2)}, u32[]{:S(2)}) collective-permute-start(bf16[2,64,192]{2,1,0:T(8,128)(2,1)} %get-tuple-element.31), channel_id=1, source_target_pairs={{0,2},{1,3},{2,0},{3,1},{4,6},{5,7},{6,4},{7,5},{8,10},{9,11},{10,... | collective-permute-start | bytes 147464 | tf_op jit(solution)/shard_map/ppermute | solution.py:21
  101.3 8.6 %collective-permute-start.18 = (bf16[2,64,192]{2,1,0:T(8,128)(2,1)}, bf16[2,64,192]{2,1,0:T(8,128)(2,1)S(1)}, u32[]{:S(2)}, u32[]{:S(2)}) collective-permute-start(bf16[2,64,192]{2,1,0:T(8,128)(2,1)} %get-tuple-element.32), channel_id=1, source_target_pairs={{0,3},{1,2},{2,1},{3,0},{4,7},{5,6},{6,5},{7,4},{8,11},{9,10},{10,... | collective-permute-start | bytes 147464 | tf_op jit(solution)/shard_map/ppermute | solution.py:21
  115.1 11.3 %collective-permute-start.21 = (bf16[128,768]{1,0:T(8,128)(2,1)}, bf16[128,768]{1,0:T(8,128)(2,1)S(1)}, u32[]{:S(2)}, u32[]{:S(2)}) collective-permute-start(bf16[128,768]{1,0:T(8,128)(2,1)} %get-tuple-element.65), channel_id=1, source_target_pairs={{0,24},{4,28},{8,16},{12,20},{16,8},{20,12},{24,0},{28,4},{1,25},{... | collective-permute-start | bytes 589832 | tf_op jit(solution)/shard_map/ppermute | solution.py:21
  116.6 12.3 %collective-permute-start.20 = (bf16[128,768]{1,0:T(8,128)(2,1)}, bf16[128,768]{1,0:T(8,128)(2,1)S(1)}, u32[]{:S(2)}, u32[]{:S(2)}) collective-permute-start(bf16[128,768]{1,0:T(8,128)(2,1)} %get-tuple-element.65), channel_id=1, source_target_pairs={{0,16},{4,20},{8,24},{12,28},{16,0},{20,4},{24,8},{28,12},{1,17},{... | collective-permute-start | bytes 589832 | tf_op jit(solution)/shard_map/ppermute | solution.py:21
  117.4 11.4 %collective-permute-start.19 = (bf16[128,768]{1,0:T(8,128)(2,1)}, bf16[128,768]{1,0:T(8,128)(2,1)S(1)}, u32[]{:S(2)}, u32[]{:S(2)}) collective-permute-start(bf16[128,768]{1,0:T(8,128)(2,1)} %get-tuple-element.65), channel_id=1, source_target_pairs={{0,8},{4,12},{8,0},{12,4},{16,24},{20,28},{24,16},{28,20},{1,9},{5... | collective-permute-start | bytes 589832 | tf_op jit(solution)/shard_map/ppermute | solution.py:21
  120.8 10.6 %collective-permute-start.22 = (bf16[128,768]{1,0:T(8,128)(2,1)}, bf16[128,768]{1,0:T(8,128)(2,1)}, u32[]{:S(2)}, u32[]{:S(2)}) collective-permute-start(bf16[128,768]{1,0:T(8,128)(2,1)} %get-tuple-element.65), channel_id=1, source_target_pairs={{0,4},{4,0},{8,12},{12,8},{16,20},{20,16},{24,28},{28,24},{1,5},{5... | collective-permute-start | bytes 589832 | tf_op jit(solution)/shard_map/ppermute | solution.py:21
  126.4 8.0 %collective-permute-start.25 = (bf16[128,768]{1,0:T(8,128)(2,1)S(1)}, bf16[128,768]{1,0:T(8,128)(2,1)S(1)}, u32[]{:S(2)}, u32[]{:S(2)}) collective-permute-start(bf16[128,768]{1,0:T(8,128)(2,1)S(1)} %collective-permute-done.21), channel_id=1, source_target_pairs={{0,4},{4,0},{8,12},{12,8},{16,20},{20,16},{24,28},{28,24},{1,5},{5... | collective-permute-start | bytes 589832 | tf_op jit(solution)/shard_map/ppermute | solution.py:21
  150.5 8.1 %collective-permute-start.27 = (bf16[128,768]{1,0:T(8,128)(2,1)}, bf16[128,768]{1,0:T(8,128)(2,1)}, u32[]{:S(2)}, u32[]{:S(2)}) collective-permute-start(bf16[128,768]{1,0:T(8,128)(2,1)} %get-tuple-element.76), channel_id=1, source_target_pairs={{0,8},{4,12},{8,0},{12,4},{16,24},{20,28},{24,16},{28,20},{1,9},{5... | collective-permute-start | bytes 589832 | tf_op jit(solution)/shard_map/ppermute | solution.py:21
  151.7 10.7 %collective-permute-start.29 = (bf16[128,768]{1,0:T(8,128)(2,1)}, bf16[128,768]{1,0:T(8,128)(2,1)}, u32[]{:S(2)}, u32[]{:S(2)}) collective-permute-start(bf16[128,768]{1,0:T(8,128)(2,1)} %get-tuple-element.77), channel_id=1, source_target_pairs={{0,24},{4,28},{8,16},{12,20},{16,8},{20,12},{24,0},{28,4},{1,25},{... | collective-permute-start | bytes 589832 | tf_op jit(solution)/shard_map/ppermute | solution.py:21
  152.6 10.9 %collective-permute-start.28 = (bf16[128,768]{1,0:T(8,128)(2,1)S(1)}, bf16[128,768]{1,0:T(8,128)(2,1)}, u32[]{:S(2)}, u32[]{:S(2)}) collective-permute-start(bf16[128,768]{1,0:T(8,128)(2,1)S(1)} %get-tuple-element.78), channel_id=1, source_target_pairs={{0,16},{4,20},{8,24},{12,28},{16,0},{20,4},{24,8},{28,12},{1,17},{... | collective-permute-start | bytes 589832 | tf_op jit(solution)/shard_map/ppermute | solution.py:21
  171.1 65.4 %reduce-scatter.5.cloned.1.call-start = ((), (), s32[]{:S(2)}) async-start(), calls=%async_computation.7 | async-start | bytes 1474560 | tf_op jit(solution)/shard_map/reduce_scatter | solution.py:549
  177.2 145.6 %all-reduce.5.cloned.1.call-start = ((), (), s32[]{:S(2)}) async-start(), calls=%async_computation.6 | async-start | bytes 638976 | tf_op jit(solution)/shard_map/psum | solution.py:577
  179.2 8.7 %collective-permute-start.34 = (bf16[2,64,192]{2,1,0:T(8,128)(2,1)S(1)}, bf16[2,64,192]{2,1,0:T(8,128)(2,1)S(1)}, u32[]{:S(2)}, u32[]{:S(2)}) collective-permute-start(bf16[2,64,192]{2,1,0:T(8,128)(2,1)S(1)} %bitcast.323), channel_id=1, source_target_pairs={{0,1},{1,0},{2,3},{3,2},{4,5},{5,4},{6,7},{7,6},{8,9},{9,8},{10,11... | collective-permute-start | bytes 147464 | tf_op jit(solution)/shard_map/ppermute | solution.py:21
  181.3 11.9 %collective-permute-start.35 = (bf16[2,64,192]{2,1,0:T(8,128)(2,1)S(1)}, bf16[2,64,192]{2,1,0:T(8,128)(2,1)S(1)}, u32[]{:S(2)}, u32[]{:S(2)}) collective-permute-start(bf16[2,64,192]{2,1,0:T(8,128)(2,1)S(1)} %bitcast.322), channel_id=1, source_target_pairs={{0,2},{1,3},{2,0},{3,1},{4,6},{5,7},{6,4},{7,5},{8,10},{9,11},{10,... | collective-permute-start | bytes 147464 | tf_op jit(solution)/shard_map/ppermute | solution.py:21
  182.5 10.7 %collective-permute-start.36 = (bf16[2,64,192]{2,1,0:T(8,128)(2,1)S(1)}, bf16[2,64,192]{2,1,0:T(8,128)(2,1)S(1)}, u32[]{:S(2)}, u32[]{:S(2)}) collective-permute-start(bf16[2,64,192]{2,1,0:T(8,128)(2,1)S(1)} %bitcast.321), channel_id=1, source_target_pairs={{0,3},{1,2},{2,1},{3,0},{4,7},{5,6},{6,5},{7,4},{8,11},{9,10},{10,... | collective-permute-start | bytes 147464 | tf_op jit(solution)/shard_map/ppermute | solution.py:21
  214.2 22.3 %collective-permute-start.37 = (bf16[4,2,256,384]{3,2,1,0:T(8,128)(2,1)}, bf16[4,2,256,384]{3,2,1,0:T(8,128)(2,1)}, u32[]{:S(2)}, u32[]{:S(2)}) collective-permute-start(bf16[4,2,256,384]{3,2,1,0:T(8,128)(2,1)} %get-tuple-element.39), channel_id=1, source_target_pairs={{0,4},{4,0},{8,12},{12,8},{16,20},{20,16},{24,28},{28,24},{1,5},{5... | collective-permute-start | bytes 4718600 | tf_op jit(solution)/shard_map/ppermute | solution.py:21
  217.7 25.7 %collective-permute-start.30 = (bf16[4,128,768]{2,1,0:T(8,128)(2,1)}, bf16[4,128,768]{2,1,0:T(8,128)(2,1)}, u32[]{:S(2)}, u32[]{:S(2)}) collective-permute-start(bf16[4,128,768]{2,1,0:T(8,128)(2,1)} %slice_bitcast_fusion), channel_id=1, source_target_pairs={{0,4},{4,0},{8,12},{12,8},{16,20},{20,16},{24,28},{28,24},{1,5},{5... | collective-permute-start | bytes 2359304 | tf_op jit(solution)/shard_map/ppermute | solution.py:21
  218.2 115.8 %all-gather.11.cloned.1.call-start = ((), (), s32[]{:S(2)}) async-start(), calls=%async_computation.8 | async-start | bytes 2654208 | tf_op jit(solution)/shard_map/all_gather | solution.py:550
  238.9 13.4 %collective-permute-start.38 = (bf16[2,256,384]{2,1,0:T(8,128)(2,1)}, bf16[2,256,384]{2,1,0:T(8,128)(2,1)}, u32[]{:S(2)}, u32[]{:S(2)}) collective-permute-start(bf16[2,256,384]{2,1,0:T(8,128)(2,1)} %get-tuple-element.68), channel_id=1, source_target_pairs={{0,8},{4,12},{8,0},{12,4},{16,24},{20,28},{24,16},{28,20},{1,9},{5... | collective-permute-start | bytes 1179656 | tf_op jit(solution)/shard_map/ppermute | solution.py:21
  240.4 21.5 %collective-permute-start.40 = (bf16[2,256,384]{2,1,0:T(8,128)(2,1)}, bf16[2,256,384]{2,1,0:T(8,128)(2,1)}, u32[]{:S(2)}, u32[]{:S(2)}) collective-permute-start(bf16[2,256,384]{2,1,0:T(8,128)(2,1)} %get-tuple-element.69), channel_id=1, source_target_pairs={{0,24},{4,28},{8,16},{12,20},{16,8},{20,12},{24,0},{28,4},{1,25},{... | collective-permute-start | bytes 1179656 | tf_op jit(solution)/shard_map/ppermute | solution.py:21
  241.9 22.5 %collective-permute-start.39 = (bf16[2,256,384]{2,1,0:T(8,128)(2,1)}, bf16[2,256,384]{2,1,0:T(8,128)(2,1)}, u32[]{:S(2)}, u32[]{:S(2)}) collective-permute-start(bf16[2,256,384]{2,1,0:T(8,128)(2,1)} %get-tuple-element.70), channel_id=1, source_target_pairs={{0,16},{4,20},{8,24},{12,28},{16,0},{20,4},{24,8},{28,12},{1,17},{... | collective-permute-start | bytes 1179656 | tf_op jit(solution)/shard_map/ppermute | solution.py:21
  245.6 29.2 %collective-permute-start.31 = (bf16[128,768]{1,0:T(8,128)(2,1)}, bf16[128,768]{1,0:T(8,128)(2,1)S(1)}, u32[]{:S(2)}, u32[]{:S(2)}) collective-permute-start(bf16[128,768]{1,0:T(8,128)(2,1)} %get-tuple-element.73), channel_id=1, source_target_pairs={{0,8},{4,12},{8,0},{12,4},{16,24},{20,28},{24,16},{28,20},{1,9},{5... | collective-permute-start | bytes 589832 | tf_op jit(solution)/shard_map/ppermute | solution.py:21
  247.2 29.0 %collective-permute-start.33 = (bf16[128,768]{1,0:T(8,128)(2,1)}, bf16[128,768]{1,0:T(8,128)(2,1)}, u32[]{:S(2)}, u32[]{:S(2)}) collective-permute-start(bf16[128,768]{1,0:T(8,128)(2,1)} %get-tuple-element.74), channel_id=1, source_target_pairs={{0,24},{4,28},{8,16},{12,20},{16,8},{20,12},{24,0},{28,4},{1,25},{... | collective-permute-start | bytes 589832 | tf_op jit(solution)/shard_map/ppermute | solution.py:21
  252.3 26.8 %collective-permute-start.32 = (bf16[128,768]{1,0:T(8,128)(2,1)}, bf16[128,768]{1,0:T(8,128)(2,1)}, u32[]{:S(2)}, u32[]{:S(2)}) collective-permute-start(bf16[128,768]{1,0:T(8,128)(2,1)} %get-tuple-element.75), channel_id=1, source_target_pairs={{0,16},{4,20},{8,24},{12,28},{16,0},{20,4},{24,8},{28,12},{1,17},{... | collective-permute-start | bytes 589832 | tf_op jit(solution)/shard_map/ppermute | solution.py:21
  274.7 17.6 %collective-permute-start.44 = (bf16[4,4,32,576]{3,2,1,0:T(8,128)(2,1)}, bf16[4,4,32,576]{3,2,1,0:T(8,128)(2,1)S(1)}, u32[]{:S(2)}, u32[]{:S(2)}) collective-permute-start(bf16[4,4,32,576]{3,2,1,0:T(8,128)(2,1)} %get-tuple-element.42), channel_id=1, source_target_pairs={{0,4},{4,0},{8,12},{12,8},{16,20},{20,16},{24,28},{28,24},{1,5},{5... | collective-permute-start | bytes 1769480 | tf_op jit(solution)/shard_map/ppermute | solution.py:21
  274.7 10.9 %collective-permute-start.41 = (bf16[2,64,768]{2,1,0:T(8,128)(2,1)S(1)}, bf16[2,64,768]{2,1,0:T(8,128)(2,1)S(1)}, u32[]{:S(2)}, u32[]{:S(2)}) collective-permute-start(bf16[2,64,768]{2,1,0:T(8,128)(2,1)S(1)} %get-tuple-element.86), channel_id=1, source_target_pairs={{0,1},{1,0},{2,3},{3,2},{4,5},{5,4},{6,7},{7,6},{8,9},{9,8},{10,11... | collective-permute-start | bytes 589832 | tf_op jit(solution)/shard_map/ppermute | solution.py:21
  274.8 17.1 %collective-permute-start.42 = (bf16[2,64,768]{2,1,0:T(8,128)(2,1)S(1)}, bf16[2,64,768]{2,1,0:T(8,128)(2,1)S(1)}, u32[]{:S(2)}, u32[]{:S(2)}) collective-permute-start(bf16[2,64,768]{2,1,0:T(8,128)(2,1)S(1)} %get-tuple-element.87), channel_id=1, source_target_pairs={{0,2},{1,3},{2,0},{3,1},{4,6},{5,7},{6,4},{7,5},{8,10},{9,11},{10,... | collective-permute-start | bytes 589832 | tf_op jit(solution)/shard_map/ppermute | solution.py:21
  276.2 15.8 %collective-permute-start.43 = (bf16[2,64,768]{2,1,0:T(8,128)(2,1)S(1)}, bf16[2,64,768]{2,1,0:T(8,128)(2,1)S(1)}, u32[]{:S(2)}, u32[]{:S(2)}) collective-permute-start(bf16[2,64,768]{2,1,0:T(8,128)(2,1)S(1)} %get-tuple-element.88), channel_id=1, source_target_pairs={{0,3},{1,2},{2,1},{3,0},{4,7},{5,6},{6,5},{7,4},{8,11},{9,10},{10,... | collective-permute-start | bytes 589832 | tf_op jit(solution)/shard_map/ppermute | solution.py:21
  292.4 7.3 %collective-permute-start.45 = (bf16[4,32,576]{2,1,0:T(8,128)(2,1)S(1)}, bf16[4,32,576]{2,1,0:T(8,128)(2,1)S(1)}, u32[]{:S(2)}, u32[]{:S(2)}) collective-permute-start(bf16[4,32,576]{2,1,0:T(8,128)(2,1)S(1)} %get-tuple-element.80), channel_id=1, source_target_pairs={{0,8},{4,12},{8,0},{12,4},{16,24},{20,28},{24,16},{28,20},{1,9},{5... | collective-permute-start | bytes 442376 | tf_op jit(solution)/shard_map/ppermute | solution.py:21
  294.0 7.4 %collective-permute-start.47 = (bf16[4,32,576]{2,1,0:T(8,128)(2,1)S(1)}, bf16[4,32,576]{2,1,0:T(8,128)(2,1)S(1)}, u32[]{:S(2)}, u32[]{:S(2)}) collective-permute-start(bf16[4,32,576]{2,1,0:T(8,128)(2,1)S(1)} %get-tuple-element.81), channel_id=1, source_target_pairs={{0,24},{4,28},{8,16},{12,20},{16,8},{20,12},{24,0},{28,4},{1,25},{... | collective-permute-start | bytes 442376 | tf_op jit(solution)/shard_map/ppermute | solution.py:21
  294.0 8.9 %collective-permute-start.46 = (bf16[4,32,576]{2,1,0:T(8,128)(2,1)S(1)}, bf16[4,32,576]{2,1,0:T(8,128)(2,1)S(1)}, u32[]{:S(2)}, u32[]{:S(2)}) collective-permute-start(bf16[4,32,576]{2,1,0:T(8,128)(2,1)S(1)} %get-tuple-element.82), channel_id=1, source_target_pairs={{0,16},{4,20},{8,24},{12,28},{16,0},{20,4},{24,8},{28,12},{1,17},{... | collective-permute-start | bytes 442376 | tf_op jit(solution)/shard_map/ppermute | solution.py:21
  313.3 7.3 %collective-permute-start.53 = (bf16[4,32,576]{2,1,0:T(8,128)(2,1)S(1)}, bf16[4,32,576]{2,1,0:T(8,128)(2,1)S(1)}, u32[]{:S(2)}, u32[]{:S(2)}) collective-permute-start(bf16[4,32,576]{2,1,0:T(8,128)(2,1)S(1)} %pad_maximum_fusion.11.refs_0_), channel_id=1, source_target_pairs={{0,24},{4,28},{8,16},{12,20},{16,8},{20,12},{24,0},{28,4},{1,25},{... | collective-permute-start | bytes 442376 | tf_op jit(solution)/shard_map/ppermute | solution.py:21
  317.8 9.8 %collective-permute-start.54 = (bf16[4,32,576]{2,1,0:T(8,128)(2,1)S(1)}, bf16[4,32,576]{2,1,0:T(8,128)(2,1)S(1)}, u32[]{:S(2)}, u32[]{:S(2)}) collective-permute-start(bf16[4,32,576]{2,1,0:T(8,128)(2,1)S(1)} %pad_maximum_fusion.11.refs_0_), channel_id=1, source_target_pairs={{0,4},{4,0},{8,12},{12,8},{16,20},{20,16},{24,28},{28,24},{1,5},{5... | collective-permute-start | bytes 442376 | tf_op jit(solution)/shard_map/ppermute | solution.py:21
  (62 other events, 416.4 us)
Sparse Core Ops, SparseCore 0:
  30.5 32.2 all-gather.4
  65.0 30.2 all-gather.6
  97.1 32.4 all-gather.8
  171.2 34.5 reduce-scatter.2
  208.0 28.4 reduce-scatter.4
  239.7 58.7 all-reduce.4
  300.5 31.2 all-gather.10
where the time goes:
time: 347 us; the launch traced here: 345 us
  waiting for transfers between devices  126 us (36%)
  starting transfers between devices  62 us (18%)
  Pallas kernels  54.6 us (16%)
  local copies, waits for them, and re-layouts  34.2 us (10%)
  other arithmetic  32.5 us (9%)
  matrix products  20.4 us (6%)
  between operations  15.1 us (4%)
    ppermute x58, waiting for transfers between devices, swap(): lax.ppermute(x, axis, [(i, i ^ mask) for i in range(lax.axis_size(axis))])  109 us
    ppermute x58, starting transfers between devices, swap(): lax.ppermute(x, axis, [(i, i ^ mask) for i in range(lax.axis_size(axis))])  61.3 us
    pallas_call x4, Pallas kernels, in_vmem(): pl.pallas_call(kernel, grid_spec=pltpu.PrefetchScalarGridSpec(num_scalar_...  48.2 us
    reduce_scatter x1, waiting for transfers between devices, per_device(): lax.psum_scatter(ffn_terms, 'fsdp', scatter_dimension=0, tiled=True)  17.8 us
    unnamed x101, local copies, waits for them, and re-layouts  11.2 us
    dot_general x4, matrix products, contract_cols(): lax.dot_general(left, right, (((1,), (1,)), ((), ())), preferred_element_...  8.03 us
  transfers between devices with their start and end apart: 65, of which 32 were waited for; matrix products, arithmetic and copies ran while one was open for 17% of the time, Pallas kernels for 15%

commit v1 on v0

--- a/solution.py
+++ b/solution.py
@@ -49,10 +49,7 @@
 def ctx_collect(keep, send):
     came = swap(send, "ctx", 1)
     pieces = [add16(keep[r], came[r]) for r in range(keep.shape[0])]
-    return sum(
-        piece.astype(F32)
-        for piece in [pieces[0]] + [swap(pieces[r], "ctx", 2 * r) for r in range(1, len(pieces))]
-    )
+    return [pieces[0]] + [swap(pieces[r], "ctx", 2 * r) for r in range(1, len(pieces))]
 
 
 def pick(stacked, index):
@@ -250,23 +247,146 @@
         to_ref[i % (pieces // 2)] = acc_ref[2 * i : 2 * i + 2].astype(BF16)
 
 
-def in_grad_kernel(meta, normed_ref, grad_ref, late_ref, keep_ref, send_ref, term_ref, *, cut, share):
-    term_ref[...] = contract_rows(normed_ref[...], grad_ref[...])
+def project_kernel(meta, *refs, groups, fetch):
+    tokens = refs[:groups]
+    norm_ref = refs[groups]
+    parts = refs[groups + 1 : groups + 1 + fetch]
+    kv_ref, q_ref, normed_ref, unit_ref, proj_ref = refs[groups + 1 + fetch :]
+    member, chip = meta[1], meta[2]
+    depth, across = proj_ref.shape
+    share = depth // groups
+    for c in range(fetch):
+        for z in range(groups):
+            start = (member ^ z) * share + (chip ^ c) * (share // fetch)
+            proj_ref[pl.ds(pl.multiple_of(start, 16), share // fetch)] = parts[c][z]
+    rows = [norm_ref[member ^ z][:1].astype(F32) for z in range(groups)]
+    gain = jnp.concatenate([row[:, :share] for row in rows], axis=1)
+    shift = jnp.concatenate([row[:, share : 2 * share] for row in rows], axis=1)
+    part2 = kv_ref.shape[2]
+    wide = q_ref.shape[2]
+    size = kv_ref.shape[1]
+    for j in range(2):
+        x = jnp.concatenate([ref[j] for ref in tokens], axis=0).astype(F32)
+        unit, _ = norm_parts(x)
+        normed = (unit * gain + shift).astype(BF16)
+        unit_ref[j] = unit
+        normed_ref[j] = normed
+        mixed = mm(normed, proj_ref[...]).astype(BF16)
+        kv_ref[j] = mixed[:, :part2]
+        q_ref[j, :, : across - part2] = mixed[:, part2:]
+        if wide > across - part2:
+            q_ref[j, :, across - part2 :] = jnp.zeros((size, wide - across + part2), BF16)
+
+
+def second_kernel(meta, *refs, groups):
+    pieces = refs[:groups]
+    x_ref, proj_ref, vec_ref, resid_ref, second_ref = refs[groups:]
+    member = meta[1]
+    slot, part = pieces[0].shape[1:]
+    total = x_ref[...].astype(F32) + vec_ref[0:1]
+    for z in range(groups):
+        total += mm(pieces[z][...].reshape(2 * slot, part), proj_ref[member ^ z])
+    resid_ref[...] = total
+    unit, _ = norm_parts(total)
+    second_ref[...] = (unit * vec_ref[1:2] + vec_ref[2:3]).astype(BF16)
+
+
+def branch_kernel(meta, *refs, groups, chips):
+    sums = refs[:chips]
+    resid_ref, grad_ref, proj_ref, vec_ref = refs[chips : chips + 4]
+    outs = refs[chips + 4 : chips + 4 + groups]
+    resid_grad_ref, branch_ref, totals_ref = refs[chips + 4 + groups :]
+    member = meta[1]
+    slot, part = outs[0].shape[1:]
+    second_grad = sum(ref[...].astype(F32) for ref in sums)
+    unit, rate = norm_parts(resid_ref[...])
+    dout = grad_ref[...].astype(F32)
+    resid_grad = dout + norm_back(unit, rate, vec_ref[1:2], second_grad)
+    resid_grad_ref[...] = resid_grad
+    branch = resid_grad.astype(BF16)
+    branch_ref[...] = branch
+    for z in range(groups):
+        grads = contract_cols(branch, proj_ref[member ^ z]).astype(BF16)
+        outs[z][...] = grads.reshape(2, slot, part)
+    totals_ref[0:1] = jnp.sum(branch.astype(F32), axis=0, keepdims=True)
+    totals_ref[1:2] = jnp.sum(second_grad * unit, axis=0, keepdims=True)
+    totals_ref[2:3] = jnp.sum(second_grad, axis=0, keepdims=True)
+    totals_ref[3:4] = jnp.sum(dout, axis=0, keepdims=True)
+    totals_ref[4:] = jnp.zeros((4, totals_ref.shape[1]), F32)
+
+
+def handed_kernel(meta, *refs, groups, chips, cut, share, with_out):
+    sums = refs[:chips]
+    dq_ref, normed_ref, unit_ref, proj_ref, totals_ref, up_bias_ref = refs[chips : chips + 6]
+    at = chips + 6
+    attended = refs[at : at + groups] if with_out else ()
+    branches = refs[at + groups] if with_out else None
+    at += (groups + 1) * with_out
+    outs = refs[at : at + groups]
+    keep_ref, send_ref, grad_ref, term_ref, out_term_ref, vec_ref = refs[at + groups :]
     here, member = meta[0], meta[1]
-    fetch, groups, tall, wide = keep_ref.shape
+    fetch = keep_ref.shape[0]
+    across = keep_ref.shape[3]
+    part2 = sums[0].shape[2]
+    slot = outs[0].shape[1]
+    size = slot * groups
+    width = unit_ref.shape[2]
+    gain_total = jnp.zeros((1, width), F32)
+    shift_total = jnp.zeros((1, width), F32)
+    for j in range(2):
+        keyval = sum(ref[j].astype(F32) for ref in sums).astype(BF16)
+        grad = jnp.concatenate([keyval, dq_ref[j]], axis=1)
+        grad_ref[j] = grad
+        normed_grad = contract_cols(grad, proj_ref[...])
+        gain_total += jnp.sum(normed_grad * unit_ref[j], axis=0, keepdims=True)
+        shift_total += jnp.sum(normed_grad, axis=0, keepdims=True)
+        for z in range(groups):
+            outs[z][j] = normed_grad[z * slot : (z + 1) * slot].astype(BF16)
+    term_ref[...] = contract_rows(
+        normed_ref[...].reshape(2 * size, width), grad_ref[...].reshape(2 * size, across)
+    )
+    if with_out:
+        out_term_ref[...] = sum(
+            contract_rows(piece[...].reshape(2 * slot, share), branches[z])
+            for z, piece in enumerate(attended)
+        )
+    hidden = up_bias_ref.shape[1]
+    vec_ref[...] = jnp.zeros_like(vec_ref)
+    for z in range(groups):
+        cols = slice(z * share, (z + 1) * share)
+        vec_ref[z, 0:1, :share] = gain_total[:, cols]
+        vec_ref[z, 0:1, share : 2 * share] = shift_total[:, cols]
+        vec_ref[z, 1:2, :share] = totals_ref[0:1, cols]
+        vec_ref[z, 1:2, share : 2 * share] = totals_ref[1:2, cols]
+        vec_ref[z, 2:3, :share] = totals_ref[2:3, cols]
+        vec_ref[z, 2:3, share : 2 * share] = totals_ref[3:4, cols]
+        done = 0
+        while done < hidden:
+            size_now = min(across, hidden - done)
+            row = 3 + done // across
+            vec_ref[z, row : row + 1, :size_now] = up_bias_ref[z : z + 1, done : done + size_now]
+            done += size_now
     for core, to_ref in enumerate((keep_ref, send_ref)):
         for r in range(fetch):
+            mine = ((here ^ (2 * r + core)) & (2 * fetch - 1)) * cut
             for z in range(groups):
                 owner = member ^ z
-                start = owner * share + ((here ^ (2 * r + core)) & (2 * fetch - 1)) * cut
-                rows = term_ref[pl.ds(pl.multiple_of(start, 8), cut)]
-                to_ref[r, z] = jnp.concatenate([rows, late_ref[owner]], axis=0).astype(BF16)
-
-
-def in_home_kernel(meta, *refs, cut, fetch, part, width):
-    pieces, out_ref, late_ref = refs[:-2], refs[-2], refs[-1]
+                start = pl.multiple_of(owner * share + mine, 8)
+                rows = term_ref[pl.ds(start, cut)]
+                to_ref[r, z] = jnp.concatenate([rows, vec_ref[owner]], axis=0).astype(BF16)
+            if with_out:
+                rows = out_term_ref[pl.ds(pl.multiple_of(mine, 8), cut)]
+                rest = jnp.concatenate(
+                    [rows[8 * i : 8 * i + 8, across:] for i in range(cut // 8)], axis=1
+                )
+                to_ref[r, groups] = jnp.concatenate([rows[:, :across], rest], axis=0).astype(BF16)
+
+
+def home_kernel(meta, *refs, groups, cut, fetch, part, width, with_out):
+    pieces = refs[: 2 * fetch]
+    out_ref, out_out_ref = refs[2 * fetch :]
     here, member = meta[0], meta[1]
-    groups = pieces[0].shape[0]
+    across = 3 * part
     for i, piece in enumerate(pieces):
         r = 2 * (i % fetch) + i // fetch
         start = pl.multiple_of(((here ^ r) & (2 * fetch - 1)) * cut, 8)
@@ -274,8 +394,25 @@
         for k, home in enumerate((width, 2 * width, 0)):
             whole = jnp.concatenate([h[:cut, k * part : (k + 1) * part] for h in held], axis=1)
             out_ref[pl.ds(start, cut), home : home + width] = whole[:, :width]
-        if i == 0:
-            late_ref[...] = sum(h[cut:] for h in held)
+        if with_out:
+            block = piece[groups].astype(F32)
+            rest = jnp.concatenate(
+                [
+                    block[cut : cut + 8, i * (width - across) : (i + 1) * (width - across)]
+                    for i in range(cut // 8)
+                ],
+                axis=0,
+            )
+            out_out_ref[pl.ds(start, cut)] = jnp.concatenate([block[:cut], rest], axis=1)
+        elif i == 0:
+            out_out_ref[...] = jnp.zeros_like(out_out_ref)
+
+
+def tokens_kernel(meta, grad_ref, x_ref, gain_ref, resid_grad_ref, out_ref):
+    rows, width = x_ref.shape
+    grad = grad_ref[...].astype(F32).reshape(rows, width)
+    unit, rate = norm_parts(x_ref[...].astype(F32))
+    out_ref[...] = resid_grad_ref[...] + norm_back(unit, rate, gain_ref[...], grad)
 
 
 def in_vmem(kernel, meta, arrays, outs, scratch=(), flops=0, there=()):
@@ -351,16 +488,13 @@
     fold = max(f for f in (1, 2, 4, 8, 16) if f <= chips and share % (16 * f) == 0)
     chip = (here // 2) % fetch
     cut = share // (2 * fold)
-    spread_f = jnp.arange(groups, dtype=jnp.int32)
     spread_c = jnp.arange(n_ctx, dtype=jnp.int32)
-    spread_h = jnp.arange(fetch, dtype=jnp.int32)
 
     own = tokens.reshape(2, slot, width)
-    rows = own.reshape(local_rows, width).astype(F32)
-    grad16 = out_grad.reshape(2, slot, width)
-    place_index = jnp.stack([here, member]).astype(jnp.int32)
-
-    group_tokens = jnp.stack(z_gather(own), axis=1).reshape(count_rows, width)
+    rows16 = tokens.reshape(local_rows, width)
+    grad16 = out_grad.reshape(local_rows, width)
+    index = jnp.stack([here, member, chip]).astype(jnp.int32)
+
     in_cut = lax.dynamic_slice_in_dim(mixer_in, chip * (share // fetch), share // fetch, 0)
     in_cut = in_cut.reshape(-1, 3, width)
     in_cut = jnp.pad(in_cut, ((0, 0), (0, 0), (0, groups * part - width)))
@@ -370,29 +504,30 @@
     norm_row = jnp.pad(jnp.concatenate([first_gain, first_shift]), (0, 3 * part - 2 * share))
     norm_rows = jnp.broadcast_to(norm_row, (groups, 16, 3 * part))
     in_cut = jnp.concatenate([in_cut, norm_rows], axis=1)
-    in_pieces = jnp.stack(z_exchange([pick(in_cut, member ^ r) for r in range(groups)]))
-    norm_nat = jnp.concatenate(
-        [pick(in_pieces[:, share // fetch], member ^ r)[None] for r in range(groups)]
-    ).astype(F32)
-    gain_one = norm_nat[:, :share].reshape(width)
-    shift_one = norm_nat[:, share : 2 * share].reshape(width)
-    in_parts = jnp.stack(chip_spread(in_pieces[:, : share // fetch], fetch))
-    fetch_table = (
-        (spread_h[None, :] ^ chip) * groups + (spread_f[:, None] ^ member)
-    ).reshape(-1)
-    proj_in = shuffle(
-        in_parts.reshape(fetch * groups, share // fetch, 3 * part),
-        fetch_table,
-        BF16,
-        2 * part + wide,
-    ).reshape(width, 2 * part + wide)
-
-    unit_one, _ = norm_parts(group_tokens.astype(F32))
-    normed16 = (unit_one * gain_one + shift_one).astype(BF16)
-    mixed = mm(normed16, proj_in).astype(BF16)
-    keyval = mixed[:, : 2 * part].reshape(2, block_len, 2 * part)
-    query = mixed[:, 2 * part :].reshape(2, block_len, wide)
-    keyvals = ctx_spread(keyval)
+    in_pieces = z_exchange([pick(in_cut, member ^ r) for r in range(groups)])
+    in_pieces = jnp.stack(in_pieces)
+    group_tokens = z_gather(after(own, in_pieces))
+    norm_part = in_pieces[:, share // fetch :]
+    in_parts = chip_spread(in_pieces[:, : share // fetch], fetch)
+    group_tokens = after(tuple(group_tokens), *in_parts)
+    gain_one = jnp.concatenate(
+        [pick(norm_part[:, 0, :share], member ^ r)[None] for r in range(groups)]
+    ).reshape(1, width).astype(F32)
+
+    pieces = jax.ShapeDtypeStruct((2, block_len, width), BF16)
+    keyval, query, normed16, unit_one, proj_in = in_vmem(
+        functools.partial(project_kernel, groups=groups, fetch=fetch),
+        index,
+        list(group_tokens) + [norm_part] + in_parts,
+        [
+            jax.ShapeDtypeStruct((2, block_len, 2 * part), BF16),
+            jax.ShapeDtypeStruct((2, block_len, wide), BF16),
+            pieces,
+            jax.ShapeDtypeStruct((2, block_len, width), F32),
+            jax.ShapeDtypeStruct((width, 3 * part), BF16),
+        ],
+    )
+    keyvals = chip_spread(keyval, chips)
 
     owners = block_owner.reshape(-1)
     numbers = jnp.arange(blocks, dtype=jnp.int32)
@@ -407,36 +542,40 @@
         ]
     ).astype(jnp.int32)
 
-    grads_all = lax.all_gather(grad16.reshape(local_rows, width), "ctx", axis=0, tiled=True)
+    grads_all = lax.all_gather(grad16, "ctx", axis=0, tiled=True)
     order = jnp.concatenate([spread_c[0::2], spread_c[1::2]]) ^ here
     grads_all = shuffle(grads_all.reshape(n_ctx, local_rows, width), order, BF16)
     grads_all = grads_all.reshape(n_ctx * local_rows, width)
     extra = jnp.concatenate([mixer_bias, second_gain, second_shift, down_bias]).reshape(1, 4 * share)
     extra = jnp.concatenate([extra, jnp.pad(up_bias, (0, 4 * share - hidden))[None]])
     extra = jnp.pad(extra, ((0, 14), (0, width - 4 * share)))
-    out_pack = after(jnp.concatenate([mixer_out, extra]), group_tokens)
+    out_pack = after(jnp.concatenate([mixer_out, extra]), *group_tokens)
     out_pack = lax.all_gather(out_pack, "fsdp", axis=0, tiled=True)
     out_pack = out_pack.reshape(groups, share + 16, width)
     proj_out = out_pack[:, :share].reshape(width, width)
-    mix_bias, gain_two, shift_two, bias_down = (
-        out_pack[:, share, i * share : (i + 1) * share].reshape(width).astype(F32)
-        for i in range(4)
-    )
+    proj_out = jnp.pad(proj_out, ((0, groups * part - width), (0, 0)))
+    proj_out = proj_out.reshape(groups, part, width)
+    vectors = jnp.concatenate(
+        [out_pack[:, share, i * share : (i + 1) * share].reshape(1, width) for i in range(4)]
+        + [jnp.zeros((4, width), BF16)]
+    ).astype(F32)
     up_bias_part = lax.dynamic_slice_in_dim(
         out_pack[:, share + 1], here * hidden_cut, hidden_cut, 1
     ).reshape(groups * hidden_cut)
+    *keyvals, grads_all = lax.optimization_barrier((*keyvals, grads_all))
+    keyvals = keyvals + [swap(piece, "ctx", 1) for piece in keyvals]
     ffn_cut = jnp.concatenate(
         [
             lax.dynamic_slice_in_dim(up_weight, here * hidden_cut, hidden_cut, 0),
             lax.dynamic_slice_in_dim(down_weight, here * hidden_cut, hidden_cut, 0),
         ]
     )
-    ffn_parts = lax.all_gather(after(ffn_cut, group_tokens), "fsdp", axis=0, tiled=True)
+    ffn_parts = lax.all_gather(after(ffn_cut, grads_all), "fsdp", axis=0, tiled=True)
     ffn_parts = ffn_parts.reshape(groups, 2, hidden_cut, width)
     up_part = ffn_parts[:, 0].reshape(groups * hidden_cut, width)
     down_part = ffn_parts[:, 1].reshape(groups * hidden_cut, width)
 
-    attend_flops = 10 * blocks * block_len * block_len * wide * heads
+    attend_flops = 40 * blocks * block_len * block_len * wide * heads
     pair = jax.ShapeDtypeStruct((2, slot, part), BF16)
     results = in_vmem(
         functools.partial(attend_kernel, heads=heads, pieces=n_ctx, groups=groups),
@@ -454,14 +593,19 @@
         attend_flops,
         range(1, 1 + n_ctx),
     )
+    own_attended = results[:groups]
     sums, lse = results[groups:]
-    attended = jnp.stack(z_exchange(results[:groups])).reshape(groups, local_rows, part)
-    attend16 = jnp.concatenate([pick(attended, member ^ i) for i in range(groups)], axis=1)
-    attend16 = attend16[:, :width]
-
-    resid = rows + (mm(attend16, proj_out) + mix_bias)
-    unit_two, rate_two = norm_parts(resid)
-    second16 = (unit_two * gain_two + shift_two).astype(BF16)
+    attended = z_exchange(results[:groups])
+    proj_out, vectors, *attended = lax.optimization_barrier((proj_out, vectors, *attended))
+    resid, second16 = in_vmem(
+        functools.partial(second_kernel, groups=groups),
+        index,
+        attended + [rows16, proj_out, vectors],
+        [
+            jax.ShapeDtypeStruct((local_rows, width), F32),
+            jax.ShapeDtypeStruct((local_rows, width), BF16),
+        ],
+    )
 
     second_all = jnp.concatenate(ctx_spread(second16))
     pre = contract_cols(second_all, up_part) + up_bias_part.astype(F32)
@@ -469,15 +613,43 @@
     act16 = act.astype(BF16)
     pre_grad = gate_pull(contract_cols(grads_all, down_part))[0].astype(BF16)
     second_part = mm(pre_grad, up_part).astype(BF16).reshape(2, chips, local_rows, width)
-    second_grad = ctx_collect(second_part[0], second_part[1])
-    resid_grad = grad16.reshape(local_rows, width).astype(F32) + norm_back(
-        unit_two, rate_two, gain_two, second_grad
-    )
-    branch_grad16 = resid_grad.astype(BF16)
-    attend_grad = contract_cols(branch_grad16, proj_out).astype(BF16)
-    attend_grad = jnp.pad(attend_grad, ((0, 0), (0, groups * part - width)))
-    attend_grad = attend_grad.reshape(2, slot, groups, part).transpose(2, 0, 1, 3)
-    attend_grads = z_exchange([pick(attend_grad, member ^ r) for r in range(groups)])
+    up_term = contract_rows(pre_grad, second_all).astype(BF16)
+    down_term = contract_rows(act16, grads_all).astype(BF16)
+    feed_part = mm(act16, down_part).astype(BF16)
+    second_sums = ctx_collect(second_part[0], second_part[1])
+    back_order = spread_c ^ here
+    back_order = (back_order % 2) * chips + back_order // 2
+    feed = shuffle(feed_part.reshape(n_ctx, local_rows, width), back_order, BF16)
+    feed = feed.reshape(n_ctx * local_rows, width)
+    ffn_terms = jnp.concatenate(
+        [
+            up_term.reshape(groups, hidden_cut, width),
+            down_term.reshape(groups, hidden_cut, width),
+        ],
+        axis=1,
+    ).reshape(groups * 2 * hidden_cut, width)
+    feed, ffn_terms, *second_sums = lax.optimization_barrier((feed, ffn_terms, *second_sums))
+    feed = lax.psum_scatter(feed, "ctx", scatter_dimension=0, tiled=True)
+    results = in_vmem(
+        functools.partial(branch_kernel, groups=groups, chips=chips),
+        index,
+        second_sums + [resid, grad16, proj_out, vectors],
+        [pair] * groups
+        + [
+            jax.ShapeDtypeStruct((local_rows, width), F32),
+            jax.ShapeDtypeStruct((local_rows, width), BF16),
+            jax.ShapeDtypeStruct((8, width), F32),
+        ],
+    )
+    resid_grad, branch_grad16, totals = results[groups:]
+    attend_grads = z_exchange(results[:groups])
+    branches = branch_grad16[None]
+    branches = jnp.concatenate([branches, swap(branches, "fsdp", 1)])
+    branches, *attend_grads = lax.optimization_barrier((branches, *attend_grads))
+    mask = 2
+    while mask < groups:
+        branches = jnp.concatenate([branches, swap(branches, "fsdp", mask)])
+        mask *= 2
 
     half = jax.ShapeDtypeStruct((chips, 2, block_len, 2 * part), BF16)
     query_grad, keyval_keep, keyval_send = in_vmem(
@@ -494,102 +666,110 @@
         attend_flops,
         range(1, 1 + n_ctx),
     )
-    keyval_grad = ctx_collect(keyval_keep, keyval_send).astype(BF16)
-    mixed_grad = jnp.concatenate(
-        [keyval_grad.reshape(count_rows, 2 * part), query_grad.reshape(count_rows, part)], axis=1
-    )
-    normed_part = contract_cols(mixed_grad, proj_in[:, : 3 * part])
-    normed_pieces = normed_part.astype(BF16).reshape(2, groups, slot, width)
-    normed_grad = z_sum([normed_pieces[:, r] for r in range(groups)]).reshape(local_rows, width)
-    unit_own, rate_own = norm_parts(rows)
-    tokens_grad = resid_grad + norm_back(unit_own, rate_own, gain_one, normed_grad)
-
-    late = jnp.stack([jnp.sum(normed_part * unit_one, axis=0), jnp.sum(normed_part, axis=0)])
-    late = late.reshape(2, groups, share).transpose(1, 0, 2).reshape(groups, 1, 2 * share)
-    late = jnp.pad(late, ((0, 0), (0, 7), (0, 3 * part - 2 * share)))
-    tall = cut + 8
-    half = jax.ShapeDtypeStruct((fold, groups, tall, 3 * part), BF16)
-    in_keep, in_send = in_vmem(
-        functools.partial(in_grad_kernel, cut=cut, share=share),
-        place_index,
-        [normed16, mixed_grad, late],
-        [half, half],
-        [pltpu.VMEM((width, 3 * part), F32)],
-    )
-    in_came = swap(in_send, "ctx", 1)
-    in_sums = [add16(in_keep[r], in_came[r]) for r in range(fold)]
-    in_term = sum(
-        piece.astype(F32)
-        for piece in [in_sums[0]] + [swap(in_sums[r], "ctx", 2 * r) for r in range(1, fold)]
-    ).astype(BF16)
+    keyval_sums = ctx_collect(keyval_keep, after(keyval_send, branches, feed))
+
+    ffn_terms = after(ffn_terms, branches, query_grad)
+    ffn_term = lax.psum_scatter(ffn_terms, "fsdp", scatter_dimension=0, tiled=True)
+
+    with_out = part == share and (cut // 8) * (width - 3 * part) == 3 * part
+    up_bias_terms = jnp.sum(pre_grad.astype(F32), axis=0).reshape(groups, hidden_cut)
+    up_bias_terms = lax.dynamic_update_slice(
+        jnp.zeros((groups, hidden), F32), up_bias_terms, (0, here * hidden_cut)
+    )
+    half = jax.ShapeDtypeStruct((fold, groups + with_out, cut + 8, 3 * part), BF16)
+    results = in_vmem(
+        functools.partial(
+            handed_kernel, groups=groups, chips=chips, cut=cut, share=share, with_out=with_out
+        ),
+        index,
+        keyval_sums
+        + [query_grad, normed16, unit_one, proj_in, totals, up_bias_terms]
+        + (list(own_attended) + [branches] if with_out else []),
+        [jax.ShapeDtypeStruct((2, slot, width), BF16)] * groups + [half, half],
+        [
+            pltpu.VMEM((2, block_len, 3 * part), BF16),
+            pltpu.VMEM((width, 3 * part), F32),
+            pltpu.VMEM((share, width), F32),
+            pltpu.VMEM((groups, 8, 3 * part), F32),
+        ],
+    )
+    in_keep, in_send = results[groups:]
+    ffn_grads = lax.all_gather(after(ffn_term, in_keep), "ctx", axis=0, tiled=True)
+    in_sums = ctx_collect(in_keep, in_send)
+    normed_pieces = list(results[:groups])
+    mask = groups // 2
+    while mask:
+        came = swap(jnp.stack(normed_pieces[mask:]), "fsdp", mask)
+        if mask == groups // 2:
+            came, *in_sums = lax.optimization_barrier((came, *in_sums))
+        normed_pieces = [add16(piece, came[i]) for i, piece in enumerate(normed_pieces[:mask])]
+        mask //= 2
+    normed_grad = normed_pieces[0]
+    in_term = sum(piece.astype(F32) for piece in in_sums).astype(BF16)
     mask = 2 * fold
     while mask < n_ctx:
         in_term = add16(in_term, swap(in_term, "ctx", mask))
         mask *= 2
-    in_term = jnp.stack(z_exchange([in_term[r] for r in range(groups)]))
+    handed = z_exchange([in_term[r] for r in range(groups)])
+    small = sum(piece[cut:].astype(F32) for piece in handed)
+    in_term = jnp.stack(handed + [in_term[groups]] if with_out else handed)
     in_held = chip_spread(in_term, fold)
     in_held = in_held + [swap(piece, "ctx", 1) for piece in in_held]
-    mixer_in_grad, late = in_vmem(
-        functools.partial(in_home_kernel, cut=cut, fetch=fold, part=part, width=width),
-        place_index,
+    tokens_grad = in_vmem(
+        tokens_kernel,
+        index,
+        [normed_grad, rows16, gain_one, resid_grad],
+        [jax.ShapeDtypeStruct((local_rows, width), F32)],
+    )[0]
+    block_out = (resid + feed.astype(F32) + vectors[3:4]).astype(BF16)
+
+    ffn_grads = ffn_grads.reshape(n_ctx, 2, hidden_cut, width).astype(F32)
+    up_grad = ffn_grads[:, 0].reshape(hidden, width)
+    down_grad = ffn_grads[:, 1].reshape(hidden, width)
+    up_grad, down_grad, tokens_grad, *in_held = lax.optimization_barrier(
+        (up_grad, down_grad, tokens_grad, *in_held)
+    )
+    mixer_in_grad, mixer_out_grad = in_vmem(
+        functools.partial(
+            home_kernel,
+            groups=groups,
+            cut=cut,
+            fetch=fold,
+            part=part,
+            width=width,
+            with_out=with_out,
+        ),
+        index,
         in_held,
         [
             jax.ShapeDtypeStruct((share, 3 * width), F32),
-            jax.ShapeDtypeStruct((8, 3 * part), F32),
+            jax.ShapeDtypeStruct((share, width), F32),
         ],
     )
 
-    ffn_terms = jnp.concatenate(
-        [
-            contract_rows(pre_grad, second_all).astype(BF16).reshape(groups, hidden_cut, width),
-            contract_rows(act16, grads_all).astype(BF16).reshape(groups, hidden_cut, width),
-        ],
-        axis=1,
-    ).reshape(groups * 2 * hidden_cut, width)
-    ffn_term = lax.psum_scatter(ffn_terms, "fsdp", scatter_dimension=0, tiled=True)
-    ffn_grads = lax.all_gather(ffn_term, "ctx", axis=0, tiled=True)
-    ffn_grads = ffn_grads.reshape(n_ctx, 2, hidden_cut, width).astype(F32)
-
-    feed_part = mm(act16, down_part).astype(BF16).reshape(2, chips, local_rows, width)
-    feed_part = after(feed_part, branch_grad16)
-    feed = ctx_collect(feed_part[0], feed_part[1])
-    block_out = (resid + feed + bias_down).astype(BF16)
-
-    early = jnp.stack(
-        [
-            jnp.sum(branch_grad16.astype(F32), axis=0),
-            jnp.sum(second_grad * unit_two, axis=0),
-            jnp.sum(second_grad, axis=0),
-            jnp.sum(grad16.reshape(local_rows, width).astype(F32), axis=0),
-        ]
-    )
-    early = early.reshape(4, groups, share).transpose(1, 0, 2).reshape(groups, 1, 4 * share)
-    up_bias_terms = jnp.sum(pre_grad.astype(F32), axis=0).reshape(groups, 1, hidden_cut)
-    up_bias_terms = lax.dynamic_update_slice(
-        jnp.zeros((groups, 1, width), F32), up_bias_terms, (0, 0, here * hidden_cut)
-    )
-    early = jnp.pad(early, ((0, 0), (0, 0), (0, width - 4 * share)))
-    early = jnp.concatenate([early, up_bias_terms, jnp.zeros((groups, 14, width), F32)], axis=1)
-    out_term = contract_rows(attend16, branch_grad16).reshape(groups, share, width)
-    out_term = jnp.concatenate([out_term, early], axis=1).astype(BF16)
-    out_term = out_term.reshape(groups * (share + 16), width)
-    out_term = lax.psum_scatter(out_term, "fsdp", scatter_dimension=0, tiled=True)
-    out_term = lax.psum(out_term, "ctx").astype(F32)
-
+    if not with_out:
+        whole = jnp.stack(attended).reshape(groups, local_rows, part)
+        whole = jnp.concatenate([pick(whole, member ^ i) for i in range(groups)], axis=1)
+        out_term = contract_rows(whole[:, :width], branch_grad16).astype(BF16)
+        out_term = lax.psum_scatter(out_term, "fsdp", scatter_dimension=0, tiled=True)
+        mixer_out_grad = lax.psum(out_term, "ctx").astype(F32)
+
+    bias_rows = -(-hidden // (3 * part))
+    up_bias_grad = small[3 : 3 + bias_rows].reshape(-1)[:hidden]
     return (
         block_out.reshape(1, 2, slot, width),
         tokens_grad.reshape(1, 2, slot, width),
-        late[0, :share],
-        late[0, share : 2 * share],
+        small[0, :share],
+        small[0, share : 2 * share],
         mixer_in_grad,
-        out_term[:share],
-        out_term[share, :share],
-        out_term[share, share : 2 * share],
-        out_term[share, 2 * share : 3 * share],
-        ffn_grads[:, 0].reshape(hidden, width),
-        out_term[share + 1, :hidden],
-        ffn_grads[:, 1].reshape(hidden, width),
-        out_term[share, 3 * share : 4 * share],
+        mixer_out_grad,
+        small[1, :share],
+        small[1, share : 2 * share],
+        small[2, :share],
+        up_grad,
+        up_bias_grad,
+        down_grad,
+        small[2, share : 2 * share],
     )
 
 

time: 347 us -> 295 us (0.85)
  waiting for transfers between devices: 126 us -> 98.8 us
  other arithmetic: 32.5 us -> 11.6 us
  Pallas kernels: 54.6 us -> 73.8 us
  matrix products: 20.4 us -> 7.97 us
  local copies, waits for them, and re-layouts: 34.2 us -> 22.4 us
    pallas_call x4 -> x8, Pallas kernels: 48.2 us -> 67 us  [in_vmem(): pl.pallas_call(kernel, grid_spec=pltpu.PrefetchScalarGridSpec(num_scalar_...]
    reduce_scatter x1, waiting for transfers between devices: 17.8 us -> 0.02 us  [per_device(): lax.psum_scatter(ffn_terms, 'fsdp', scatter_dimension=0, tiled=True)]
    ppermute x58 -> x55, waiting for transfers between devices: 109 us -> 93.9 us  [swap(): lax.ppermute(x, axis, [(i, i ^ mask) for i in range(lax.axis_size(axis))])]
    reduce_sum x9 -> x0, other arithmetic: 6.45 us -> none  [the longest x1 2.24 us: per_device(): jnp.sum(second_grad * unit_two, axis=0)]
    unnamed x101 -> x128, local copies, waits for them, and re-layouts: 11.2 us -> 5.92 us
    dot_general x4 -> x2, matrix products: 8.03 us -> 2.84 us  [contract_cols(): lax.dot_general(left, right, (((1,), (1,)), ((), ())), preferred_element_...]
    convert_element_type x6 -> x4, other arithmetic: 6.19 us -> 1.46 us  [the longest x1 0.73 us: per_device(): block_out = (resid + feed.astype(F32) + vectors[3:4]).astype(BF16)]
    dot_general x3 -> x2, matrix products: 6.37 us -> 1.78 us  [contract_rows(): lax.dot_general(left, right, (((0,), (0,)), ((), ())), preferred_element_...]
  transfers between devices with their start and end apart: 65 -> 61, of which waited for: 32 -> 26; matrix products, arithmetic and copies ran while one was open for 17% -> 11% of each run, Pallas kernels for 15% -> 22%
where the time goes in v1:
time: 295 us; the launch traced here: 294 us
  waiting for transfers between devices  98.8 us (33%)
  Pallas kernels  73.8 us (25%)
  starting transfers between devices  64.2 us (22%)
  local copies, waits for them, and re-layouts  22.4 us (8%)
  between operations  15 us (5%)
  other arithmetic  11.6 us (4%)
  matrix products  7.97 us (3%)
    ppermute x55, waiting for transfers between devices, swap(): lax.ppermute(x, axis, [(i, i ^ mask) for i in range(lax.axis_size(axis))])  93.9 us
    pallas_call x8, Pallas kernels, in_vmem(): pl.pallas_call(kernel, grid_spec=pltpu.PrefetchScalarGridSpec(num_scalar_...  67 us
    ppermute x55, starting transfers between devices, swap(): lax.ppermute(x, axis, [(i, i ^ mask) for i in range(lax.axis_size(axis))])  64 us
    pallas_call x2, Pallas kernels, shuffle(): pl.pallas_call(shuffle_kernel, grid_spec=pltpu.PrefetchScalarGridSpec(num...  6.76 us
    unnamed x128, local copies, waits for them, and re-layouts  5.92 us
  transfers between devices with their start and end apart: 61, of which 26 were waited for; matrix products, arithmetic and copies ran while one was open for 11% of the time, Pallas kernels for 22%

profile of v1, /device:TPU:0, one launch (start us, length us, event | category | flops | bytes accessed | tf_op | source)
XLA Modules:
  0.0 293.9 jit_solution(8289056783790154010)
XLA Ops:
  9.9 3.1 %collective-permute-start = (bf16[64,576]{1,0:T(8,128)(2,1)S(1)}, bf16[64,576]{1,0:T(8,128)(2,1)S(1)}, u32[]{:S(2)}, u32[]{:S(2)}) collective-permute-start(bf16[64,576]{1,0:T(8,128)(2,1)S(1)} %get-tuple-element.194), channel_id=1, source_target_pairs={{0,1},{1,0},{2,3},{3,2},{4,5},{5,4},{6,7},{7,6},{8,9},{9,8},{10,11... | collective-permute-start | bytes 221192 | tf_op jit(solution)/shard_map/ppermute | solution.py:21
  13.0 2.6 collective-permute-start.1
  15.6 6.6 %collective-permute-done.1 = bf16[64,576]{1,0:T(8,128)(2,1)S(1)} collective-permute-done((bf16[64,576]{1,0:T(8,128)(2,1)S(1)}, bf16[64,576]{1,0:T(8,128)(2,1)S(1)}, u32[]{:S(2)}, u32[]{:S(2)}) %collective-permute-start.1) | collective-permute-done | bytes 73760 | tf_op jit(solution)/shard_map/ppermute | solution.py:21
  22.3 2.5 collective-permute-start.5
  27.0 2.4 collective-permute-start.8
  29.9 2.0 collective-permute-done.5.refs_3_
  34.2 7.3 %collective-permute-done.4.refs_2_ = bf16[2,64,768]{2,1,0:T(8,128)(2,1)S(1)} collective-permute-done((bf16[2,64,768]{2,1,0:T(8,128)(2,1)S(1)}, bf16[2,64,768]{2,1,0:T(8,128)(2,1)S(1)}, u32[]{:S(2)}, u32[]{:S(2)}) %collective-permute-start.4) | collective-permute-done | bytes 196640 | tf_op jit(solution)/shard_map/ppermute | solution.py:21
  43.8 4.9 %shard_map.237 = (bf16[2,256,384]{2,1,0:T(8,128)(2,1)}, bf16[2,256,256]{2,1,0:T(8,128)(2,1)}, bf16[2,256,768]{2,1,0:T(8,128)(2,1)}, f32[2,256,768]{2,1,0:T(8,128)}, bf16[768,576]{1,0:T(8,128)(2,1)}) custom-call(s32[3]{0:T(128)} %pad_add_fusion.meta, bf16[2,64,768]{2,1,0:T(8,128)(2,1)} %bitcast.141, bf16[2,64,768]{2,1,0:T(8,128)(2,1)} %copy-done.33, ...), custom_call_target="tpu_custom_call" | custom-call | bytes 1048576 | tf_op jit(solution)/shard_map/pallas_call | solution.py:421
  48.7 1.8 collective-permute-start.11
  53.3 3.4 %shard_map.238 = bf16[8,128,768]{2,1,0:T(8,128)(2,1)} custom-call(s32[8]{0:T(128)} %add_xor_fusion.table, bf16[8,128,768]{2,1,0:T(8,128)(2,1)} %bitcast.147), custom_call_target="tpu_custom_call" | custom-call | tf_op jit(solution)/shard_map/pallas_call | solution.py:70
  56.8 5.2 %collective-permute-done.11.refs_4_ = bf16[2,256,384]{2,1,0:T(8,128)(2,1)S(1)} collective-permute-done((bf16[2,256,384]{2,1,0:T(8,128)(2,1)}, bf16[2,256,384]{2,1,0:T(8,128)(2,1)S(1)}, u32[]{:S(2)}, u32[]{:S(2)}) %collective-permute-start.11) | collective-permute-done | bytes 393248 | tf_op jit(solution)/shard_map/ppermute | solution.py:21
  61.9 6.7 %collective-permute-done.10.refs_3_ = bf16[2,256,384]{2,1,0:T(8,128)(2,1)S(1)} collective-permute-done((bf16[2,256,384]{2,1,0:T(8,128)(2,1)}, bf16[2,256,384]{2,1,0:T(8,128)(2,1)S(1)}, u32[]{:S(2)}, u32[]{:S(2)}) %collective-permute-start.10) | collective-permute-done | bytes 393248 | tf_op jit(solution)/shard_map/ppermute | solution.py:21
  73.3 20.5 %shard_map.239 = (bf16[2,64,192]{2,1,0:T(8,128)(2,1)}, bf16[2,64,192]{2,1,0:T(8,128)(2,1)}, bf16[2,64,192]{2,1,0:T(8,128)(2,1)}, bf16[2,64,192]{2,1,0:T(8,128)(2...) custom-call(s32[19]{0:T(128)} %pad_add_fusion.1.meta, bf16[2,256,256]{2,1,0:T(8,128)(2,1)} %get-tuple-element.98.refs_0_, ...), custom_call_target="tpu_custom_call" | custom-call | flops 32212254720 | bytes 1048576 | tf_op jit(solution)/shard_map/pallas_call | solution.py:421
  93.8 3.3 %collective-permute-start.16 = (bf16[2,64,192]{2,1,0:T(8,128)(2,1)}, bf16[2,64,192]{2,1,0:T(8,128)(2,1)S(1)}, u32[]{:S(2)}, u32[]{:S(2)}) collective-permute-start(bf16[2,64,192]{2,1,0:T(8,128)(2,1)} %get-tuple-element.105.refs_11_), channel_id=1, source_target_pairs={{0,1},{1,0},{2,3},{3,2},{4,5},{5,4},{6,7},{7,6},{8,9},{9,8},{10,11... | collective-permute-start | bytes 147464 | tf_op jit(solution)/shard_map/ppermute | solution.py:21
  97.1 2.4 collective-permute-start.18
  100.5 2.4 slice.273.refs_5_.refs_6_
  104.4 5.2 %collective-permute-done.17.refs_2_ = bf16[2,64,192]{2,1,0:T(8,128)(2,1)S(1)} collective-permute-done((bf16[2,64,192]{2,1,0:T(8,128)(2,1)}, bf16[2,64,192]{2,1,0:T(8,128)(2,1)S(1)}, u32[]{:S(2)}, u32[]{:S(2)}) %collective-permute-start.17) | collective-permute-done | bytes 49184 | tf_op jit(solution)/shard_map/ppermute | solution.py:21
  110.3 3.3 %shard_map.240 = (f32[128,768]{1,0:T(8,128)}, bf16[128,768]{1,0:T(8,128)(2,1)}) custom-call(s32[3]{0:T(128)} %pad_add_fusion.meta, bf16[2,64,192]{2,1,0:T(8,128)(2,1)} %get-tuple-element.108.refs_0_.refs_10_, bf16[2,64,192]{2,1,0:T(8,128)(2,1)} %copy-done.34, bf16[2,64,192]{2,1,0:T(8,128)(2,1)} %copy-done.35, bf16[2,64,192]{2,1,0:T(8,128)(2,1)} %copy-done.36, ...), custom_call_target="tpu_custom_call" | custom-call | bytes 1048576 | tf_op jit(solution)/shard_map/pallas_call | solution.py:421
  113.6 2.2 collective-permute-start.21
  119.0 3.2 %collective-permute-done.21 = bf16[128,768]{1,0:T(8,128)(2,1)S(1)} collective-permute-done((bf16[128,768]{1,0:T(8,128)(2,1)}, bf16[128,768]{1,0:T(8,128)(2,1)S(1)}, u32[]{:S(2)}, u32[]{:S(2)}) %collective-permute-start.21) | collective-permute-done | bytes 196640 | tf_op jit(solution)/shard_map/ppermute | solution.py:21
  122.2 2.1 collective-permute-done.20
  128.8 1.8 convert_reduce_fusion
  132.5 2.4 convolution_convert_fusion.1
  136.7 1.7 collective-permute-start.29
  141.0 3.3 %shard_map.241 = bf16[8,128,768]{2,1,0:T(8,128)(2,1)} custom-call(s32[8]{0:T(128)} %fusion.49.table, bf16[8,128,768]{2,1,0:T(8,128)(2,1)} %bitcast.150), custom_call_target="tpu_custom_call" | custom-call | tf_op jit(solution)/shard_map/pallas_call | solution.py:70
  145.5 3.5 %collective-permute-done.28.refs_2_ = bf16[128,768]{1,0:T(8,128)(2,1)S(1)} collective-permute-done((bf16[128,768]{1,0:T(8,128)(2,1)S(1)}, bf16[128,768]{1,0:T(8,128)(2,1)S(1)}, u32[]{:S(2)}, u32[]{:S(2)}) %collective-permute-start.28) | collective-permute-done | bytes 196640 | tf_op jit(solution)/shard_map/ppermute | solution.py:21
  149.7 4.1 %shard_map.242 = (bf16[2,64,192]{2,1,0:T(8,128)(2,1)}, bf16[2,64,192]{2,1,0:T(8,128)(2,1)}, bf16[2,64,192]{2,1,0:T(8,128)(2,1)}, bf16[2,64,192]{2,1,0:T(8,128)(2...) custom-call(s32[3]{0:T(128)} %pad_add_fusion.meta, ...), custom_call_target="tpu_custom_call" | custom-call | bytes 1048576 | tf_op jit(solution)/shard_map/pallas_call | solution.py:421
  153.8 5.7 %collective-permute-start.30 = (bf16[1,128,768]{2,1,0:T(8,128)(2,1)}, bf16[1,128,768]{2,1,0:T(8,128)(2,1)S(1)}, u32[]{:S(2)}, u32[]{:S(2)}) collective-permute-start(bf16[1,128,768]{2,1,0:T(8,128)(2,1)} %bitcast.167), channel_id=1, source_target_pairs={{0,1},{1,0},{2,3},{3,2},{4,5},{5,4},{6,7},{7,6},{8,9},{9,8},{10,11... | collective-permute-start | bytes 589832 | tf_op jit(solution)/shard_map/ppermute | solution.py:21
  160.7 3.4 %collective-permute-start.33 = (bf16[2,64,192]{2,1,0:T(8,128)(2,1)S(1)}, bf16[2,64,192]{2,1,0:T(8,128)(2,1)S(1)}, u32[]{:S(2)}, u32[]{:S(2)}) collective-permute-start(bf16[2,64,192]{2,1,0:T(8,128)(2,1)S(1)} %copy-done.53), channel_id=1, source_target_pairs={{0,3},{1,2},{2,1},{3,0},{4,7},{5,6},{6,5},{7,4},{8,11},{9,10},{10,... | collective-permute-start | bytes 147464 | tf_op jit(solution)/shard_map/ppermute | solution.py:21
  164.1 2.8 collective-permute-done.30
  169.2 1.9 collective-permute-start.34
  171.0 20.4 %shard_map.243 = (bf16[2,256,192]{2,1,0:T(8,128)(2,1)}, bf16[4,2,256,384]{3,2,1,0:T(8,128)(2,1)}, bf16[4,2,256,384]{3,2,1,0:T(8,128)(2,1)}) custom-call(s32[19]{0:T(128)} %pad_add_fusion.1.meta, bf16[2,256,256]{2,1,0:T(8,128)(2,1)} %get-tuple-element.98.refs_0_, bf16[2,256,384]{2,1,0:T(8,128)(2,1)} %get-tuple-element.100.refs_1_, ...), custom_call_target="tpu_custom_call" | custom-call | flops 32212254720 | bytes 1048576 | tf_op jit(solution)/shard_map/pallas_call | solution.py:421
  191.6 4.1 %reduce-scatter.3.cloned.1.call-done = bf16[128,768]{1,0:T(8,128)(2,1)} async-done(((bf16[1024,768]{1,0:T(8,128)(2,1)}), bf16[128,768]{1,0:T(8,128)(2,1)}) %reduce-scatter.3.cloned.1.call-update) | async-done | bytes 196624 | tf_op jit(solution)/shard_map/reduce_scatter | solution.py:632
  195.7 3.6 %collective-permute-done.35 = bf16[4,2,256,384]{3,2,1,0:T(8,128)(2,1)S(1)} collective-permute-done((bf16[4,2,256,384]{3,2,1,0:T(8,128)(2,1)}, bf16[4,2,256,384]{3,2,1,0:T(8,128)(2,1)S(1)}, u32[]{:S(2)}, u32[]{:S(2)}) %collective-permute-start.35) | collective-permute-done | bytes 1572896 | tf_op jit(solution)/shard_map/ppermute | solution.py:21
  204.4 9.4 %collective-permute-done.38.refs_3_ = bf16[2,256,384]{2,1,0:T(8,128)(2,1)S(1)} collective-permute-done((bf16[2,256,384]{2,1,0:T(8,128)(2,1)}, bf16[2,256,384]{2,1,0:T(8,128)(2,1)S(1)}, u32[]{:S(2)}, u32[]{:S(2)}) %collective-permute-start.38) | collective-permute-done | bytes 393248 | tf_op jit(solution)/shard_map/ppermute | solution.py:21
  213.8 7.6 %collective-permute-done.37.refs_2_ = bf16[2,256,384]{2,1,0:T(8,128)(2,1)S(1)} collective-permute-done((bf16[2,256,384]{2,1,0:T(8,128)(2,1)}, bf16[2,256,384]{2,1,0:T(8,128)(2,1)S(1)}, u32[]{:S(2)}, u32[]{:S(2)}) %collective-permute-start.37) | collective-permute-done | bytes 393248 | tf_op jit(solution)/shard_map/ppermute | solution.py:21
  222.3 6.7 %shard_map.244 = (bf16[2,64,768]{2,1,0:T(8,128)(2,1)}, bf16[2,64,768]{2,1,0:T(8,128)(2,1)}, bf16[2,64,768]{2,1,0:T(8,128)(2,1)}, bf16[2,64,768]{2,1,0:T(8,128)(2...) custom-call(s32[3]{0:T(128)} %pad_add_fusion.meta, ...), custom_call_target="tpu_custom_call" | custom-call | bytes 1048576 | tf_op jit(solution)/shard_map/pallas_call | solution.py:421
  231.8 2.5 collective-permute-start.39
  234.5 1.5 collective-permute-start.43
  238.8 13.8 %collective-permute-done.39 = bf16[2,2,64,768]{3,2,1,0:T(8,128)(2,1)S(1)} collective-permute-done((bf16[2,2,64,768]{3,2,1,0:T(8,128)(2,1)S(1)}, bf16[2,2,64,768]{3,2,1,0:T(8,128)(2,1)S(1)}, u32[]{:S(2)}, u32[]{:S(2)}) %collective-permute-start.39) | collective-permute-done | bytes 393248 | tf_op jit(solution)/shard_map/ppermute | solution.py:21
  253.4 1.6 collective-permute-start.44
  255.0 3.3 %collective-permute-start.47 = (bf16[32,576]{1,0:T(8,128)(2,1)S(1)}, bf16[32,576]{1,0:T(8,128)(2,1)S(1)}, u32[]{:S(2)}, u32[]{:S(2)}) collective-permute-start(bf16[32,576]{1,0:T(8,128)(2,1)S(1)} %get-tuple-element.200), channel_id=1, source_target_pairs={{0,3},{1,2},{2,1},{3,0},{4,7},{5,6},{6,5},{7,4},{8,11},{9,10},{10,... | collective-permute-start | bytes 110600 | tf_op jit(solution)/shard_map/ppermute | solution.py:21
  258.3 5.2 %collective-permute-done.46 = bf16[32,576]{1,0:T(8,128)(2,1)S(1)} collective-permute-done((bf16[32,576]{1,0:T(8,128)(2,1)S(1)}, bf16[32,576]{1,0:T(8,128)(2,1)S(1)}, u32[]{:S(2)}, u32[]{:S(2)}) %collective-permute-start.46) | collective-permute-done | bytes 36896 | tf_op jit(solution)/shard_map/ppermute | solution.py:21
  264.3 1.5 collective-permute-start.50
  269.9 2.9 %shard_map.245 = f32[128,768]{1,0:T(8,128)} custom-call(s32[3]{0:T(128)} %pad_add_fusion.meta, bf16[2,64,768]{2,1,0:T(8,128)(2,1)} %fusion.11.grad_ref, bf16[128,768]{1,0:T(8,128)(2,1)} %bitcast.143, f32[1,768]{1,0:T(1,128)} %reshape.210.gain_ref, f32[128,768]{1,0:T(8,128)} %get-tuple-element.153.resid_grad_ref), custom_call_target="tpu_custom_call" | custom-call | bytes 1048576 | tf_op jit(solution)/shard_map/pallas_call | solution.py:421
  273.2 3.9 %collective-permute-done.49.refs_2_ = bf16[5,32,576]{2,1,0:T(8,128)(2,1)S(1)} collective-permute-done((bf16[5,32,576]{2,1,0:T(8,128)(2,1)S(1)}, bf16[5,32,576]{2,1,0:T(8,128)(2,1)S(1)}, u32[]{:S(2)}, u32[]{:S(2)}) %collective-permute-start.49) | collective-permute-done | bytes 184352 | tf_op jit(solution)/shard_map/ppermute | solution.py:21
  277.6 4.4 %fusion.51 = (f32[8,1,96,768]{3,2,1,0:T(8,128)}, f32[8,1,96,768]{3,2,1,0:T(8,128)}) fusion(bf16[8,2,96,768]{3,2,1,0:T(8,128)(2,1)} %bitcast.135), kind=kLoop, calls=%fused_computation.156 | loop fusion | bytes 9437184 | tf_op jit(solution)/shard_map/slice | solution.py:728
  282.9 4.1 %shard_map.246 = (f32[192,2304]{1,0:T(8,128)}, f32[192,768]{1,0:T(8,128)}) custom-call(s32[3]{0:T(128)} %pad_add_fusion.meta, bf16[5,32,576]{2,1,0:T(8,128)(2,1)} %copy-done.12, bf16[5,32,576]{2,1,0:T(8,128)(2,1)} %copy-done.20, bf16[5,32,576]{2,1,0:T(8,128)(2,1)} %copy-done.19, bf16[5,32,576]{2,1,0:T(8,128)(2,1)} %copy-done.18, ...), custom_call_target="tpu_custom_call" | custom-call | bytes 1048576 | tf_op jit(solution)/shard_map/pallas_call | solution.py:421
  (297 shorter events, 58.6 us)
Async XLA Ops:
  7.2 46.1 %all-gather.7.cloned.1.call-start = ((), (), s32[]{:S(2)}) async-start(), calls=%async_computation.3 | async-start | bytes 1769472 | tf_op jit(solution)/shard_map/all_gather | solution.py:545
  7.9 91.6 %all-gather.5.cloned.1.call-start = ((), (), s32[]{:S(2)}) async-start(), calls=%async_computation.2 | async-start | bytes 1597440 | tf_op jit(solution)/shard_map/all_gather | solution.py:553
  9.9 5.7 %collective-permute-start = (bf16[64,576]{1,0:T(8,128)(2,1)S(1)}, bf16[64,576]{1,0:T(8,128)(2,1)S(1)}, u32[]{:S(2)}, u32[]{:S(2)}) collective-permute-start(bf16[64,576]{1,0:T(8,128)(2,1)S(1)} %get-tuple-element.194), channel_id=1, source_target_pairs={{0,1},{1,0},{2,3},{3,2},{4,5},{5,4},{6,7},{7,6},{8,9},{9,8},{10,11... | collective-permute-start | bytes 221192 | tf_op jit(solution)/shard_map/ppermute | solution.py:21
  13.0 9.2 %collective-permute-start.1 = (bf16[64,576]{1,0:T(8,128)(2,1)S(1)}, bf16[64,576]{1,0:T(8,128)(2,1)S(1)}, u32[]{:S(2)}, u32[]{:S(2)}) collective-permute-start(bf16[64,576]{1,0:T(8,128)(2,1)S(1)} %get-tuple-element.195), channel_id=1, source_target_pairs={{0,2},{1,3},{2,0},{3,1},{4,6},{5,7},{6,4},{7,5},{8,10},{9,11},{10,... | collective-permute-start | bytes 221192 | tf_op jit(solution)/shard_map/ppermute | solution.py:21
  15.6 6.6 %collective-permute-start.2 = (bf16[64,576]{1,0:T(8,128)(2,1)S(1)}, bf16[64,576]{1,0:T(8,128)(2,1)S(1)}, u32[]{:S(2)}, u32[]{:S(2)}) collective-permute-start(bf16[64,576]{1,0:T(8,128)(2,1)S(1)} %get-tuple-element.196), channel_id=1, source_target_pairs={{0,3},{1,2},{2,1},{3,0},{4,7},{5,6},{6,5},{7,4},{8,11},{9,10},{10,... | collective-permute-start | bytes 221192 | tf_op jit(solution)/shard_map/ppermute | solution.py:21
  22.3 9.6 %collective-permute-start.5 = (bf16[2,64,768]{2,1,0:T(8,128)(2,1)S(1)}, bf16[2,64,768]{2,1,0:T(8,128)(2,1)S(1)}, u32[]{:S(2)}, u32[]{:S(2)}) collective-permute-start(bf16[2,64,768]{2,1,0:T(8,128)(2,1)S(1)} %bitcast.144), channel_id=1, source_target_pairs={{0,3},{1,2},{2,1},{3,0},{4,7},{5,6},{6,5},{7,4},{8,11},{9,10},{10,... | collective-permute-start | bytes 589832 | tf_op jit(solution)/shard_map/ppermute | solution.py:21
  25.0 16.5 %collective-permute-start.4 = (bf16[2,64,768]{2,1,0:T(8,128)(2,1)S(1)}, bf16[2,64,768]{2,1,0:T(8,128)(2,1)S(1)}, u32[]{:S(2)}, u32[]{:S(2)}) collective-permute-start(bf16[2,64,768]{2,1,0:T(8,128)(2,1)S(1)} %bitcast.145), channel_id=1, source_target_pairs={{0,2},{1,3},{2,0},{3,1},{4,6},{5,7},{6,4},{7,5},{8,10},{9,11},{10,... | collective-permute-start | bytes 589832 | tf_op jit(solution)/shard_map/ppermute | solution.py:21
  25.5 16.0 %collective-permute-start.3 = (bf16[2,64,768]{2,1,0:T(8,128)(2,1)S(1)}, bf16[2,64,768]{2,1,0:T(8,128)(2,1)S(1)}, u32[]{:S(2)}, u32[]{:S(2)}) collective-permute-start(bf16[2,64,768]{2,1,0:T(8,128)(2,1)S(1)} %bitcast.146), channel_id=1, source_target_pairs={{0,1},{1,0},{2,3},{3,2},{4,5},{5,4},{6,7},{7,6},{8,9},{9,8},{10,11... | collective-permute-start | bytes 589832 | tf_op jit(solution)/shard_map/ppermute | solution.py:21
  27.0 14.5 %collective-permute-start.8 = (bf16[4,48,576]{2,1,0:T(8,128)(2,1)S(1)}, bf16[4,48,576]{2,1,0:T(8,128)(2,1)S(1)}, u32[]{:S(2)}, u32[]{:S(2)}) collective-permute-start(bf16[4,48,576]{2,1,0:T(8,128)(2,1)S(1)} %slice.272.refs_5_), channel_id=1, source_target_pairs={{0,24},{4,28},{8,16},{12,20},{16,8},{20,12},{24,0},{28,4},{1,25},{... | collective-permute-start | bytes 663560 | tf_op jit(solution)/shard_map/ppermute | solution.py:21
  29.4 12.8 %collective-permute-start.7 = (bf16[4,48,576]{2,1,0:T(8,128)(2,1)S(1)}, bf16[4,48,576]{2,1,0:T(8,128)(2,1)S(1)}, u32[]{:S(2)}, u32[]{:S(2)}) collective-permute-start(bf16[4,48,576]{2,1,0:T(8,128)(2,1)S(1)} %slice.272.refs_5_), channel_id=1, source_target_pairs={{0,16},{4,20},{8,24},{12,28},{16,0},{20,4},{24,8},{28,12},{1,17},{... | collective-permute-start | bytes 663560 | tf_op jit(solution)/shard_map/ppermute | solution.py:21
  31.9 10.5 %collective-permute-start.6 = (bf16[4,48,576]{2,1,0:T(8,128)(2,1)S(1)}, bf16[4,48,576]{2,1,0:T(8,128)(2,1)S(1)}, u32[]{:S(2)}, u32[]{:S(2)}) collective-permute-start(bf16[4,48,576]{2,1,0:T(8,128)(2,1)S(1)} %slice.272.refs_5_), channel_id=1, source_target_pairs={{0,8},{4,12},{8,0},{12,4},{16,24},{20,28},{24,16},{28,20},{1,9},{5... | collective-permute-start | bytes 663560 | tf_op jit(solution)/shard_map/ppermute | solution.py:21
  42.4 83.7 %all-gather.9.cloned.1.call-start = ((), (), s32[]{:S(2)}) async-start(), calls=%async_computation.4 | async-start | bytes 1474560 | tf_op jit(solution)/shard_map/all_gather | solution.py:573
  48.7 13.2 %collective-permute-start.11 = (bf16[2,256,384]{2,1,0:T(8,128)(2,1)}, bf16[2,256,384]{2,1,0:T(8,128)(2,1)S(1)}, u32[]{:S(2)}, u32[]{:S(2)}) collective-permute-start(bf16[2,256,384]{2,1,0:T(8,128)(2,1)} %get-tuple-element.100.refs_1_), channel_id=1, source_target_pairs={{0,24},{4,28},{8,16},{12,20},{16,8},{20,12},{24,0},{28,4},{1,25},{... | collective-permute-start | bytes 1179656 | tf_op jit(solution)/shard_map/ppermute | solution.py:21
  50.5 18.1 %collective-permute-start.10 = (bf16[2,256,384]{2,1,0:T(8,128)(2,1)}, bf16[2,256,384]{2,1,0:T(8,128)(2,1)S(1)}, u32[]{:S(2)}, u32[]{:S(2)}) collective-permute-start(bf16[2,256,384]{2,1,0:T(8,128)(2,1)} %get-tuple-element.100.refs_1_), channel_id=1, source_target_pairs={{0,16},{4,20},{8,24},{12,28},{16,0},{20,4},{24,8},{28,12},{1,17},{... | collective-permute-start | bytes 1179656 | tf_op jit(solution)/shard_map/ppermute | solution.py:21
  51.7 17.0 %collective-permute-start.9 = (bf16[2,256,384]{2,1,0:T(8,128)(2,1)}, bf16[2,256,384]{2,1,0:T(8,128)(2,1)S(1)}, u32[]{:S(2)}, u32[]{:S(2)}) collective-permute-start(bf16[2,256,384]{2,1,0:T(8,128)(2,1)} %get-tuple-element.100.refs_1_), channel_id=1, source_target_pairs={{0,8},{4,12},{8,0},{12,4},{16,24},{20,28},{24,16},{28,20},{1,9},{5... | collective-permute-start | bytes 1179656 | tf_op jit(solution)/shard_map/ppermute | solution.py:21
  72.4 123.3 %reduce-scatter.3.cloned.1.call-start = ((), (), s32[]{:S(2)}) async-start(), calls=%async_computation.5 | async-start | bytes 1769472 | tf_op jit(solution)/shard_map/reduce_scatter | solution.py:632
  93.8 10.7 %collective-permute-start.16 = (bf16[2,64,192]{2,1,0:T(8,128)(2,1)}, bf16[2,64,192]{2,1,0:T(8,128)(2,1)S(1)}, u32[]{:S(2)}, u32[]{:S(2)}) collective-permute-start(bf16[2,64,192]{2,1,0:T(8,128)(2,1)} %get-tuple-element.105.refs_11_), channel_id=1, source_target_pairs={{0,1},{1,0},{2,3},{3,2},{4,5},{5,4},{6,7},{7,6},{8,9},{9,8},{10,11... | collective-permute-start | bytes 147464 | tf_op jit(solution)/shard_map/ppermute | solution.py:21
  97.1 12.5 %collective-permute-start.17 = (bf16[2,64,192]{2,1,0:T(8,128)(2,1)}, bf16[2,64,192]{2,1,0:T(8,128)(2,1)S(1)}, u32[]{:S(2)}, u32[]{:S(2)}) collective-permute-start(bf16[2,64,192]{2,1,0:T(8,128)(2,1)} %get-tuple-element.106.refs_12_), channel_id=1, source_target_pairs={{0,2},{1,3},{2,0},{3,1},{4,6},{5,7},{6,4},{7,5},{8,10},{9,11},{10,... | collective-permute-start | bytes 147464 | tf_op jit(solution)/shard_map/ppermute | solution.py:21
  97.1 12.5 %collective-permute-start.18 = (bf16[2,64,192]{2,1,0:T(8,128)(2,1)}, bf16[2,64,192]{2,1,0:T(8,128)(2,1)S(1)}, u32[]{:S(2)}, u32[]{:S(2)}) collective-permute-start(bf16[2,64,192]{2,1,0:T(8,128)(2,1)} %get-tuple-element.107.refs_13_), channel_id=1, source_target_pairs={{0,3},{1,2},{2,1},{3,0},{4,7},{5,6},{6,5},{7,4},{8,11},{9,10},{10,... | collective-permute-start | bytes 147464 | tf_op jit(solution)/shard_map/ppermute | solution.py:21
  113.6 8.6 %collective-permute-start.21 = (bf16[128,768]{1,0:T(8,128)(2,1)}, bf16[128,768]{1,0:T(8,128)(2,1)S(1)}, u32[]{:S(2)}, u32[]{:S(2)}) collective-permute-start(bf16[128,768]{1,0:T(8,128)(2,1)} %get-tuple-element.115), channel_id=1, source_target_pairs={{0,24},{4,28},{8,16},{12,20},{16,8},{20,12},{24,0},{28,4},{1,25},{... | collective-permute-start | bytes 589832 | tf_op jit(solution)/shard_map/ppermute | solution.py:21
  115.7 8.5 %collective-permute-start.20 = (bf16[128,768]{1,0:T(8,128)(2,1)}, bf16[128,768]{1,0:T(8,128)(2,1)S(1)}, u32[]{:S(2)}, u32[]{:S(2)}) collective-permute-start(bf16[128,768]{1,0:T(8,128)(2,1)} %get-tuple-element.115), channel_id=1, source_target_pairs={{0,16},{4,20},{8,24},{12,28},{16,0},{20,4},{24,8},{28,12},{1,17},{... | collective-permute-start | bytes 589832 | tf_op jit(solution)/shard_map/ppermute | solution.py:21
  116.5 7.8 %collective-permute-start.19 = (bf16[128,768]{1,0:T(8,128)(2,1)}, bf16[128,768]{1,0:T(8,128)(2,1)S(1)}, u32[]{:S(2)}, u32[]{:S(2)}) collective-permute-start(bf16[128,768]{1,0:T(8,128)(2,1)} %get-tuple-element.115), channel_id=1, source_target_pairs={{0,8},{4,12},{8,0},{12,4},{16,24},{20,28},{24,16},{28,20},{1,9},{5... | collective-permute-start | bytes 589832 | tf_op jit(solution)/shard_map/ppermute | solution.py:21
  118.1 6.8 %collective-permute-start.22 = (bf16[128,768]{1,0:T(8,128)(2,1)}, bf16[128,768]{1,0:T(8,128)(2,1)S(1)}, u32[]{:S(2)}, u32[]{:S(2)}) collective-permute-start(bf16[128,768]{1,0:T(8,128)(2,1)} %get-tuple-element.115), channel_id=1, source_target_pairs={{0,4},{4,0},{8,12},{12,8},{16,20},{20,16},{24,28},{28,24},{1,5},{5... | collective-permute-start | bytes 589832 | tf_op jit(solution)/shard_map/ppermute | solution.py:21
  136.7 8.7 %collective-permute-start.29 = (bf16[128,768]{1,0:T(8,128)(2,1)S(1)}, bf16[128,768]{1,0:T(8,128)(2,1)S(1)}, u32[]{:S(2)}, u32[]{:S(2)}) collective-permute-start(bf16[128,768]{1,0:T(8,128)(2,1)S(1)} %get-tuple-element.183), channel_id=1, source_target_pairs={{0,24},{4,28},{8,16},{12,20},{16,8},{20,12},{24,0},{28,4},{1,25},{... | collective-permute-start | bytes 589832 | tf_op jit(solution)/shard_map/ppermute | solution.py:21
  138.5 10.4 %collective-permute-start.28 = (bf16[128,768]{1,0:T(8,128)(2,1)S(1)}, bf16[128,768]{1,0:T(8,128)(2,1)S(1)}, u32[]{:S(2)}, u32[]{:S(2)}) collective-permute-start(bf16[128,768]{1,0:T(8,128)(2,1)S(1)} %get-tuple-element.184), channel_id=1, source_target_pairs={{0,16},{4,20},{8,24},{12,28},{16,0},{20,4},{24,8},{28,12},{1,17},{... | collective-permute-start | bytes 589832 | tf_op jit(solution)/shard_map/ppermute | solution.py:21
  139.7 9.3 %collective-permute-start.27 = (bf16[128,768]{1,0:T(8,128)(2,1)S(1)}, bf16[128,768]{1,0:T(8,128)(2,1)S(1)}, u32[]{:S(2)}, u32[]{:S(2)}) collective-permute-start(bf16[128,768]{1,0:T(8,128)(2,1)S(1)} %get-tuple-element.185), channel_id=1, source_target_pairs={{0,8},{4,12},{8,0},{12,4},{16,24},{20,28},{24,16},{28,20},{1,9},{5... | collective-permute-start | bytes 589832 | tf_op jit(solution)/shard_map/ppermute | solution.py:21
  153.8 13.0 %collective-permute-start.30 = (bf16[1,128,768]{2,1,0:T(8,128)(2,1)}, bf16[1,128,768]{2,1,0:T(8,128)(2,1)S(1)}, u32[]{:S(2)}, u32[]{:S(2)}) collective-permute-start(bf16[1,128,768]{2,1,0:T(8,128)(2,1)} %bitcast.167), channel_id=1, source_target_pairs={{0,1},{1,0},{2,3},{3,2},{4,5},{5,4},{6,7},{7,6},{8,9},{9,8},{10,11... | collective-permute-start | bytes 589832 | tf_op jit(solution)/shard_map/ppermute | solution.py:21
  159.5 69.5 %reduce-scatter.5.cloned.1.call-start = ((), (), s32[]{:S(2)}) async-start(), calls=%async_computation.6 | async-start | bytes 1474560 | tf_op jit(solution)/shard_map/reduce_scatter | solution.py:672
  159.6 8.7 %collective-permute-start.31 = (bf16[2,64,192]{2,1,0:T(8,128)(2,1)S(1)}, bf16[2,64,192]{2,1,0:T(8,128)(2,1)S(1)}, u32[]{:S(2)}, u32[]{:S(2)}) collective-permute-start(bf16[2,64,192]{2,1,0:T(8,128)(2,1)S(1)} %copy-done.57), channel_id=1, source_target_pairs={{0,1},{1,0},{2,3},{3,2},{4,5},{5,4},{6,7},{7,6},{8,9},{9,8},{10,11... | collective-permute-start | bytes 147464 | tf_op jit(solution)/shard_map/ppermute | solution.py:21
  160.3 8.1 %collective-permute-start.32 = (bf16[2,64,192]{2,1,0:T(8,128)(2,1)S(1)}, bf16[2,64,192]{2,1,0:T(8,128)(2,1)S(1)}, u32[]{:S(2)}, u32[]{:S(2)}) collective-permute-start(bf16[2,64,192]{2,1,0:T(8,128)(2,1)S(1)} %copy-done.55), channel_id=1, source_target_pairs={{0,2},{1,3},{2,0},{3,1},{4,6},{5,7},{6,4},{7,5},{8,10},{9,11},{10,... | collective-permute-start | bytes 147464 | tf_op jit(solution)/shard_map/ppermute | solution.py:21
  160.7 8.5 %collective-permute-start.33 = (bf16[2,64,192]{2,1,0:T(8,128)(2,1)S(1)}, bf16[2,64,192]{2,1,0:T(8,128)(2,1)S(1)}, u32[]{:S(2)}, u32[]{:S(2)}) collective-permute-start(bf16[2,64,192]{2,1,0:T(8,128)(2,1)S(1)} %copy-done.53), channel_id=1, source_target_pairs={{0,3},{1,2},{2,1},{3,0},{4,7},{5,6},{6,5},{7,4},{8,11},{9,10},{10,... | collective-permute-start | bytes 147464 | tf_op jit(solution)/shard_map/ppermute | solution.py:21
  169.2 22.3 %collective-permute-start.34 = (bf16[2,128,768]{2,1,0:T(8,128)(2,1)S(1)}, bf16[2,128,768]{2,1,0:T(8,128)(2,1)S(1)}, u32[]{:S(2)}, u32[]{:S(2)}) collective-permute-start(bf16[2,128,768]{2,1,0:T(8,128)(2,1)S(1)} %pad_maximum_fusion.1), channel_id=1, source_target_pairs={{0,2},{1,3},{2,0},{3,1},{4,6},{5,7},{6,4},{7,5},{8,10},{9,11},{10,... | collective-permute-start | bytes 1179656 | tf_op jit(solution)/shard_map/ppermute | solution.py:21
  191.6 86.0 %all-gather.11.cloned.1.call-start = ((), (), s32[]{:S(2)}) async-start(), calls=%async_computation.7 | async-start | bytes 2654208 | tf_op jit(solution)/shard_map/all_gather | solution.py:697
  200.7 13.1 %collective-permute-start.38 = (bf16[2,256,384]{2,1,0:T(8,128)(2,1)}, bf16[2,256,384]{2,1,0:T(8,128)(2,1)S(1)}, u32[]{:S(2)}, u32[]{:S(2)}) collective-permute-start(bf16[2,256,384]{2,1,0:T(8,128)(2,1)} %get-tuple-element.177), channel_id=1, source_target_pairs={{0,24},{4,28},{8,16},{12,20},{16,8},{20,12},{24,0},{28,4},{1,25},{... | collective-permute-start | bytes 1179656 | tf_op jit(solution)/shard_map/ppermute | solution.py:21
  202.2 19.3 %collective-permute-start.37 = (bf16[2,256,384]{2,1,0:T(8,128)(2,1)}, bf16[2,256,384]{2,1,0:T(8,128)(2,1)S(1)}, u32[]{:S(2)}, u32[]{:S(2)}) collective-permute-start(bf16[2,256,384]{2,1,0:T(8,128)(2,1)} %get-tuple-element.178), channel_id=1, source_target_pairs={{0,16},{4,20},{8,24},{12,28},{16,0},{20,4},{24,8},{28,12},{1,17},{... | collective-permute-start | bytes 1179656 | tf_op jit(solution)/shard_map/ppermute | solution.py:21
  203.6 17.8 %collective-permute-start.36 = (bf16[2,256,384]{2,1,0:T(8,128)(2,1)}, bf16[2,256,384]{2,1,0:T(8,128)(2,1)S(1)}, u32[]{:S(2)}, u32[]{:S(2)}) collective-permute-start(bf16[2,256,384]{2,1,0:T(8,128)(2,1)} %get-tuple-element.179), channel_id=1, source_target_pairs={{0,8},{4,12},{8,0},{12,4},{16,24},{20,28},{24,16},{28,20},{1,9},{5... | collective-permute-start | bytes 1179656 | tf_op jit(solution)/shard_map/ppermute | solution.py:21
  231.8 20.8 %collective-permute-start.39 = (bf16[2,2,64,768]{3,2,1,0:T(8,128)(2,1)S(1)}, bf16[2,2,64,768]{3,2,1,0:T(8,128)(2,1)S(1)}, u32[]{:S(2)}, u32[]{:S(2)}) collective-permute-start(bf16[2,2,64,768]{3,2,1,0:T(8,128)(2,1)S(1)} %pad_maximum_fusion.2), channel_id=1, source_target_pairs={{0,2},{1,3},{2,0},{3,1},{4,6},{5,7},{6,4},{7,5},{8,10},{9,11},{10,... | collective-permute-start | bytes 1179656 | tf_op jit(solution)/shard_map/ppermute | solution.py:21
  234.5 18.1 %collective-permute-start.43 = (bf16[5,32,576]{2,1,0:T(8,128)(2,1)S(1)}, bf16[5,32,576]{2,1,0:T(8,128)(2,1)S(1)}, u32[]{:S(2)}, u32[]{:S(2)}) collective-permute-start(bf16[5,32,576]{2,1,0:T(8,128)(2,1)S(1)} %get-tuple-element.187), channel_id=1, source_target_pairs={{0,24},{4,28},{8,16},{12,20},{16,8},{20,12},{24,0},{28,4},{1,25},{... | collective-permute-start | bytes 552968 | tf_op jit(solution)/shard_map/ppermute | solution.py:21
  236.1 16.6 %collective-permute-start.42 = (bf16[5,32,576]{2,1,0:T(8,128)(2,1)S(1)}, bf16[5,32,576]{2,1,0:T(8,128)(2,1)S(1)}, u32[]{:S(2)}, u32[]{:S(2)}) collective-permute-start(bf16[5,32,576]{2,1,0:T(8,128)(2,1)S(1)} %get-tuple-element.188), channel_id=1, source_target_pairs={{0,16},{4,20},{8,24},{12,28},{16,0},{20,4},{24,8},{28,12},{1,17},{... | collective-permute-start | bytes 552968 | tf_op jit(solution)/shard_map/ppermute | solution.py:21
  237.5 15.2 %collective-permute-start.41 = (bf16[5,32,576]{2,1,0:T(8,128)(2,1)S(1)}, bf16[5,32,576]{2,1,0:T(8,128)(2,1)S(1)}, u32[]{:S(2)}, u32[]{:S(2)}) collective-permute-start(bf16[5,32,576]{2,1,0:T(8,128)(2,1)S(1)} %get-tuple-element.189), channel_id=1, source_target_pairs={{0,8},{4,12},{8,0},{12,4},{16,24},{20,28},{24,16},{28,20},{1,9},{5... | collective-permute-start | bytes 552968 | tf_op jit(solution)/shard_map/ppermute | solution.py:21
  252.8 5.5 %collective-permute-start.45 = (bf16[32,576]{1,0:T(8,128)(2,1)S(1)}, bf16[32,576]{1,0:T(8,128)(2,1)S(1)}, u32[]{:S(2)}, u32[]{:S(2)}) collective-permute-start(bf16[32,576]{1,0:T(8,128)(2,1)S(1)} %get-tuple-element.202), channel_id=1, source_target_pairs={{0,1},{1,0},{2,3},{3,2},{4,5},{5,4},{6,7},{7,6},{8,9},{9,8},{10,11... | collective-permute-start | bytes 110600 | tf_op jit(solution)/shard_map/ppermute | solution.py:21
  253.4 15.8 %collective-permute-start.44 = (bf16[1,2,64,768]{3,2,1,0:T(8,128)(2,1)S(1)}, bf16[1,2,64,768]{3,2,1,0:T(8,128)(2,1)S(1)}, u32[]{:S(2)}, u32[]{:S(2)}) collective-permute-start(bf16[1,2,64,768]{3,2,1,0:T(8,128)(2,1)S(1)} %fusion.22), channel_id=1, source_target_pairs={{0,1},{1,0},{2,3},{3,2},{4,5},{5,4},{6,7},{7,6},{8,9},{9,8},{10,11... | collective-permute-start | bytes 589832 | tf_op jit(solution)/shard_map/ppermute | solution.py:21
  255.0 9.2 %collective-permute-start.47 = (bf16[32,576]{1,0:T(8,128)(2,1)S(1)}, bf16[32,576]{1,0:T(8,128)(2,1)S(1)}, u32[]{:S(2)}, u32[]{:S(2)}) collective-permute-start(bf16[32,576]{1,0:T(8,128)(2,1)S(1)} %get-tuple-element.200), channel_id=1, source_target_pairs={{0,3},{1,2},{2,1},{3,0},{4,7},{5,6},{6,5},{7,4},{8,11},{9,10},{10,... | collective-permute-start | bytes 110600 | tf_op jit(solution)/shard_map/ppermute | solution.py:21
  264.2 17.8 %collective-permute-start.51 = (bf16[5,32,576]{2,1,0:T(8,128)(2,1)S(1)}, bf16[5,32,576]{2,1,0:T(8,128)(2,1)S(1)}, u32[]{:S(2)}, u32[]{:S(2)}) collective-permute-start(bf16[5,32,576]{2,1,0:T(8,128)(2,1)S(1)} %slice_dynamic-update-slice_fusion.refs_0_), channel_id=1, source_target_pairs={{0,4},{4,0},{8,12},{12,8},{16,20},{20,16},{24,28},{28,24},{1,5},{5... | collective-permute-start | bytes 552968 | tf_op jit(solution)/shard_map/ppermute | solution.py:21
  264.3 8.9 %collective-permute-start.50 = (bf16[5,32,576]{2,1,0:T(8,128)(2,1)S(1)}, bf16[5,32,576]{2,1,0:T(8,128)(2,1)S(1)}, u32[]{:S(2)}, u32[]{:S(2)}) collective-permute-start(bf16[5,32,576]{2,1,0:T(8,128)(2,1)S(1)} %slice_dynamic-update-slice_fusion.refs_0_), channel_id=1, source_target_pairs={{0,24},{4,28},{8,16},{12,20},{16,8},{20,12},{24,0},{28,4},{1,25},{... | collective-permute-start | bytes 552968 | tf_op jit(solution)/shard_map/ppermute | solution.py:21
  265.8 11.3 %collective-permute-start.49 = (bf16[5,32,576]{2,1,0:T(8,128)(2,1)S(1)}, bf16[5,32,576]{2,1,0:T(8,128)(2,1)S(1)}, u32[]{:S(2)}, u32[]{:S(2)}) collective-permute-start(bf16[5,32,576]{2,1,0:T(8,128)(2,1)S(1)} %slice_dynamic-update-slice_fusion.refs_0_), channel_id=1, source_target_pairs={{0,16},{4,20},{8,24},{12,28},{16,0},{20,4},{24,8},{28,12},{1,17},{... | collective-permute-start | bytes 552968 | tf_op jit(solution)/shard_map/ppermute | solution.py:21
  267.2 9.9 %collective-permute-start.48 = (bf16[5,32,576]{2,1,0:T(8,128)(2,1)S(1)}, bf16[5,32,576]{2,1,0:T(8,128)(2,1)S(1)}, u32[]{:S(2)}, u32[]{:S(2)}) collective-permute-start(bf16[5,32,576]{2,1,0:T(8,128)(2,1)S(1)} %slice_dynamic-update-slice_fusion.refs_0_), channel_id=1, source_target_pairs={{0,8},{4,12},{8,0},{12,4},{16,24},{20,28},{24,16},{28,20},{1,9},{5... | collective-permute-start | bytes 552968 | tf_op jit(solution)/shard_map/ppermute | solution.py:21
  273.2 8.8 %collective-permute-start.54 = (bf16[5,32,576]{2,1,0:T(8,128)(2,1)S(1)}, bf16[5,32,576]{2,1,0:T(8,128)(2,1)S(1)}, u32[]{:S(2)}, u32[]{:S(2)}) collective-permute-start(bf16[5,32,576]{2,1,0:T(8,128)(2,1)S(1)} %collective-permute-done.50.refs_3_), channel_id=1, source_target_pairs={{0,4},{4,0},{8,12},{12,8},{16,20},{20,16},{24,28},{28,24},{1,5},{5... | collective-permute-start | bytes 552968 | tf_op jit(solution)/shard_map/ppermute | solution.py:21
  (71 other events, 488.3 us)
Sparse Core Ops, SparseCore 0:
  9.9 33.3 all-gather.6
  45.5 31.6 all-gather.4
  78.7 35.3 all-gather.8
  159.7 35.9 reduce-scatter.2
  197.8 29.1 reduce-scatter.4
  229.2 33.5 all-gather.10

commit v2 on v1

--- a/solution.py
+++ b/solution.py
@@ -92,14 +92,6 @@
     return lax.dot_general(left, right, (((1,), (1,)), ((), ())), preferred_element_type=F32)
 
 
-def head_rows(values, at, heads):
-    rows = lax.broadcasted_iota(jnp.int32, values.shape, 0) - at
-    return [
-        jnp.where((rows >= h * HEAD_DIM) & (rows < (h + 1) * HEAD_DIM), values, 0.0).astype(BF16)
-        for h in range(heads)
-    ]
-
-
 def head_cols(values, at, heads):
     cols = lax.broadcasted_iota(jnp.int32, values.shape, 1) - at
     return [
@@ -108,10 +100,20 @@
     ]
 
 
-def causal_mask(size, flip):
-    keys = lax.broadcasted_iota(jnp.int32, (size, size), 0) ^ flip
-    queries = lax.broadcasted_iota(jnp.int32, (size, size), 1) ^ flip
+def causal_mask(heads, size, flip):
+    queries = lax.broadcasted_iota(jnp.int32, (heads * size, size), 0) % size ^ flip
+    keys = lax.broadcasted_iota(jnp.int32, (heads * size, size), 1) ^ flip
     return keys <= queries
+
+
+def lanes(combine, values):
+    return functools.reduce(
+        combine, [values[:, i : i + 128] for i in range(0, values.shape[1], 128)]
+    )
+
+
+def widen(values, width):
+    return jnp.concatenate([values] * (width // 128), axis=1)
 
 
 def load_pieces(pieces, kv_ref, sems):
@@ -124,11 +126,27 @@
     return copies
 
 
-def attend_kernel(meta, *refs, heads, pieces, groups):
+def in_pairs(start, stop, step):
+    def both(i, carry):
+        step((start + 2 * i, start + 2 * i + 1))
+        return carry
+
+    def one(n, carry):
+        step((n,))
+        return carry
+
+    half = (stop - start) // 2
+    lax.fori_loop(0, half, both, 0)
+    lax.fori_loop(start + 2 * half, stop, one, 0)
+
+
+def attend_kernel(meta, *refs, heads, pieces, groups, rows):
     q_ref = refs[0]
     piece_refs = refs[1 : 1 + pieces]
     outs = refs[1 + pieces : 1 + pieces + groups]
-    sum_ref, lse_ref, kv_ref, sems = refs[1 + pieces + groups :]
+    sum_ref, lse_ref, kv_ref, sems, score_ref, top_ref, total_ref, acc_ref = refs[
+        1 + pieces + groups :
+    ]
     size, wide = q_ref.shape[1:]
     slot = size // groups
     count = 2 * pieces
@@ -139,41 +157,65 @@
         copy.wait()
     for j in range(2):
         block = meta[count + j]
-        turned = head_rows(jnp.transpose(q_ref[j].astype(F32)) * scale, 0, heads)
-
-        def visit(place, carry, diagonal):
-            keys = kv_ref[place, :, :wide]
-            values = jnp.transpose(kv_ref[place, :, 2 * width - wide :].astype(F32)).astype(BF16)
-            later = []
+        for tile in range(size // rows):
+            spot = pl.ds(tile * rows, rows)
+            query = jnp.concatenate(head_cols(q_ref[j, spot].astype(F32) * scale, 0, heads), axis=0)
+
+            def score(n):
+                return contract_cols(query, kv_ref[meta[n], :, :wide])
+
+            def scores(ns):
+                found = [score(n) for n in ns]
+                top = top_ref[...]
+                for n, value in zip(ns, found, strict=True):
+                    score_ref[n] = value
+                    top = jnp.maximum(top, lanes(jnp.maximum, value))
+                top_ref[...] = top
+
+            def weights(ns):
+                total = total_ref[...]
+                acc = acc_ref[...]
+                top = widen(top_ref[...], size)
+                for n in ns:
+                    weight = jnp.exp(score_ref[n] - top)
+                    total += lanes(jnp.add, weight)
+                    acc += mm(weight.astype(BF16), kv_ref[meta[n], :, 2 * width - wide :])
+                total_ref[...] = total
+                acc_ref[...] = acc
+
+            seen = causal_mask(heads, size, meta[count + 2])
+            if rows < size:
+                seen = jnp.concatenate(
+                    [seen[h * size + tile * rows :][:rows] for h in range(heads)], axis=0
+                )
+            own = jnp.where(seen, score(block), MASKED)
+            score_ref[block] = own
+            top_ref[...] = lanes(jnp.maximum, own)
+            in_pairs(0, block, scores)
+            top_ref[...] = jnp.broadcast_to(
+                jnp.max(top_ref[...], axis=1, keepdims=True), top_ref.shape
+            )
+            total_ref[...] = jnp.zeros_like(total_ref)
+            acc_ref[...] = jnp.zeros_like(acc_ref)
+            in_pairs(0, block + 1, weights)
+            total = jnp.sum(total_ref[...], axis=1, keepdims=True)
+            lse = jnp.broadcast_to(top_ref[:, :1] + jnp.log(total), top_ref.shape)
+            result = acc_ref[...] / total
+            mine = lax.broadcasted_iota(jnp.int32, (rows, wide), 1) - (wide - width)
+            whole = sum(
+                jnp.where(
+                    (mine >= h * HEAD_DIM) & (mine < (h + 1) * HEAD_DIM),
+                    result[h * rows : (h + 1) * rows],
+                    0.0,
+                )
+                for h in range(heads)
+            )
+            sum_ref[j, spot] = whole
+            whole = whole[:, wide - width :].astype(BF16)
             for h in range(heads):
-                score = mm(keys, turned[h])
-                if diagonal:
-                    score = jnp.where(causal_mask(size, meta[count + 2]), score, MASKED)
-                top = jnp.max(score, axis=0, keepdims=True)
-                if not diagonal:
-                    top = jnp.maximum(top, carry[2 * h])
-                weight = jnp.exp(score - top)
-                total = jnp.sum(weight, axis=0, keepdims=True)
-                at = wide - width + h * HEAD_DIM
-                gain = mm(values[at : at + HEAD_DIM], weight.astype(BF16))
-                spot = slice(h * HEAD_DIM, (h + 1) * HEAD_DIM)
-                if not diagonal:
-                    fade = jnp.exp(carry[2 * h] - top)
-                    total = total + carry[2 * h + 1] * fade
-                    gain = gain + sum_ref[j, spot] * fade
-                sum_ref[j, spot] = gain
-                later += [top, total]
-            return tuple(later)
-
-        carry = visit(j, None, True)
-        carry = lax.fori_loop(0, block, lambda n, c: visit(meta[n], c, False), carry)
-        for h in range(heads):
-            spot = slice(h * HEAD_DIM, (h + 1) * HEAD_DIM)
-            sum_ref[j, spot] = sum_ref[j, spot] / carry[2 * h + 1]
-            lse_ref[j, h : h + 1] = carry[2 * h] + jnp.log(carry[2 * h + 1])
-        result = jnp.transpose(sum_ref[j]).astype(BF16)
-        for r in range(groups):
-            outs[r][j] = result[r * slot : (r + 1) * slot]
+                lse_ref[j, pl.ds(h * size + tile * rows, rows)] = lse[h * rows : (h + 1) * rows]
+            for i in range(rows // slot):
+                outs[tile * rows // slot + i][j] = whole[i * slot : (i + 1) * slot]
 
 
 def attend_back_kernel(meta, *refs, heads, pieces, groups):
@@ -195,56 +237,112 @@
     for j in range(2):
         block = meta[count + j]
         query = q_ref[j].astype(F32) * scale
-        plain = head_cols(query, 0, heads)
-        turned = head_rows(jnp.transpose(query), 0, heads)
+        query_turned = jnp.transpose(query).astype(BF16)
+        queries = jnp.concatenate(head_cols(query, 0, heads), axis=0)
         grad = jnp.concatenate([grad_refs[r][j] for r in range(groups)], axis=0)
         grad_turned = jnp.transpose(grad.astype(F32))
-        dots = [
-            jnp.sum(
-                grad_turned[h * HEAD_DIM : (h + 1) * HEAD_DIM]
-                * sum_ref[j, h * HEAD_DIM : (h + 1) * HEAD_DIM],
-                axis=0,
-                keepdims=True,
+        if pad:
+            grad_turned = jnp.concatenate([jnp.zeros((pad, size), F32), grad_turned], axis=0)
+        grad = jnp.transpose(grad_turned)
+        grad_turned = grad_turned.astype(BF16)
+        cols = head_cols(grad, pad, heads)
+        grads = jnp.concatenate(cols, axis=0)
+        dots = jnp.concatenate(
+            [jnp.sum(col.astype(F32) * sum_ref[j], axis=1, keepdims=True) for col in cols], axis=0
+        )
+        dots = jnp.broadcast_to(dots, (heads * size, 128))
+        dq_acc[...] = jnp.zeros_like(dq_acc)
+
+        def visit(ns, diagonal=False):
+            dq = dq_acc[...]
+            for n in ns:
+                place = meta[n]
+                keys = kv_ref[place, :, :wide]
+                values = kv_ref[place, :, 2 * width - wide :]
+                score = contract_cols(queries, keys)
+                if diagonal:
+                    score = jnp.where(causal_mask(heads, size, meta[count + 2]), score, MASKED)
+                prob = jnp.exp(score - widen(lse_ref[j], size))
+                prob_grad = contract_cols(grads, values)
+                score_grad = (prob * (prob_grad - widen(dots, size))).astype(BF16)
+                prob = prob.astype(BF16)
+                dq += mm(score_grad, keys)
+                for h in range(heads):
+                    mine = slice(h * size, (h + 1) * size)
+                    at = h * HEAD_DIM
+                    acc_ref[place, at : at + HEAD_DIM] += mm(
+                        query_turned[at : at + HEAD_DIM], score_grad[mine]
+                    )
+                    acc_ref[place, width + at : width + at + HEAD_DIM] += mm(
+                        grad_turned[pad + at : pad + at + HEAD_DIM], prob[mine]
+                    )
+            dq_acc[...] = dq
+
+        visit((block,), True)
+        in_pairs(0, block, visit)
+        mine = lax.broadcasted_iota(jnp.int32, (size, wide), 1)
+        whole = sum(
+            jnp.where(
+                (mine >= h * HEAD_DIM) & (mine < (h + 1) * HEAD_DIM),
+                dq_acc[h * size : (h + 1) * size],
+                0.0,
             )
             for h in range(heads)
-        ]
-        if pad:
-            grad_turned = jnp.concatenate([jnp.zeros((pad, size), F32), grad_turned], axis=0)
-        grads = head_cols(jnp.transpose(grad_turned), pad, heads)
-        grads_turned = head_rows(grad_turned, pad, heads)
-        dq_acc[...] = jnp.zeros_like(dq_acc)
-
-        def visit(place, diagonal):
-            keys = kv_ref[place, :, :wide]
-            values = kv_ref[place, :, 2 * width - wide :]
-            keys_turned = jnp.transpose(keys.astype(F32)).astype(BF16)
-            key_grad = jnp.zeros((size, wide), F32)
-            value_grad = jnp.zeros((size, wide), F32)
-            for h in range(heads):
-                score = mm(keys, turned[h])
-                if diagonal:
-                    score = jnp.where(causal_mask(size, meta[count + 2]), score, MASKED)
-                prob = jnp.exp(score - lse_ref[j, h : h + 1])
-                prob_grad = mm(values, grads_turned[h])
-                score_grad = (prob * (prob_grad - dots[h])).astype(BF16)
-                value_grad += mm(prob.astype(BF16), grads[h])
-                key_grad += mm(score_grad, plain[h])
-                spot = slice(h * HEAD_DIM, (h + 1) * HEAD_DIM)
-                dq_acc[spot] += mm(keys_turned[spot], score_grad)
-            acc_ref[place, :, :wide] += key_grad
-            acc_ref[place, :, 2 * width - wide :] += value_grad
-
-        visit(j, True)
-
-        def step(n, carry):
-            visit(meta[n], False)
-            return carry
-
-        lax.fori_loop(0, block, step, 0)
-        dq_ref[j] = jnp.transpose(dq_acc[...] * scale).astype(BF16)
-    for i in range(pieces):
-        to_ref = keep_ref if i < pieces // 2 else send_ref
-        to_ref[i % (pieces // 2)] = acc_ref[2 * i : 2 * i + 2].astype(BF16)
+        )
+        dq_ref[j] = (whole[:, :width] * scale).astype(BF16)
+    for i in range(count):
+        to_ref = keep_ref if i < pieces else send_ref
+        to_ref[i % pieces // 2, i % 2] = jnp.transpose(acc_ref[i]).astype(BF16)
+
+
+def forward_call(meta, query, keyvals, heads, groups):
+    size, wide = query.shape[1:]
+    part = heads * HEAD_DIM
+    pieces = len(keyvals)
+    rows = size
+    while heads * rows * size * 2 * pieces > 1 << 22 and rows > size // groups:
+        rows //= 2
+    return in_vmem(
+        functools.partial(attend_kernel, heads=heads, pieces=pieces, groups=groups, rows=rows),
+        meta,
+        [query] + keyvals,
+        [jax.ShapeDtypeStruct((2, size // groups, part), BF16)] * groups
+        + [
+            jax.ShapeDtypeStruct((2, size, wide), F32),
+            jax.ShapeDtypeStruct((2, heads * size, 128), F32),
+        ],
+        [
+            pltpu.VMEM((2 * pieces, size, 2 * part), BF16),
+            pltpu.SemaphoreType.DMA((pieces,)),
+            pltpu.VMEM((2 * pieces, heads * rows, size), F32),
+            pltpu.VMEM((heads * rows, 128), F32),
+            pltpu.VMEM((heads * rows, 128), F32),
+            pltpu.VMEM((heads * rows, wide), F32),
+        ],
+        16 * pieces * size * size * wide * heads,
+        range(1, 1 + pieces),
+    )
+
+
+def backward_call(meta, query, keyvals, grads, sums, lse, heads, groups):
+    size, wide = query.shape[1:]
+    part = heads * HEAD_DIM
+    pieces = len(keyvals)
+    half = jax.ShapeDtypeStruct((pieces // 2, 2, size, 2 * part), BF16)
+    return in_vmem(
+        functools.partial(attend_back_kernel, heads=heads, pieces=pieces, groups=groups),
+        meta,
+        [query] + keyvals + grads + [sums, lse],
+        [jax.ShapeDtypeStruct((2, size, part), BF16), half, half],
+        [
+            pltpu.VMEM((2 * pieces, size, 2 * part), BF16),
+            pltpu.SemaphoreType.DMA((pieces,)),
+            pltpu.VMEM((2 * pieces, 2 * part, size), F32),
+            pltpu.VMEM((heads * size, wide), F32),
+        ],
+        24 * pieces * size * size * wide * heads,
+        range(1, 1 + pieces),
+    )
 
 
 def project_kernel(meta, *refs, groups, fetch):
@@ -322,8 +420,9 @@
     attended = refs[at : at + groups] if with_out else ()
     branches = refs[at + groups] if with_out else None
     at += (groups + 1) * with_out
-    outs = refs[at : at + groups]
-    keep_ref, send_ref, grad_ref, term_ref, out_term_ref, vec_ref = refs[at + groups :]
+    half = groups // 2
+    outs = refs[at : at + half]
+    far_ref, keep_ref, send_ref, grad_ref, term_ref, out_term_ref, vec_ref = refs[at + half :]
     here, member = meta[0], meta[1]
     fetch = keep_ref.shape[0]
     across = keep_ref.shape[3]
@@ -341,7 +440,11 @@
         gain_total += jnp.sum(normed_grad * unit_ref[j], axis=0, keepdims=True)
         shift_total += jnp.sum(normed_grad, axis=0, keepdims=True)
         for z in range(groups):
-            outs[z][j] = normed_grad[z * slot : (z + 1) * slot].astype(BF16)
+            piece = normed_grad[z * slot : (z + 1) * slot].astype(BF16)
+            if z < half:
+                outs[z][j] = piece
+            else:
+                far_ref[z - half, j] = piece
     term_ref[...] = contract_rows(
         normed_ref[...].reshape(2 * size, width), grad_ref[...].reshape(2 * size, across)
     )
@@ -382,30 +485,46 @@
                 to_ref[r, groups] = jnp.concatenate([rows[:, :across], rest], axis=0).astype(BF16)
 
 
-def home_kernel(meta, *refs, groups, cut, fetch, part, width, with_out):
+def rows_kernel(meta, *refs, groups, cut, part, width, with_out):
+    pieces = refs[:groups]
+    block_ref, small_ref, turned = refs[-3:]
+    member = meta[1]
+    across = 3 * part
+    total = jnp.zeros(small_ref.shape, F32)
+    for z in range(groups):
+        value = pieces[z][...].astype(F32)
+        total += value[cut:]
+        turned[member ^ z] = value[:cut]
+    small_ref[...] = total
+    held = [turned[z] for z in range(groups)]
+    for k, home in enumerate((width, 2 * width, 0)):
+        whole = jnp.concatenate([h[:, k * part : (k + 1) * part] for h in held], axis=1)
+        block_ref[:, home : home + width] = whole[:, :width].astype(BF16)
+    if with_out:
+        block = refs[groups][...].astype(F32)
+        rest = jnp.concatenate(
+            [
+                block[cut : cut + 8, i * (width - across) : (i + 1) * (width - across)]
+                for i in range(cut // 8)
+            ],
+            axis=0,
+        )
+        block = jnp.concatenate([block[:cut], rest], axis=1)
+        block_ref[:, 3 * width :] = block.astype(BF16)
+
+
+def home_kernel(meta, *refs, cut, fetch, with_out):
     pieces = refs[: 2 * fetch]
-    out_ref, out_out_ref = refs[2 * fetch :]
-    here, member = meta[0], meta[1]
-    across = 3 * part
+    outs = refs[2 * fetch :]
+    here = meta[0]
     for i, piece in enumerate(pieces):
         r = 2 * (i % fetch) + i // fetch
         start = pl.multiple_of(((here ^ r) & (2 * fetch - 1)) * cut, 8)
-        held = [piece[z ^ member].astype(F32) for z in range(groups)]
-        for k, home in enumerate((width, 2 * width, 0)):
-            whole = jnp.concatenate([h[:cut, k * part : (k + 1) * part] for h in held], axis=1)
-            out_ref[pl.ds(start, cut), home : home + width] = whole[:, :width]
-        if with_out:
-            block = piece[groups].astype(F32)
-            rest = jnp.concatenate(
-                [
-                    block[cut : cut + 8, i * (width - across) : (i + 1) * (width - across)]
-                    for i in range(cut // 8)
-                ],
-                axis=0,
-            )
-            out_out_ref[pl.ds(start, cut)] = jnp.concatenate([block[:cut], rest], axis=1)
-        elif i == 0:
-            out_out_ref[...] = jnp.zeros_like(out_out_ref)
+        block = piece[...].astype(F32)
+        at = 0
+        for out in outs:
+            out[pl.ds(start, cut)] = block[:, at : at + out.shape[1]]
+            at += out.shape[1]
 
 
 def tokens_kernel(meta, grad_ref, x_ref, gain_ref, resid_grad_ref, out_ref):
@@ -570,29 +689,13 @@
             lax.dynamic_slice_in_dim(down_weight, here * hidden_cut, hidden_cut, 0),
         ]
     )
-    ffn_parts = lax.all_gather(after(ffn_cut, grads_all), "fsdp", axis=0, tiled=True)
+    ffn_parts = lax.all_gather(after(ffn_cut, *group_tokens), "fsdp", axis=0, tiled=True)
     ffn_parts = ffn_parts.reshape(groups, 2, hidden_cut, width)
     up_part = ffn_parts[:, 0].reshape(groups * hidden_cut, width)
     down_part = ffn_parts[:, 1].reshape(groups * hidden_cut, width)
 
-    attend_flops = 40 * blocks * block_len * block_len * wide * heads
     pair = jax.ShapeDtypeStruct((2, slot, part), BF16)
-    results = in_vmem(
-        functools.partial(attend_kernel, heads=heads, pieces=n_ctx, groups=groups),
-        meta,
-        [query] + keyvals,
-        [pair] * groups
-        + [
-            jax.ShapeDtypeStruct((2, part, block_len), F32),
-            jax.ShapeDtypeStruct((2, heads, block_len), F32),
-        ],
-        [
-            pltpu.VMEM((blocks, block_len, 2 * part), BF16),
-            pltpu.SemaphoreType.DMA((n_ctx,)),
-        ],
-        attend_flops,
-        range(1, 1 + n_ctx),
-    )
+    results = forward_call(meta, query, keyvals, heads, groups)
     own_attended = results[:groups]
     sums, lse = results[groups:]
     attended = z_exchange(results[:groups])
@@ -607,7 +710,9 @@
         ],
     )
 
-    second_all = jnp.concatenate(ctx_spread(second16))
+    second_held = chip_spread(second16, chips)
+    up_part, down_part, *second_held = lax.optimization_barrier((up_part, down_part, *second_held))
+    second_all = jnp.concatenate(second_held + [swap(s, "ctx", 1) for s in second_held])
     pre = contract_cols(second_all, up_part) + up_bias_part.astype(F32)
     act, gate_pull = jax.vjp(functools.partial(jax.nn.gelu, approximate=True), pre)
     act16 = act.astype(BF16)
@@ -651,22 +756,11 @@
         branches = jnp.concatenate([branches, swap(branches, "fsdp", mask)])
         mask *= 2
 
-    half = jax.ShapeDtypeStruct((chips, 2, block_len, 2 * part), BF16)
-    query_grad, keyval_keep, keyval_send = in_vmem(
-        functools.partial(attend_back_kernel, heads=heads, pieces=n_ctx, groups=groups),
-        meta,
-        [query] + keyvals + attend_grads + [sums, lse],
-        [jax.ShapeDtypeStruct((2, block_len, part), BF16), half, half],
-        [
-            pltpu.VMEM((blocks, block_len, 2 * part), BF16),
-            pltpu.SemaphoreType.DMA((n_ctx,)),
-            pltpu.VMEM((blocks, block_len, 2 * part), F32),
-            pltpu.VMEM((part, block_len), F32),
-        ],
-        attend_flops,
-        range(1, 1 + n_ctx),
-    )
-    keyval_sums = ctx_collect(keyval_keep, after(keyval_send, branches, feed))
+    query_grad, keyval_keep, keyval_send = backward_call(
+        meta, query, keyvals, attend_grads, sums, lse, heads, groups
+    )
+    keyval_sums = ctx_collect(keyval_keep, after(keyval_send, branches))
+    feed, *keyval_sums = lax.optimization_barrier((feed, *keyval_sums))
 
     ffn_terms = after(ffn_terms, branches, query_grad)
     ffn_term = lax.psum_scatter(ffn_terms, "fsdp", scatter_dimension=0, tiled=True)
@@ -685,7 +779,8 @@
         keyval_sums
         + [query_grad, normed16, unit_one, proj_in, totals, up_bias_terms]
         + (list(own_attended) + [branches] if with_out else []),
-        [jax.ShapeDtypeStruct((2, slot, width), BF16)] * groups + [half, half],
+        [jax.ShapeDtypeStruct((2, slot, width), BF16)] * (groups // 2)
+        + [jax.ShapeDtypeStruct((groups // 2, 2, slot, width), BF16), half, half],
         [
             pltpu.VMEM((2, block_len, 3 * part), BF16),
             pltpu.VMEM((width, 3 * part), F32),
@@ -693,17 +788,17 @@
             pltpu.VMEM((groups, 8, 3 * part), F32),
         ],
     )
-    in_keep, in_send = results[groups:]
-    ffn_grads = lax.all_gather(after(ffn_term, in_keep), "ctx", axis=0, tiled=True)
+    *normed_pieces, normed_far, in_keep, in_send = results
     in_sums = ctx_collect(in_keep, in_send)
-    normed_pieces = list(results[:groups])
+    ffn_grads = lax.all_gather(after(ffn_term, in_sums[0]), "ctx", axis=0, tiled=True)
     mask = groups // 2
-    while mask:
+    came = swap(normed_far, "fsdp", mask)
+    came, *in_sums = lax.optimization_barrier((came, *in_sums))
+    normed_pieces = [add16(piece, came[i]) for i, piece in enumerate(normed_pieces)]
+    while mask > 1:
+        mask //= 2
         came = swap(jnp.stack(normed_pieces[mask:]), "fsdp", mask)
-        if mask == groups // 2:
-            came, *in_sums = lax.optimization_barrier((came, *in_sums))
         normed_pieces = [add16(piece, came[i]) for i, piece in enumerate(normed_pieces[:mask])]
-        mask //= 2
     normed_grad = normed_pieces[0]
     in_term = sum(piece.astype(F32) for piece in in_sums).astype(BF16)
     mask = 2 * fold
@@ -711,10 +806,20 @@
         in_term = add16(in_term, swap(in_term, "ctx", mask))
         mask *= 2
     handed = z_exchange([in_term[r] for r in range(groups)])
-    small = sum(piece[cut:].astype(F32) for piece in handed)
-    in_term = jnp.stack(handed + [in_term[groups]] if with_out else handed)
-    in_held = chip_spread(in_term, fold)
-    in_held = in_held + [swap(piece, "ctx", 1) for piece in in_held]
+    across = (3 + with_out) * width
+    in_block, small = in_vmem(
+        functools.partial(
+            rows_kernel, groups=groups, cut=cut, part=part, width=width, with_out=with_out
+        ),
+        index,
+        handed + ([in_term[groups]] if with_out else []),
+        [
+            jax.ShapeDtypeStruct((cut, across), BF16),
+            jax.ShapeDtypeStruct((8, 3 * part), F32),
+        ],
+        [pltpu.VMEM((groups, cut, 3 * part), F32)],
+    )
+    in_held = chip_spread(in_block, fold)
     tokens_grad = in_vmem(
         tokens_kernel,
         index,
@@ -726,26 +831,19 @@
     ffn_grads = ffn_grads.reshape(n_ctx, 2, hidden_cut, width).astype(F32)
     up_grad = ffn_grads[:, 0].reshape(hidden, width)
     down_grad = ffn_grads[:, 1].reshape(hidden, width)
-    up_grad, down_grad, tokens_grad, *in_held = lax.optimization_barrier(
-        (up_grad, down_grad, tokens_grad, *in_held)
-    )
-    mixer_in_grad, mixer_out_grad = in_vmem(
-        functools.partial(
-            home_kernel,
-            groups=groups,
-            cut=cut,
-            fetch=fold,
-            part=part,
-            width=width,
-            with_out=with_out,
-        ),
+    up_grad, down_grad, *in_held = lax.optimization_barrier((up_grad, down_grad, *in_held))
+    in_held = in_held + [swap(piece, "ctx", 1) for piece in in_held]
+    tokens_grad, *in_held = lax.optimization_barrier((tokens_grad, *in_held))
+    homes = in_vmem(
+        functools.partial(home_kernel, cut=cut, fetch=fold, with_out=with_out),
         index,
         in_held,
         [
-            jax.ShapeDtypeStruct((share, 3 * width), F32),
-            jax.ShapeDtypeStruct((share, width), F32),
+            jax.ShapeDtypeStruct((share, wide_out), F32)
+            for wide_out in ((3 * width, width) if with_out else (3 * width,))
         ],
     )
+    mixer_in_grad, mixer_out_grad = homes[0], homes[-1]
 
     if not with_out:
         whole = jnp.stack(attended).reshape(groups, local_rows, part)

time: 295 us -> 281 us (0.953)
  Pallas kernels: 73.8 us -> 64.2 us
  waiting for transfers between devices: 98.8 us -> 90.8 us
    pallas_call x8 -> x9, Pallas kernels: 67 us -> 57.4 us  [in_vmem(): pl.pallas_call(kernel, grid_spec=pltpu.PrefetchScalarGridSpec(num_scalar_...]
    ppermute x55, waiting for transfers between devices: 93.9 us -> 87.5 us  [swap(): lax.ppermute(x, axis, [(i, i ^ mask) for i in range(lax.axis_size(axis))])]
    reduce_scatter x1, waiting for transfers between devices: 4.06 us -> 0.02 us  [per_device(): feed = lax.psum_scatter(feed, 'ctx', scatter_dimension=0, tiled=True)]
    unnamed x128 -> x129, local copies, waits for them, and re-layouts: 5.92 us -> 5.98 us
  transfers between devices with their start and end apart: 61 -> 61, of which waited for: 26 -> 32; matrix products, arithmetic and copies ran while one was open for 11% -> 13% of each run, Pallas kernels for 22% -> 22%
where the time goes in v2:
time: 281 us; the launch traced here: 280 us
  waiting for transfers between devices  90.8 us (32%)
  Pallas kernels  64.2 us (23%)
  starting transfers between devices  63.2 us (22%)
  local copies, waits for them, and re-layouts  24.7 us (9%)
  between operations  15 us (5%)
  other arithmetic  13.9 us (5%)
  matrix products  7.93 us (3%)
    ppermute x55, waiting for transfers between devices, swap(): lax.ppermute(x, axis, [(i, i ^ mask) for i in range(lax.axis_size(axis))])  87.5 us
    ppermute x55, starting transfers between devices, swap(): lax.ppermute(x, axis, [(i, i ^ mask) for i in range(lax.axis_size(axis))])  63 us
    pallas_call x9, Pallas kernels, in_vmem(): pl.pallas_call(kernel, grid_spec=pltpu.PrefetchScalarGridSpec(num_scalar_...  57.4 us
    pallas_call x2, Pallas kernels, shuffle(): pl.pallas_call(shuffle_kernel, grid_spec=pltpu.PrefetchScalarGridSpec(num...  6.76 us
    unnamed x129, local copies, waits for them, and re-layouts  5.98 us
    convert_element_type x4, other arithmetic, add16(): return (left.astype(F32) + right.astype(F32)).astype(BF16)  5.69 us
  transfers between devices with their start and end apart: 61, of which 32 were waited for; matrix products, arithmetic and copies ran while one was open for 13% of the time, Pallas kernels for 22%

profile of v2, /device:TPU:0, one launch (start us, length us, event | category | flops | bytes accessed | tf_op | source)
XLA Modules:
  0.0 279.7 jit_solution(13769035716030084011)
XLA Ops:
  9.9 3.1 %collective-permute-start = (bf16[64,576]{1,0:T(8,128)(2,1)S(1)}, bf16[64,576]{1,0:T(8,128)(2,1)S(1)}, u32[]{:S(2)}, u32[]{:S(2)}) collective-permute-start(bf16[64,576]{1,0:T(8,128)(2,1)S(1)} %get-tuple-element.226), channel_id=1, source_target_pairs={{0,1},{1,0},{2,3},{3,2},{4,5},{5,4},{6,7},{7,6},{8,9},{9,8},{10,11... | collective-permute-start | bytes 221192 | tf_op jit(solution)/shard_map/ppermute | solution.py:21
  13.0 2.6 collective-permute-start.1
  15.6 6.6 %collective-permute-done.1 = bf16[64,576]{1,0:T(8,128)(2,1)S(1)} collective-permute-done((bf16[64,576]{1,0:T(8,128)(2,1)S(1)}, bf16[64,576]{1,0:T(8,128)(2,1)S(1)}, u32[]{:S(2)}, u32[]{:S(2)}) %collective-permute-start.1) | collective-permute-done | bytes 73760 | tf_op jit(solution)/shard_map/ppermute | solution.py:21
  22.3 2.5 collective-permute-start.5
  27.0 2.4 collective-permute-start.8
  29.9 2.0 collective-permute-done.5.refs_3_
  31.9 1.5 collective-permute-start.6
  34.2 7.3 %collective-permute-done.4.refs_2_ = bf16[2,64,768]{2,1,0:T(8,128)(2,1)S(1)} collective-permute-done((bf16[2,64,768]{2,1,0:T(8,128)(2,1)S(1)}, bf16[2,64,768]{2,1,0:T(8,128)(2,1)S(1)}, u32[]{:S(2)}, u32[]{:S(2)}) %collective-permute-start.4) | collective-permute-done | bytes 196640 | tf_op jit(solution)/shard_map/ppermute | solution.py:21
  45.6 5.0 %shard_map.237 = (bf16[2,256,384]{2,1,0:T(8,128)(2,1)}, bf16[2,256,256]{2,1,0:T(8,128)(2,1)}, bf16[2,256,768]{2,1,0:T(8,128)(2,1)}, f32[2,256,768]{2,1,0:T(8,128)}, bf16[768,576]{1,0:T(8,128)(2,1)}) custom-call(s32[3]{0:T(128)} %pad_add_fusion.meta, bf16[2,64,768]{2,1,0:T(8,128)(2,1)} %bitcast.132, bf16[2,64,768]{2,1,0:T(8,128)(2,1)} %copy-done.24, ...), custom_call_target="tpu_custom_call" | custom-call | bytes 1048576 | tf_op jit(solution)/shard_map/pallas_call | solution.py:540
  50.5 1.9 collective-permute-start.11
  55.2 3.4 %shard_map.238 = bf16[8,128,768]{2,1,0:T(8,128)(2,1)} custom-call(s32[8]{0:T(128)} %add_xor_fusion.table, bf16[8,128,768]{2,1,0:T(8,128)(2,1)} %bitcast.138), custom_call_target="tpu_custom_call" | custom-call | tf_op jit(solution)/shard_map/pallas_call | solution.py:70
  58.6 5.1 %collective-permute-done.11.refs_4_ = bf16[2,256,384]{2,1,0:T(8,128)(2,1)S(1)} collective-permute-done((bf16[2,256,384]{2,1,0:T(8,128)(2,1)}, bf16[2,256,384]{2,1,0:T(8,128)(2,1)S(1)}, u32[]{:S(2)}, u32[]{:S(2)}) %collective-permute-start.11) | collective-permute-done | bytes 393248 | tf_op jit(solution)/shard_map/ppermute | solution.py:21
  63.8 6.8 %collective-permute-done.10.refs_3_ = bf16[2,256,384]{2,1,0:T(8,128)(2,1)S(1)} collective-permute-done((bf16[2,256,384]{2,1,0:T(8,128)(2,1)}, bf16[2,256,384]{2,1,0:T(8,128)(2,1)S(1)}, u32[]{:S(2)}, u32[]{:S(2)}) %collective-permute-start.10) | collective-permute-done | bytes 393248 | tf_op jit(solution)/shard_map/ppermute | solution.py:21
  74.8 13.0 %shard_map.239 = (bf16[2,64,192]{2,1,0:T(8,128)(2,1)}, bf16[2,64,192]{2,1,0:T(8,128)(2,1)}, bf16[2,64,192]{2,1,0:T(8,128)(2,1)}, bf16[2,64,192]{2,1,0:T(8,128)(2...) custom-call(s32[19]{0:T(128)} %pad_add_fusion.1.meta, bf16[2,256,256]{2,1,0:T(8,128)(2,1)} %get-tuple-element.114.refs_0_, ...), custom_call_target="tpu_custom_call" | custom-call | flops 6442450944 | bytes 1048576 | tf_op jit(solution)/shard_map/pallas_call | solution.py:540
  87.8 3.3 %collective-permute-start.16 = (bf16[2,64,192]{2,1,0:T(8,128)(2,1)}, bf16[2,64,192]{2,1,0:T(8,128)(2,1)S(1)}, u32[]{:S(2)}, u32[]{:S(2)}) collective-permute-start(bf16[2,64,192]{2,1,0:T(8,128)(2,1)} %get-tuple-element.121.refs_11_), channel_id=1, source_target_pairs={{0,1},{1,0},{2,3},{3,2},{4,5},{5,4},{6,7},{7,6},{8,9},{9,8},{10,11... | collective-permute-start | bytes 147464 | tf_op jit(solution)/shard_map/ppermute | solution.py:21
  91.1 2.4 collective-permute-start.18
  94.4 2.3 slice.255.refs_5_.refs_6_
  98.2 5.9 %collective-permute-done.17.refs_2_ = bf16[2,64,192]{2,1,0:T(8,128)(2,1)S(1)} collective-permute-done((bf16[2,64,192]{2,1,0:T(8,128)(2,1)}, bf16[2,64,192]{2,1,0:T(8,128)(2,1)S(1)}, u32[]{:S(2)}, u32[]{:S(2)}) %collective-permute-start.17) | collective-permute-done | bytes 49184 | tf_op jit(solution)/shard_map/ppermute | solution.py:21
  104.8 3.3 %shard_map.240 = (f32[128,768]{1,0:T(8,128)}, bf16[128,768]{1,0:T(8,128)(2,1)}) custom-call(s32[3]{0:T(128)} %pad_add_fusion.meta, bf16[2,64,192]{2,1,0:T(8,128)(2,1)} %get-tuple-element.124.refs_0_.refs_10_, bf16[2,64,192]{2,1,0:T(8,128)(2,1)} %copy-done.33, bf16[2,64,192]{2,1,0:T(8,128)(2,1)} %copy-done.34, bf16[2,64,192]{2,1,0:T(8,128)(2,1)} %copy-done.35, ...), custom_call_target="tpu_custom_call" | custom-call | bytes 1048576 | tf_op jit(solution)/shard_map/pallas_call | solution.py:540
  109.4 1.6 collective-permute-start.20
  111.6 2.5 all-gather.9.cloned.1.call-done
  121.6 1.8 convert_reduce_fusion
  125.3 2.3 convolution_convert_fusion.1
  129.5 1.7 collective-permute-start.29
  133.9 3.3 %shard_map.241 = bf16[8,128,768]{2,1,0:T(8,128)(2,1)} custom-call(s32[8]{0:T(128)} %fusion.47.table, bf16[8,128,768]{2,1,0:T(8,128)(2,1)} %bitcast.141), custom_call_target="tpu_custom_call" | custom-call | tf_op jit(solution)/shard_map/pallas_call | solution.py:70
  138.3 3.4 %collective-permute-done.28.refs_2_ = bf16[128,768]{1,0:T(8,128)(2,1)S(1)} collective-permute-done((bf16[128,768]{1,0:T(8,128)(2,1)S(1)}, bf16[128,768]{1,0:T(8,128)(2,1)S(1)}, u32[]{:S(2)}, u32[]{:S(2)}) %collective-permute-start.28) | collective-permute-done | bytes 196640 | tf_op jit(solution)/shard_map/ppermute | solution.py:21
  142.4 4.1 %shard_map.242 = (bf16[2,64,192]{2,1,0:T(8,128)(2,1)}, bf16[2,64,192]{2,1,0:T(8,128)(2,1)}, bf16[2,64,192]{2,1,0:T(8,128)(2,1)}, bf16[2,64,192]{2,1,0:T(8,128)(2...) custom-call(s32[3]{0:T(128)} %pad_add_fusion.meta, ...), custom_call_target="tpu_custom_call" | custom-call | bytes 1048576 | tf_op jit(solution)/shard_map/pallas_call | solution.py:540
  146.6 6.4 %collective-permute-start.30 = (bf16[1,128,768]{2,1,0:T(8,128)(2,1)}, bf16[1,128,768]{2,1,0:T(8,128)(2,1)S(1)}, u32[]{:S(2)}, u32[]{:S(2)}) collective-permute-start(bf16[1,128,768]{2,1,0:T(8,128)(2,1)} %bitcast.156), channel_id=1, source_target_pairs={{0,1},{1,0},{2,3},{3,2},{4,5},{5,4},{6,7},{7,6},{8,9},{9,8},{10,11... | collective-permute-start | bytes 589832 | tf_op jit(solution)/shard_map/ppermute | solution.py:21
  153.4 3.9 %collective-permute-start.33 = (bf16[2,64,192]{2,1,0:T(8,128)(2,1)}, bf16[2,64,192]{2,1,0:T(8,128)(2,1)S(1)}, u32[]{:S(2)}, u32[]{:S(2)}) collective-permute-start(bf16[2,64,192]{2,1,0:T(8,128)(2,1)} %get-tuple-element.149), channel_id=1, source_target_pairs={{0,3},{1,2},{2,1},{3,0},{4,7},{5,6},{6,5},{7,4},{8,11},{9,10},{10,... | collective-permute-start | bytes 147464 | tf_op jit(solution)/shard_map/ppermute | solution.py:21
  157.4 3.5 %collective-permute-done.30 = bf16[1,128,768]{2,1,0:T(8,128)(2,1)S(1)} collective-permute-done((bf16[1,128,768]{2,1,0:T(8,128)(2,1)}, bf16[1,128,768]{2,1,0:T(8,128)(2,1)S(1)}, u32[]{:S(2)}, u32[]{:S(2)}) %collective-permute-start.30) | collective-permute-done | bytes 196640 | tf_op jit(solution)/shard_map/ppermute | solution.py:21
  162.5 2.0 collective-permute-start.34
  164.5 16.5 %shard_map.243 = (bf16[2,256,192]{2,1,0:T(8,128)(2,1)}, bf16[4,2,256,384]{3,2,1,0:T(8,128)(2,1)}, bf16[4,2,256,384]{3,2,1,0:T(8,128)(2,1)}) custom-call(s32[19]{0:T(128)} %pad_add_fusion.1.meta, bf16[2,256,256]{2,1,0:T(8,128)(2,1)} %get-tuple-element.114.refs_0_, bf16[2,256,384]{2,1,0:T(8,128)(2,1)} %get-tuple-element.116.refs_1_, ...), custom_call_target="tpu_custom_call" | custom-call | flops 9663676416 | bytes 1048576 | tf_op jit(solution)/shard_map/pallas_call | solution.py:540
  181.9 3.7 %collective-permute-done.35 = bf16[4,2,256,384]{3,2,1,0:T(8,128)(2,1)} collective-permute-done((bf16[4,2,256,384]{3,2,1,0:T(8,128)(2,1)}, bf16[4,2,256,384]{3,2,1,0:T(8,128)(2,1)}, u32[]{:S(2)}, u32[]{:S(2)}) %collective-permute-start.35) | collective-permute-done | bytes 1572896 | tf_op jit(solution)/shard_map/ppermute | solution.py:21
  185.5 2.6 fusion.10
  188.2 1.7 collective-permute-start.38
  191.9 9.4 %collective-permute-done.38.refs_3_ = bf16[2,256,384]{2,1,0:T(8,128)(2,1)S(1)} collective-permute-done((bf16[2,256,384]{2,1,0:T(8,128)(2,1)}, bf16[2,256,384]{2,1,0:T(8,128)(2,1)S(1)}, u32[]{:S(2)}, u32[]{:S(2)}) %collective-permute-start.38) | collective-permute-done | bytes 393248 | tf_op jit(solution)/shard_map/ppermute | solution.py:21
  201.3 7.6 %collective-permute-done.37.refs_2_ = bf16[2,256,384]{2,1,0:T(8,128)(2,1)S(1)} collective-permute-done((bf16[2,256,384]{2,1,0:T(8,128)(2,1)S(1)}, bf16[2,256,384]{2,1,0:T(8,128)(2,1)S(1)}, u32[]{:S(2)}, u32[]{:S(2)}) %collective-permute-start.37) | collective-permute-done | bytes 393248 | tf_op jit(solution)/shard_map/ppermute | solution.py:21
  209.7 6.7 %shard_map.244 = (bf16[2,64,768]{2,1,0:T(8,128)(2,1)}, bf16[2,64,768]{2,1,0:T(8,128)(2,1)}, bf16[2,2,64,768]{3,2,1,0:T(8,128)(2,1)}, bf16[4,5,32,576]{3,2,1,0:T(8,128)(2,1)}, bf16[4,5,32,576]{3,2,1,0:T(8,128)(2,1)}) custom-call(s32[3]{0:T(128)} %pad_add_fusion.meta, bf16[2,256,384]{2,1,0:T(8,128)(2,1)} %get-tuple-element.161.refs_0_, ...), custom_call_target="tpu_custom_call" | custom-call | bytes 1048576 | tf_op jit(solution)/shard_map/pallas_call | solution.py:540
  216.6 2.4 collective-permute-done.40
  222.7 1.6 collective-permute-start.43
  227.0 14.2 %collective-permute-done.39 = bf16[2,2,64,768]{3,2,1,0:T(8,128)(2,1)S(1)} collective-permute-done((bf16[2,2,64,768]{3,2,1,0:T(8,128)(2,1)S(1)}, bf16[2,2,64,768]{3,2,1,0:T(8,128)(2,1)S(1)}, u32[]{:S(2)}, u32[]{:S(2)}) %collective-permute-start.39) | collective-permute-done | bytes 393248 | tf_op jit(solution)/shard_map/ppermute | solution.py:21
  243.4 2.9 %collective-permute-start.45 = (bf16[32,576]{1,0:T(8,128)(2,1)S(1)}, bf16[32,576]{1,0:T(8,128)(2,1)S(1)}, u32[]{:S(2)}, u32[]{:S(2)}) collective-permute-start(bf16[32,576]{1,0:T(8,128)(2,1)S(1)} %get-tuple-element.235), channel_id=1, source_target_pairs={{0,1},{1,0},{2,3},{3,2},{4,5},{5,4},{6,7},{7,6},{8,9},{9,8},{10,11... | collective-permute-start | bytes 110600 | tf_op jit(solution)/shard_map/ppermute | solution.py:21
  249.8 2.3 shard_map.246
  252.1 1.5 collective-permute-start.50
  257.0 1.6 fusion.51
  258.6 4.4 %fusion.49 = (f32[8,1,96,768]{3,2,1,0:T(8,128)}, f32[8,1,96,768]{3,2,1,0:T(8,128)}) fusion(bf16[8,2,96,768]{3,2,1,0:T(8,128)(2,1)} %bitcast.126), kind=kLoop, calls=%fused_computation.148 | loop fusion | bytes 9437184 | tf_op jit(solution)/shard_map/slice | solution.py:833
  264.9 2.9 %shard_map.245 = f32[128,768]{1,0:T(8,128)} custom-call(s32[3]{0:T(128)} %pad_add_fusion.meta, bf16[2,64,768]{2,1,0:T(8,128)(2,1)} %fusion.11.grad_ref, bf16[128,768]{1,0:T(8,128)(2,1)} %bitcast.134, f32[1,768]{1,0:T(1,128)} %reshape.206.gain_ref, f32[128,768]{1,0:T(8,128)} %get-tuple-element.176.resid_grad_ref), custom_call_target="tpu_custom_call" | custom-call | bytes 1048576 | tf_op jit(solution)/shard_map/pallas_call | solution.py:540
  269.3 3.5 %shard_map.247 = (f32[192,2304]{1,0:T(8,128)}, f32[192,768]{1,0:T(8,128)}) custom-call(s32[3]{0:T(128)} %pad_add_fusion.meta, bf16[24,3072]{1,0:T(8,128)(2,1)} %get-tuple-element.191.refs_0_, bf16[24,3072]{1,0:T(8,128)(2,1)} %copy-done.28, bf16[24,3072]{1,0:T(8,128)(2,1)} %copy-done.27, bf16[24,3072]{1,0:T(8,128)(2,1)} %copy-done.26, ...), custom_call_target="tpu_custom_call" | custom-call | bytes 1048576 | tf_op jit(solution)/shard_map/pallas_call | solution.py:540
  (296 shorter events, 62.1 us)
Async XLA Ops:
  7.2 48.0 %all-gather.7.cloned.1.call-start = ((), (), s32[]{:S(2)}) async-start(), calls=%async_computation.3 | async-start | bytes 1769472 | tf_op jit(solution)/shard_map/all_gather | solution.py:664
  7.9 85.6 %all-gather.5.cloned.1.call-start = ((), (), s32[]{:S(2)}) async-start(), calls=%async_computation.2 | async-start | bytes 1597440 | tf_op jit(solution)/shard_map/all_gather | solution.py:672
  9.9 5.7 %collective-permute-start = (bf16[64,576]{1,0:T(8,128)(2,1)S(1)}, bf16[64,576]{1,0:T(8,128)(2,1)S(1)}, u32[]{:S(2)}, u32[]{:S(2)}) collective-permute-start(bf16[64,576]{1,0:T(8,128)(2,1)S(1)} %get-tuple-element.226), channel_id=1, source_target_pairs={{0,1},{1,0},{2,3},{3,2},{4,5},{5,4},{6,7},{7,6},{8,9},{9,8},{10,11... | collective-permute-start | bytes 221192 | tf_op jit(solution)/shard_map/ppermute | solution.py:21
  13.0 9.2 %collective-permute-start.1 = (bf16[64,576]{1,0:T(8,128)(2,1)S(1)}, bf16[64,576]{1,0:T(8,128)(2,1)S(1)}, u32[]{:S(2)}, u32[]{:S(2)}) collective-permute-start(bf16[64,576]{1,0:T(8,128)(2,1)S(1)} %get-tuple-element.227), channel_id=1, source_target_pairs={{0,2},{1,3},{2,0},{3,1},{4,6},{5,7},{6,4},{7,5},{8,10},{9,11},{10,... | collective-permute-start | bytes 221192 | tf_op jit(solution)/shard_map/ppermute | solution.py:21
  15.6 6.6 %collective-permute-start.2 = (bf16[64,576]{1,0:T(8,128)(2,1)S(1)}, bf16[64,576]{1,0:T(8,128)(2,1)S(1)}, u32[]{:S(2)}, u32[]{:S(2)}) collective-permute-start(bf16[64,576]{1,0:T(8,128)(2,1)S(1)} %get-tuple-element.228), channel_id=1, source_target_pairs={{0,3},{1,2},{2,1},{3,0},{4,7},{5,6},{6,5},{7,4},{8,11},{9,10},{10,... | collective-permute-start | bytes 221192 | tf_op jit(solution)/shard_map/ppermute | solution.py:21
  22.3 9.6 %collective-permute-start.5 = (bf16[2,64,768]{2,1,0:T(8,128)(2,1)S(1)}, bf16[2,64,768]{2,1,0:T(8,128)(2,1)S(1)}, u32[]{:S(2)}, u32[]{:S(2)}) collective-permute-start(bf16[2,64,768]{2,1,0:T(8,128)(2,1)S(1)} %bitcast.135), channel_id=1, source_target_pairs={{0,3},{1,2},{2,1},{3,0},{4,7},{5,6},{6,5},{7,4},{8,11},{9,10},{10,... | collective-permute-start | bytes 589832 | tf_op jit(solution)/shard_map/ppermute | solution.py:21
  25.0 16.5 %collective-permute-start.4 = (bf16[2,64,768]{2,1,0:T(8,128)(2,1)S(1)}, bf16[2,64,768]{2,1,0:T(8,128)(2,1)S(1)}, u32[]{:S(2)}, u32[]{:S(2)}) collective-permute-start(bf16[2,64,768]{2,1,0:T(8,128)(2,1)S(1)} %bitcast.136), channel_id=1, source_target_pairs={{0,2},{1,3},{2,0},{3,1},{4,6},{5,7},{6,4},{7,5},{8,10},{9,11},{10,... | collective-permute-start | bytes 589832 | tf_op jit(solution)/shard_map/ppermute | solution.py:21
  25.5 16.0 %collective-permute-start.3 = (bf16[2,64,768]{2,1,0:T(8,128)(2,1)S(1)}, bf16[2,64,768]{2,1,0:T(8,128)(2,1)S(1)}, u32[]{:S(2)}, u32[]{:S(2)}) collective-permute-start(bf16[2,64,768]{2,1,0:T(8,128)(2,1)S(1)} %bitcast.137), channel_id=1, source_target_pairs={{0,1},{1,0},{2,3},{3,2},{4,5},{5,4},{6,7},{7,6},{8,9},{9,8},{10,11... | collective-permute-start | bytes 589832 | tf_op jit(solution)/shard_map/ppermute | solution.py:21
  27.0 14.5 %collective-permute-start.8 = (bf16[4,48,576]{2,1,0:T(8,128)(2,1)S(1)}, bf16[4,48,576]{2,1,0:T(8,128)(2,1)S(1)}, u32[]{:S(2)}, u32[]{:S(2)}) collective-permute-start(bf16[4,48,576]{2,1,0:T(8,128)(2,1)S(1)} %slice.254.refs_5_), channel_id=1, source_target_pairs={{0,24},{4,28},{8,16},{12,20},{16,8},{20,12},{24,0},{28,4},{1,25},{... | collective-permute-start | bytes 663560 | tf_op jit(solution)/shard_map/ppermute | solution.py:21
  29.4 12.8 %collective-permute-start.7 = (bf16[4,48,576]{2,1,0:T(8,128)(2,1)S(1)}, bf16[4,48,576]{2,1,0:T(8,128)(2,1)S(1)}, u32[]{:S(2)}, u32[]{:S(2)}) collective-permute-start(bf16[4,48,576]{2,1,0:T(8,128)(2,1)S(1)} %slice.254.refs_5_), channel_id=1, source_target_pairs={{0,16},{4,20},{8,24},{12,28},{16,0},{20,4},{24,8},{28,12},{1,17},{... | collective-permute-start | bytes 663560 | tf_op jit(solution)/shard_map/ppermute | solution.py:21
  31.9 10.5 %collective-permute-start.6 = (bf16[4,48,576]{2,1,0:T(8,128)(2,1)S(1)}, bf16[4,48,576]{2,1,0:T(8,128)(2,1)S(1)}, u32[]{:S(2)}, u32[]{:S(2)}) collective-permute-start(bf16[4,48,576]{2,1,0:T(8,128)(2,1)S(1)} %slice.254.refs_5_), channel_id=1, source_target_pairs={{0,8},{4,12},{8,0},{12,4},{16,24},{20,28},{24,16},{28,20},{1,9},{5... | collective-permute-start | bytes 663560 | tf_op jit(solution)/shard_map/ppermute | solution.py:21
  42.4 71.7 %all-gather.9.cloned.1.call-start = ((), (), s32[]{:S(2)}) async-start(), calls=%async_computation.4 | async-start | bytes 1474560 | tf_op jit(solution)/shard_map/all_gather | solution.py:692
  44.2 147.7 %reduce-scatter.3.cloned.1.call-start = ((), (), s32[]{:S(2)}) async-start(), calls=%async_computation.5 | async-start | bytes 1769472 | tf_op jit(solution)/shard_map/reduce_scatter | solution.py:737
  50.5 13.2 %collective-permute-start.11 = (bf16[2,256,384]{2,1,0:T(8,128)(2,1)}, bf16[2,256,384]{2,1,0:T(8,128)(2,1)S(1)}, u32[]{:S(2)}, u32[]{:S(2)}) collective-permute-start(bf16[2,256,384]{2,1,0:T(8,128)(2,1)} %get-tuple-element.116.refs_1_), channel_id=1, source_target_pairs={{0,24},{4,28},{8,16},{12,20},{16,8},{20,12},{24,0},{28,4},{1,25},{... | collective-permute-start | bytes 1179656 | tf_op jit(solution)/shard_map/ppermute | solution.py:21
  52.4 18.1 %collective-permute-start.10 = (bf16[2,256,384]{2,1,0:T(8,128)(2,1)}, bf16[2,256,384]{2,1,0:T(8,128)(2,1)S(1)}, u32[]{:S(2)}, u32[]{:S(2)}) collective-permute-start(bf16[2,256,384]{2,1,0:T(8,128)(2,1)} %get-tuple-element.116.refs_1_), channel_id=1, source_target_pairs={{0,16},{4,20},{8,24},{12,28},{16,0},{20,4},{24,8},{28,12},{1,17},{... | collective-permute-start | bytes 1179656 | tf_op jit(solution)/shard_map/ppermute | solution.py:21
  53.5 17.2 %collective-permute-start.9 = (bf16[2,256,384]{2,1,0:T(8,128)(2,1)}, bf16[2,256,384]{2,1,0:T(8,128)(2,1)S(1)}, u32[]{:S(2)}, u32[]{:S(2)}) collective-permute-start(bf16[2,256,384]{2,1,0:T(8,128)(2,1)} %get-tuple-element.116.refs_1_), channel_id=1, source_target_pairs={{0,8},{4,12},{8,0},{12,4},{16,24},{20,28},{24,16},{28,20},{1,9},{5... | collective-permute-start | bytes 1179656 | tf_op jit(solution)/shard_map/ppermute | solution.py:21
  87.8 10.4 %collective-permute-start.16 = (bf16[2,64,192]{2,1,0:T(8,128)(2,1)}, bf16[2,64,192]{2,1,0:T(8,128)(2,1)S(1)}, u32[]{:S(2)}, u32[]{:S(2)}) collective-permute-start(bf16[2,64,192]{2,1,0:T(8,128)(2,1)} %get-tuple-element.121.refs_11_), channel_id=1, source_target_pairs={{0,1},{1,0},{2,3},{3,2},{4,5},{5,4},{6,7},{7,6},{8,9},{9,8},{10,11... | collective-permute-start | bytes 147464 | tf_op jit(solution)/shard_map/ppermute | solution.py:21
  91.1 13.1 %collective-permute-start.17 = (bf16[2,64,192]{2,1,0:T(8,128)(2,1)}, bf16[2,64,192]{2,1,0:T(8,128)(2,1)S(1)}, u32[]{:S(2)}, u32[]{:S(2)}) collective-permute-start(bf16[2,64,192]{2,1,0:T(8,128)(2,1)} %get-tuple-element.122.refs_12_), channel_id=1, source_target_pairs={{0,2},{1,3},{2,0},{3,1},{4,6},{5,7},{6,4},{7,5},{8,10},{9,11},{10,... | collective-permute-start | bytes 147464 | tf_op jit(solution)/shard_map/ppermute | solution.py:21
  91.1 13.1 %collective-permute-start.18 = (bf16[2,64,192]{2,1,0:T(8,128)(2,1)}, bf16[2,64,192]{2,1,0:T(8,128)(2,1)S(1)}, u32[]{:S(2)}, u32[]{:S(2)}) collective-permute-start(bf16[2,64,192]{2,1,0:T(8,128)(2,1)} %get-tuple-element.123.refs_13_), channel_id=1, source_target_pairs={{0,3},{1,2},{2,1},{3,0},{4,7},{5,6},{6,5},{7,4},{8,11},{9,10},{10,... | collective-permute-start | bytes 147464 | tf_op jit(solution)/shard_map/ppermute | solution.py:21
  108.1 8.3 %collective-permute-start.21 = (bf16[128,768]{1,0:T(8,128)(2,1)}, bf16[128,768]{1,0:T(8,128)(2,1)S(1)}, u32[]{:S(2)}, u32[]{:S(2)}) collective-permute-start(bf16[128,768]{1,0:T(8,128)(2,1)} %get-tuple-element.133), channel_id=1, source_target_pairs={{0,24},{4,28},{8,16},{12,20},{16,8},{20,12},{24,0},{28,4},{1,25},{... | collective-permute-start | bytes 589832 | tf_op jit(solution)/shard_map/ppermute | solution.py:21
  109.4 8.4 %collective-permute-start.20 = (bf16[128,768]{1,0:T(8,128)(2,1)}, bf16[128,768]{1,0:T(8,128)(2,1)S(1)}, u32[]{:S(2)}, u32[]{:S(2)}) collective-permute-start(bf16[128,768]{1,0:T(8,128)(2,1)} %get-tuple-element.133), channel_id=1, source_target_pairs={{0,16},{4,20},{8,24},{12,28},{16,0},{20,4},{24,8},{28,12},{1,17},{... | collective-permute-start | bytes 589832 | tf_op jit(solution)/shard_map/ppermute | solution.py:21
  111.0 6.8 %collective-permute-start.19 = (bf16[128,768]{1,0:T(8,128)(2,1)}, bf16[128,768]{1,0:T(8,128)(2,1)S(1)}, u32[]{:S(2)}, u32[]{:S(2)}) collective-permute-start(bf16[128,768]{1,0:T(8,128)(2,1)} %get-tuple-element.133), channel_id=1, source_target_pairs={{0,8},{4,12},{8,0},{12,4},{16,24},{20,28},{24,16},{28,20},{1,9},{5... | collective-permute-start | bytes 589832 | tf_op jit(solution)/shard_map/ppermute | solution.py:21
  129.5 8.8 %collective-permute-start.29 = (bf16[128,768]{1,0:T(8,128)(2,1)S(1)}, bf16[128,768]{1,0:T(8,128)(2,1)S(1)}, u32[]{:S(2)}, u32[]{:S(2)}) collective-permute-start(bf16[128,768]{1,0:T(8,128)(2,1)S(1)} %get-tuple-element.215), channel_id=1, source_target_pairs={{0,24},{4,28},{8,16},{12,20},{16,8},{20,12},{24,0},{28,4},{1,25},{... | collective-permute-start | bytes 589832 | tf_op jit(solution)/shard_map/ppermute | solution.py:21
  131.2 10.5 %collective-permute-start.28 = (bf16[128,768]{1,0:T(8,128)(2,1)S(1)}, bf16[128,768]{1,0:T(8,128)(2,1)S(1)}, u32[]{:S(2)}, u32[]{:S(2)}) collective-permute-start(bf16[128,768]{1,0:T(8,128)(2,1)S(1)} %get-tuple-element.216), channel_id=1, source_target_pairs={{0,16},{4,20},{8,24},{12,28},{16,0},{20,4},{24,8},{28,12},{1,17},{... | collective-permute-start | bytes 589832 | tf_op jit(solution)/shard_map/ppermute | solution.py:21
  132.5 9.2 %collective-permute-start.27 = (bf16[128,768]{1,0:T(8,128)(2,1)S(1)}, bf16[128,768]{1,0:T(8,128)(2,1)S(1)}, u32[]{:S(2)}, u32[]{:S(2)}) collective-permute-start(bf16[128,768]{1,0:T(8,128)(2,1)S(1)} %get-tuple-element.217), channel_id=1, source_target_pairs={{0,8},{4,12},{8,0},{12,4},{16,24},{20,28},{24,16},{28,20},{1,9},{5... | collective-permute-start | bytes 589832 | tf_op jit(solution)/shard_map/ppermute | solution.py:21
  141.7 78.8 %reduce-scatter.5.cloned.1.call-start = ((), (), s32[]{:S(2)}) async-start(), calls=%async_computation.6 | async-start | bytes 1474560 | tf_op jit(solution)/shard_map/reduce_scatter | solution.py:766
  146.6 14.2 %collective-permute-start.30 = (bf16[1,128,768]{2,1,0:T(8,128)(2,1)}, bf16[1,128,768]{2,1,0:T(8,128)(2,1)S(1)}, u32[]{:S(2)}, u32[]{:S(2)}) collective-permute-start(bf16[1,128,768]{2,1,0:T(8,128)(2,1)} %bitcast.156), channel_id=1, source_target_pairs={{0,1},{1,0},{2,3},{3,2},{4,5},{5,4},{6,7},{7,6},{8,9},{9,8},{10,11... | collective-permute-start | bytes 589832 | tf_op jit(solution)/shard_map/ppermute | solution.py:21
  153.0 9.5 %collective-permute-start.31 = (bf16[2,64,192]{2,1,0:T(8,128)(2,1)}, bf16[2,64,192]{2,1,0:T(8,128)(2,1)S(1)}, u32[]{:S(2)}, u32[]{:S(2)}) collective-permute-start(bf16[2,64,192]{2,1,0:T(8,128)(2,1)} %get-tuple-element.147), channel_id=1, source_target_pairs={{0,1},{1,0},{2,3},{3,2},{4,5},{5,4},{6,7},{7,6},{8,9},{9,8},{10,11... | collective-permute-start | bytes 147464 | tf_op jit(solution)/shard_map/ppermute | solution.py:21
  153.0 9.4 %collective-permute-start.32 = (bf16[2,64,192]{2,1,0:T(8,128)(2,1)}, bf16[2,64,192]{2,1,0:T(8,128)(2,1)S(1)}, u32[]{:S(2)}, u32[]{:S(2)}) collective-permute-start(bf16[2,64,192]{2,1,0:T(8,128)(2,1)} %get-tuple-element.148), channel_id=1, source_target_pairs={{0,2},{1,3},{2,0},{3,1},{4,6},{5,7},{6,4},{7,5},{8,10},{9,11},{10,... | collective-permute-start | bytes 147464 | tf_op jit(solution)/shard_map/ppermute | solution.py:21
  153.4 9.1 %collective-permute-start.33 = (bf16[2,64,192]{2,1,0:T(8,128)(2,1)}, bf16[2,64,192]{2,1,0:T(8,128)(2,1)S(1)}, u32[]{:S(2)}, u32[]{:S(2)}) collective-permute-start(bf16[2,64,192]{2,1,0:T(8,128)(2,1)} %get-tuple-element.149), channel_id=1, source_target_pairs={{0,3},{1,2},{2,1},{3,0},{4,7},{5,6},{6,5},{7,4},{8,11},{9,10},{10,... | collective-permute-start | bytes 147464 | tf_op jit(solution)/shard_map/ppermute | solution.py:21
  162.5 19.2 %collective-permute-start.34 = (bf16[2,128,768]{2,1,0:T(8,128)(2,1)S(1)}, bf16[2,128,768]{2,1,0:T(8,128)(2,1)S(1)}, u32[]{:S(2)}, u32[]{:S(2)}) collective-permute-start(bf16[2,128,768]{2,1,0:T(8,128)(2,1)S(1)} %pad_maximum_fusion.1), channel_id=1, source_target_pairs={{0,2},{1,3},{2,0},{3,1},{4,6},{5,7},{6,4},{7,5},{8,10},{9,11},{10,... | collective-permute-start | bytes 1179656 | tf_op jit(solution)/shard_map/ppermute | solution.py:21
  181.8 76.8 %all-gather.11.cloned.1.call-start = ((), (), s32[]{:S(2)}) async-start(), calls=%async_computation.7 | async-start | bytes 2654208 | tf_op jit(solution)/shard_map/all_gather | solution.py:793
  188.2 13.1 %collective-permute-start.38 = (bf16[2,256,384]{2,1,0:T(8,128)(2,1)}, bf16[2,256,384]{2,1,0:T(8,128)(2,1)S(1)}, u32[]{:S(2)}, u32[]{:S(2)}) collective-permute-start(bf16[2,256,384]{2,1,0:T(8,128)(2,1)} %get-tuple-element.209), channel_id=1, source_target_pairs={{0,24},{4,28},{8,16},{12,20},{16,8},{20,12},{24,0},{28,4},{1,25},{... | collective-permute-start | bytes 1179656 | tf_op jit(solution)/shard_map/ppermute | solution.py:21
  189.9 19.0 %collective-permute-start.37 = (bf16[2,256,384]{2,1,0:T(8,128)(2,1)S(1)}, bf16[2,256,384]{2,1,0:T(8,128)(2,1)S(1)}, u32[]{:S(2)}, u32[]{:S(2)}) collective-permute-start(bf16[2,256,384]{2,1,0:T(8,128)(2,1)S(1)} %get-tuple-element.210), channel_id=1, source_target_pairs={{0,16},{4,20},{8,24},{12,28},{16,0},{20,4},{24,8},{28,12},{1,17},{... | collective-permute-start | bytes 1179656 | tf_op jit(solution)/shard_map/ppermute | solution.py:21
  191.0 17.9 %collective-permute-start.36 = (bf16[2,256,384]{2,1,0:T(8,128)(2,1)S(1)}, bf16[2,256,384]{2,1,0:T(8,128)(2,1)S(1)}, u32[]{:S(2)}, u32[]{:S(2)}) collective-permute-start(bf16[2,256,384]{2,1,0:T(8,128)(2,1)S(1)} %get-tuple-element.211), channel_id=1, source_target_pairs={{0,8},{4,12},{8,0},{12,4},{16,24},{20,28},{24,16},{28,20},{1,9},{5... | collective-permute-start | bytes 1179656 | tf_op jit(solution)/shard_map/ppermute | solution.py:21
  220.6 20.5 %collective-permute-start.39 = (bf16[2,2,64,768]{3,2,1,0:T(8,128)(2,1)S(1)}, bf16[2,2,64,768]{3,2,1,0:T(8,128)(2,1)S(1)}, u32[]{:S(2)}, u32[]{:S(2)}) collective-permute-start(bf16[2,2,64,768]{3,2,1,0:T(8,128)(2,1)S(1)} %copy-done.56), channel_id=1, source_target_pairs={{0,2},{1,3},{2,0},{3,1},{4,6},{5,7},{6,4},{7,5},{8,10},{9,11},{10,... | collective-permute-start | bytes 1179656 | tf_op jit(solution)/shard_map/ppermute | solution.py:21
  222.7 18.5 %collective-permute-start.43 = (bf16[5,32,576]{2,1,0:T(8,128)(2,1)S(1)}, bf16[5,32,576]{2,1,0:T(8,128)(2,1)S(1)}, u32[]{:S(2)}, u32[]{:S(2)}) collective-permute-start(bf16[5,32,576]{2,1,0:T(8,128)(2,1)S(1)} %get-tuple-element.219), channel_id=1, source_target_pairs={{0,24},{4,28},{8,16},{12,20},{16,8},{20,12},{24,0},{28,4},{1,25},{... | collective-permute-start | bytes 552968 | tf_op jit(solution)/shard_map/ppermute | solution.py:21
  224.3 16.9 %collective-permute-start.42 = (bf16[5,32,576]{2,1,0:T(8,128)(2,1)S(1)}, bf16[5,32,576]{2,1,0:T(8,128)(2,1)S(1)}, u32[]{:S(2)}, u32[]{:S(2)}) collective-permute-start(bf16[5,32,576]{2,1,0:T(8,128)(2,1)S(1)} %get-tuple-element.220), channel_id=1, source_target_pairs={{0,16},{4,20},{8,24},{12,28},{16,0},{20,4},{24,8},{28,12},{1,17},{... | collective-permute-start | bytes 552968 | tf_op jit(solution)/shard_map/ppermute | solution.py:21
  225.6 15.5 %collective-permute-start.41 = (bf16[5,32,576]{2,1,0:T(8,128)(2,1)S(1)}, bf16[5,32,576]{2,1,0:T(8,128)(2,1)S(1)}, u32[]{:S(2)}, u32[]{:S(2)}) collective-permute-start(bf16[5,32,576]{2,1,0:T(8,128)(2,1)S(1)} %get-tuple-element.221), channel_id=1, source_target_pairs={{0,8},{4,12},{8,0},{12,4},{16,24},{20,28},{24,16},{28,20},{1,9},{5... | collective-permute-start | bytes 552968 | tf_op jit(solution)/shard_map/ppermute | solution.py:21
  241.9 5.8 %collective-permute-start.47 = (bf16[32,576]{1,0:T(8,128)(2,1)S(1)}, bf16[32,576]{1,0:T(8,128)(2,1)S(1)}, u32[]{:S(2)}, u32[]{:S(2)}) collective-permute-start(bf16[32,576]{1,0:T(8,128)(2,1)S(1)} %get-tuple-element.233), channel_id=1, source_target_pairs={{0,3},{1,2},{2,1},{3,0},{4,7},{5,6},{6,5},{7,4},{8,11},{9,10},{10,... | collective-permute-start | bytes 110600 | tf_op jit(solution)/shard_map/ppermute | solution.py:21
  243.4 5.3 %collective-permute-start.46 = (bf16[32,576]{1,0:T(8,128)(2,1)S(1)}, bf16[32,576]{1,0:T(8,128)(2,1)S(1)}, u32[]{:S(2)}, u32[]{:S(2)}) collective-permute-start(bf16[32,576]{1,0:T(8,128)(2,1)S(1)} %get-tuple-element.234), channel_id=1, source_target_pairs={{0,2},{1,3},{2,0},{3,1},{4,6},{5,7},{6,4},{7,5},{8,10},{9,11},{10,... | collective-permute-start | bytes 110600 | tf_op jit(solution)/shard_map/ppermute | solution.py:21
  243.4 5.8 %collective-permute-start.45 = (bf16[32,576]{1,0:T(8,128)(2,1)S(1)}, bf16[32,576]{1,0:T(8,128)(2,1)S(1)}, u32[]{:S(2)}, u32[]{:S(2)}) collective-permute-start(bf16[32,576]{1,0:T(8,128)(2,1)S(1)} %get-tuple-element.235), channel_id=1, source_target_pairs={{0,1},{1,0},{2,3},{3,2},{4,5},{5,4},{6,7},{7,6},{8,9},{9,8},{10,11... | collective-permute-start | bytes 110600 | tf_op jit(solution)/shard_map/ppermute | solution.py:21
  246.4 17.7 %collective-permute-start.44 = (bf16[1,2,64,768]{3,2,1,0:T(8,128)(2,1)S(1)}, bf16[1,2,64,768]{3,2,1,0:T(8,128)(2,1)S(1)}, u32[]{:S(2)}, u32[]{:S(2)}) collective-permute-start(bf16[1,2,64,768]{3,2,1,0:T(8,128)(2,1)S(1)} %fusion.22), channel_id=1, source_target_pairs={{0,1},{1,0},{2,3},{3,2},{4,5},{5,4},{6,7},{7,6},{8,9},{9,8},{10,11... | collective-permute-start | bytes 589832 | tf_op jit(solution)/shard_map/ppermute | solution.py:21
  252.1 10.9 %collective-permute-start.50 = (bf16[24,3072]{1,0:T(8,128)(2,1)}, bf16[24,3072]{1,0:T(8,128)(2,1)S(1)}, u32[]{:S(2)}, u32[]{:S(2)}) collective-permute-start(bf16[24,3072]{1,0:T(8,128)(2,1)} %get-tuple-element.191.refs_0_), channel_id=1, source_target_pairs={{0,24},{4,28},{8,16},{12,20},{16,8},{20,12},{24,0},{28,4},{1,25},{... | collective-permute-start | bytes 442376 | tf_op jit(solution)/shard_map/ppermute | solution.py:21
  253.6 9.3 %collective-permute-start.49 = (bf16[24,3072]{1,0:T(8,128)(2,1)}, bf16[24,3072]{1,0:T(8,128)(2,1)S(1)}, u32[]{:S(2)}, u32[]{:S(2)}) collective-permute-start(bf16[24,3072]{1,0:T(8,128)(2,1)} %get-tuple-element.191.refs_0_), channel_id=1, source_target_pairs={{0,16},{4,20},{8,24},{12,28},{16,0},{20,4},{24,8},{28,12},{1,17},{... | collective-permute-start | bytes 442376 | tf_op jit(solution)/shard_map/ppermute | solution.py:21
  255.0 8.0 %collective-permute-start.48 = (bf16[24,3072]{1,0:T(8,128)(2,1)}, bf16[24,3072]{1,0:T(8,128)(2,1)S(1)}, u32[]{:S(2)}, u32[]{:S(2)}) collective-permute-start(bf16[24,3072]{1,0:T(8,128)(2,1)} %get-tuple-element.191.refs_0_), channel_id=1, source_target_pairs={{0,8},{4,12},{8,0},{12,4},{16,24},{20,28},{24,16},{28,20},{1,9},{5... | collective-permute-start | bytes 442376 | tf_op jit(solution)/shard_map/ppermute | solution.py:21
  263.0 4.8 %collective-permute-start.51 = (bf16[24,3072]{1,0:T(8,128)(2,1)S(1)}, bf16[24,3072]{1,0:T(8,128)(2,1)S(1)}, u32[]{:S(2)}, u32[]{:S(2)}) collective-permute-start(bf16[24,3072]{1,0:T(8,128)(2,1)S(1)} %copy-done.25), channel_id=1, source_target_pairs={{0,4},{4,0},{8,12},{12,8},{16,20},{20,16},{24,28},{28,24},{1,5},{5... | collective-permute-start | bytes 442376 | tf_op jit(solution)/shard_map/ppermute | solution.py:21
  263.1 4.7 %collective-permute-start.52 = (bf16[24,3072]{1,0:T(8,128)(2,1)S(1)}, bf16[24,3072]{1,0:T(8,128)(2,1)S(1)}, u32[]{:S(2)}, u32[]{:S(2)}) collective-permute-start(bf16[24,3072]{1,0:T(8,128)(2,1)S(1)} %collective-permute-done.48.refs_1_), channel_id=1, source_target_pairs={{0,4},{4,0},{8,12},{12,8},{16,20},{20,16},{24,28},{28,24},{1,5},{5... | collective-permute-start | bytes 442376 | tf_op jit(solution)/shard_map/ppermute | solution.py:21
  (73 other events, 411.4 us)
Sparse Core Ops, SparseCore 0:
  9.9 33.3 all-gather.6
  45.4 31.6 all-gather.4
  78.7 35.2 all-gather.8
  141.9 41.7 reduce-scatter.2
  185.8 29.1 reduce-scatter.4
  220.7 31.9 all-gather.10

commit v3 on v2

--- a/solution.py
+++ b/solution.py
@@ -153,8 +153,7 @@
     width = heads * HEAD_DIM
     scale = HEAD_DIM ** (-0.5)
     copies = load_pieces(piece_refs, kv_ref, sems)
-    for copy in copies:
-        copy.wait()
+    copies[0].wait()
     for j in range(2):
         block = meta[count + j]
         for tile in range(size // rows):
@@ -191,6 +190,9 @@
             own = jnp.where(seen, score(block), MASKED)
             score_ref[block] = own
             top_ref[...] = lanes(jnp.maximum, own)
+            if j == 0 and tile == 0:
+                for copy in copies[1:]:
+                    copy.wait()
             in_pairs(0, block, scores)
             top_ref[...] = jnp.broadcast_to(
                 jnp.max(top_ref[...], axis=1, keepdims=True), top_ref.shape
@@ -292,7 +294,7 @@
         dq_ref[j] = (whole[:, :width] * scale).astype(BF16)
     for i in range(count):
         to_ref = keep_ref if i < pieces else send_ref
-        to_ref[i % pieces // 2, i % 2] = jnp.transpose(acc_ref[i]).astype(BF16)
+        to_ref[i % pieces // 2, i % 2] = acc_ref[i].astype(BF16)
 
 
 def forward_call(meta, query, keyvals, heads, groups):
@@ -319,7 +321,7 @@
             pltpu.VMEM((heads * rows, 128), F32),
             pltpu.VMEM((heads * rows, wide), F32),
         ],
-        16 * pieces * size * size * wide * heads,
+        40 * pieces * size * size * wide * heads,
         range(1, 1 + pieces),
     )
 
@@ -328,7 +330,7 @@
     size, wide = query.shape[1:]
     part = heads * HEAD_DIM
     pieces = len(keyvals)
-    half = jax.ShapeDtypeStruct((pieces // 2, 2, size, 2 * part), BF16)
+    half = jax.ShapeDtypeStruct((pieces // 2, 2, 2 * part, size), BF16)
     return in_vmem(
         functools.partial(attend_back_kernel, heads=heads, pieces=pieces, groups=groups),
         meta,
@@ -426,14 +428,13 @@
     here, member = meta[0], meta[1]
     fetch = keep_ref.shape[0]
     across = keep_ref.shape[3]
-    part2 = sums[0].shape[2]
     slot = outs[0].shape[1]
     size = slot * groups
     width = unit_ref.shape[2]
     gain_total = jnp.zeros((1, width), F32)
     shift_total = jnp.zeros((1, width), F32)
     for j in range(2):
-        keyval = sum(ref[j].astype(F32) for ref in sums).astype(BF16)
+        keyval = jnp.transpose(sum(ref[j].astype(F32) for ref in sums)).astype(BF16)
         grad = jnp.concatenate([keyval, dq_ref[j]], axis=1)
         grad_ref[j] = grad
         normed_grad = contract_cols(grad, proj_ref[...])
@@ -789,8 +790,8 @@
         ],
     )
     *normed_pieces, normed_far, in_keep, in_send = results
+    ffn_grads = lax.all_gather(after(ffn_term, in_keep), "ctx", axis=0, tiled=True)
     in_sums = ctx_collect(in_keep, in_send)
-    ffn_grads = lax.all_gather(after(ffn_term, in_sums[0]), "ctx", axis=0, tiled=True)
     mask = groups // 2
     came = swap(normed_far, "fsdp", mask)
     came, *in_sums = lax.optimization_barrier((came, *in_sums))

time: 281 us -> 276 us (0.982)
  waiting for transfers between devices: 90.8 us -> 87.9 us
    ppermute x55, waiting for transfers between devices: 87.5 us -> 82 us  [swap(): lax.ppermute(x, axis, [(i, i ^ mask) for i in range(lax.axis_size(axis))])]
    unnamed x129 -> x125, local copies, waits for them, and re-layouts: 5.98 us -> 5.78 us
where the time goes in v3:
time: 276 us; the launch traced here: 275 us
  waiting for transfers between devices  87.9 us (32%)
  Pallas kernels  63.6 us (23%)
  starting transfers between devices  63.5 us (23%)
  local copies, waits for them, and re-layouts  24.5 us (9%)
  between operations  14.9 us (5%)
  other arithmetic  12.6 us (5%)
  matrix products  7.93 us (3%)
    ppermute x55, waiting for transfers between devices, swap(): lax.ppermute(x, axis, [(i, i ^ mask) for i in range(lax.axis_size(axis))])  82 us
    ppermute x55, starting transfers between devices, swap(): lax.ppermute(x, axis, [(i, i ^ mask) for i in range(lax.axis_size(axis))])  63.3 us
    pallas_call x9, Pallas kernels, in_vmem(): pl.pallas_call(kernel, grid_spec=pltpu.PrefetchScalarGridSpec(num_scalar_...  56.8 us
    pallas_call x2, Pallas kernels, shuffle(): pl.pallas_call(shuffle_kernel, grid_spec=pltpu.PrefetchScalarGridSpec(num...  6.76 us
    unnamed x125, local copies, waits for them, and re-layouts  5.78 us
  transfers between devices with their start and end apart: 61, of which 32 were waited for; matrix products, arithmetic and copies ran while one was open for 13% of the time, Pallas kernels for 22%

profile of v3, /device:TPU:0, one launch (start us, length us, event | category | flops | bytes accessed | tf_op | source)
XLA Modules:
  0.0 274.9 jit_solution(18020975211911392675)
XLA Ops:
  9.9 3.1 %collective-permute-start = (bf16[64,576]{1,0:T(8,128)(2,1)S(1)}, bf16[64,576]{1,0:T(8,128)(2,1)S(1)}, u32[]{:S(2)}, u32[]{:S(2)}) collective-permute-start(bf16[64,576]{1,0:T(8,128)(2,1)S(1)} %get-tuple-element.226), channel_id=1, source_target_pairs={{0,1},{1,0},{2,3},{3,2},{4,5},{5,4},{6,7},{7,6},{8,9},{9,8},{10,11... | collective-permute-start | bytes 221192 | tf_op jit(solution)/shard_map/ppermute | solution.py:21
  13.0 2.6 collective-permute-start.1
  15.6 6.6 %collective-permute-done.1 = bf16[64,576]{1,0:T(8,128)(2,1)S(1)} collective-permute-done((bf16[64,576]{1,0:T(8,128)(2,1)S(1)}, bf16[64,576]{1,0:T(8,128)(2,1)S(1)}, u32[]{:S(2)}, u32[]{:S(2)}) %collective-permute-start.1) | collective-permute-done | bytes 73760 | tf_op jit(solution)/shard_map/ppermute | solution.py:21
  22.3 2.5 collective-permute-start.5
  25.5 1.5 collective-permute-start.3
  27.0 2.4 collective-permute-start.8
  29.9 2.0 collective-permute-done.5.refs_3_
  31.9 1.5 collective-permute-start.6
  34.2 7.3 %collective-permute-done.4.refs_2_ = bf16[2,64,768]{2,1,0:T(8,128)(2,1)S(1)} collective-permute-done((bf16[2,64,768]{2,1,0:T(8,128)(2,1)S(1)}, bf16[2,64,768]{2,1,0:T(8,128)(2,1)S(1)}, u32[]{:S(2)}, u32[]{:S(2)}) %collective-permute-start.4) | collective-permute-done | bytes 196640 | tf_op jit(solution)/shard_map/ppermute | solution.py:21
  43.7 5.0 %shard_map.237 = (bf16[2,256,384]{2,1,0:T(8,128)(2,1)}, bf16[2,256,256]{2,1,0:T(8,128)(2,1)}, bf16[2,256,768]{2,1,0:T(8,128)(2,1)}, f32[2,256,768]{2,1,0:T(8,128)}, bf16[768,576]{1,0:T(8,128)(2,1)}) custom-call(s32[3]{0:T(128)} %pad_add_fusion.meta, bf16[2,64,768]{2,1,0:T(8,128)(2,1)} %bitcast.132, bf16[2,64,768]{2,1,0:T(8,128)(2,1)} %copy-done.24, ...), custom_call_target="tpu_custom_call" | custom-call | bytes 1048576 | tf_op jit(solution)/shard_map/pallas_call | solution.py:541
  48.7 1.8 collective-permute-start.11
  54.9 3.4 %shard_map.238 = bf16[8,128,768]{2,1,0:T(8,128)(2,1)} custom-call(s32[8]{0:T(128)} %add_xor_fusion.table, bf16[8,128,768]{2,1,0:T(8,128)(2,1)} %bitcast.138), custom_call_target="tpu_custom_call" | custom-call | tf_op jit(solution)/shard_map/pallas_call | solution.py:70
  58.3 3.6 %collective-permute-done.11.refs_4_ = bf16[2,256,384]{2,1,0:T(8,128)(2,1)S(1)} collective-permute-done((bf16[2,256,384]{2,1,0:T(8,128)(2,1)}, bf16[2,256,384]{2,1,0:T(8,128)(2,1)S(1)}, u32[]{:S(2)}, u32[]{:S(2)}) %collective-permute-start.11) | collective-permute-done | bytes 393248 | tf_op jit(solution)/shard_map/ppermute | solution.py:21
  61.9 6.7 %collective-permute-done.10.refs_3_ = bf16[2,256,384]{2,1,0:T(8,128)(2,1)S(1)} collective-permute-done((bf16[2,256,384]{2,1,0:T(8,128)(2,1)}, bf16[2,256,384]{2,1,0:T(8,128)(2,1)S(1)}, u32[]{:S(2)}, u32[]{:S(2)}) %collective-permute-start.10) | collective-permute-done | bytes 393248 | tf_op jit(solution)/shard_map/ppermute | solution.py:21
  72.9 12.8 %shard_map.239 = (bf16[2,64,192]{2,1,0:T(8,128)(2,1)}, bf16[2,64,192]{2,1,0:T(8,128)(2,1)}, bf16[2,64,192]{2,1,0:T(8,128)(2,1)}, bf16[2,64,192]{2,1,0:T(8,128)(2...) custom-call(s32[19]{0:T(128)} %pad_add_fusion.1.meta, bf16[2,256,256]{2,1,0:T(8,128)(2,1)} %get-tuple-element.114.refs_0_, ...), custom_call_target="tpu_custom_call" | custom-call | flops 16106127360 | bytes 1048576 | tf_op jit(solution)/shard_map/pallas_call | solution.py:541
  85.6 3.3 %collective-permute-start.16 = (bf16[2,64,192]{2,1,0:T(8,128)(2,1)}, bf16[2,64,192]{2,1,0:T(8,128)(2,1)S(1)}, u32[]{:S(2)}, u32[]{:S(2)}) collective-permute-start(bf16[2,64,192]{2,1,0:T(8,128)(2,1)} %get-tuple-element.121.refs_11_), channel_id=1, source_target_pairs={{0,1},{1,0},{2,3},{3,2},{4,5},{5,4},{6,7},{7,6},{8,9},{9,8},{10,11... | collective-permute-start | bytes 147464 | tf_op jit(solution)/shard_map/ppermute | solution.py:21
  88.9 2.4 collective-permute-start.18
  92.3 2.4 slice.255.refs_5_.refs_6_
  96.3 5.3 %collective-permute-done.17.refs_2_ = bf16[2,64,192]{2,1,0:T(8,128)(2,1)S(1)} collective-permute-done((bf16[2,64,192]{2,1,0:T(8,128)(2,1)}, bf16[2,64,192]{2,1,0:T(8,128)(2,1)S(1)}, u32[]{:S(2)}, u32[]{:S(2)}) %collective-permute-start.17) | collective-permute-done | bytes 49184 | tf_op jit(solution)/shard_map/ppermute | solution.py:21
  102.3 3.3 %shard_map.240 = (f32[128,768]{1,0:T(8,128)}, bf16[128,768]{1,0:T(8,128)(2,1)}) custom-call(s32[3]{0:T(128)} %pad_add_fusion.meta, bf16[2,64,192]{2,1,0:T(8,128)(2,1)} %get-tuple-element.124.refs_0_.refs_10_, bf16[2,64,192]{2,1,0:T(8,128)(2,1)} %copy-done.33, bf16[2,64,192]{2,1,0:T(8,128)(2,1)} %copy-done.34, bf16[2,64,192]{2,1,0:T(8,128)(2,1)} %copy-done.35, ...), custom_call_target="tpu_custom_call" | custom-call | bytes 1048576 | tf_op jit(solution)/shard_map/pallas_call | solution.py:541
  105.6 2.4 collective-permute-start.21
  109.0 5.1 %all-gather.9.cloned.1.call-done = bf16[768,768]{1,0:T(8,128)(2,1)} async-done(((bf16[192,768]{1,0:T(8,128)(2,1)}), bf16[768,768]{1,0:T(8,128)(2,1)}) %all-gather.9.cloned.1.call-update) | async-done | bytes 1179664 | tf_op jit(solution)/shard_map/all_gather | solution.py:693
  120.3 1.8 convert_reduce_fusion
  124.0 2.3 convolution_convert_fusion.1
  128.2 2.4 collective-permute-start.29
  132.5 3.3 %shard_map.241 = bf16[8,128,768]{2,1,0:T(8,128)(2,1)} custom-call(s32[8]{0:T(128)} %fusion.47.table, bf16[8,128,768]{2,1,0:T(8,128)(2,1)} %bitcast.141), custom_call_target="tpu_custom_call" | custom-call | tf_op jit(solution)/shard_map/pallas_call | solution.py:70
  137.0 3.4 %collective-permute-done.28.refs_2_ = bf16[128,768]{1,0:T(8,128)(2,1)S(1)} collective-permute-done((bf16[128,768]{1,0:T(8,128)(2,1)S(1)}, bf16[128,768]{1,0:T(8,128)(2,1)S(1)}, u32[]{:S(2)}, u32[]{:S(2)}) %collective-permute-start.28) | collective-permute-done | bytes 196640 | tf_op jit(solution)/shard_map/ppermute | solution.py:21
  141.1 4.1 %shard_map.242 = (bf16[2,64,192]{2,1,0:T(8,128)(2,1)}, bf16[2,64,192]{2,1,0:T(8,128)(2,1)}, bf16[2,64,192]{2,1,0:T(8,128)(2,1)}, bf16[2,64,192]{2,1,0:T(8,128)(2...) custom-call(s32[3]{0:T(128)} %pad_add_fusion.meta, ...), custom_call_target="tpu_custom_call" | custom-call | bytes 1048576 | tf_op jit(solution)/shard_map/pallas_call | solution.py:541
  145.2 6.4 %collective-permute-start.30 = (bf16[1,128,768]{2,1,0:T(8,128)(2,1)}, bf16[1,128,768]{2,1,0:T(8,128)(2,1)S(1)}, u32[]{:S(2)}, u32[]{:S(2)}) collective-permute-start(bf16[1,128,768]{2,1,0:T(8,128)(2,1)} %bitcast.156), channel_id=1, source_target_pairs={{0,1},{1,0},{2,3},{3,2},{4,5},{5,4},{6,7},{7,6},{8,9},{9,8},{10,11... | collective-permute-start | bytes 589832 | tf_op jit(solution)/shard_map/ppermute | solution.py:21
  151.7 4.3 %collective-permute-start.33 = (bf16[2,64,192]{2,1,0:T(8,128)(2,1)}, bf16[2,64,192]{2,1,0:T(8,128)(2,1)S(1)}, u32[]{:S(2)}, u32[]{:S(2)}) collective-permute-start(bf16[2,64,192]{2,1,0:T(8,128)(2,1)} %get-tuple-element.149), channel_id=1, source_target_pairs={{0,3},{1,2},{2,1},{3,0},{4,7},{5,6},{6,5},{7,4},{8,11},{9,10},{10,... | collective-permute-start | bytes 147464 | tf_op jit(solution)/shard_map/ppermute | solution.py:21
  156.0 3.6 %collective-permute-done.30 = bf16[1,128,768]{2,1,0:T(8,128)(2,1)S(1)} collective-permute-done((bf16[1,128,768]{2,1,0:T(8,128)(2,1)}, bf16[1,128,768]{2,1,0:T(8,128)(2,1)S(1)}, u32[]{:S(2)}, u32[]{:S(2)}) %collective-permute-start.30) | collective-permute-done | bytes 196640 | tf_op jit(solution)/shard_map/ppermute | solution.py:21
  161.1 2.0 collective-permute-start.34
  163.1 16.2 %shard_map.243 = (bf16[2,256,192]{2,1,0:T(8,128)(2,1)}, bf16[4,2,384,256]{3,2,1,0:T(8,128)(2,1)}, bf16[4,2,384,256]{3,2,1,0:T(8,128)(2,1)}) custom-call(s32[19]{0:T(128)} %pad_add_fusion.1.meta, bf16[2,256,256]{2,1,0:T(8,128)(2,1)} %get-tuple-element.114.refs_0_, bf16[2,256,384]{2,1,0:T(8,128)(2,1)} %get-tuple-element.116.refs_1_, ...), custom_call_target="tpu_custom_call" | custom-call | flops 9663676416 | bytes 1048576 | tf_op jit(solution)/shard_map/pallas_call | solution.py:541
  180.5 3.6 %collective-permute-done.35 = bf16[4,2,384,256]{3,2,1,0:T(8,128)(2,1)S(1)} collective-permute-done((bf16[4,2,384,256]{3,2,1,0:T(8,128)(2,1)}, bf16[4,2,384,256]{3,2,1,0:T(8,128)(2,1)S(1)}, u32[]{:S(2)}, u32[]{:S(2)}) %collective-permute-start.35) | collective-permute-done | bytes 1572896 | tf_op jit(solution)/shard_map/ppermute | solution.py:21
  185.5 2.2 collective-permute-start.38
  189.4 9.2 %collective-permute-done.38.refs_3_ = bf16[2,384,256]{2,1,0:T(8,128)(2,1)S(1)} collective-permute-done((bf16[2,384,256]{2,1,0:T(8,128)(2,1)}, bf16[2,384,256]{2,1,0:T(8,128)(2,1)S(1)}, u32[]{:S(2)}, u32[]{:S(2)}) %collective-permute-start.38) | collective-permute-done | bytes 393248 | tf_op jit(solution)/shard_map/ppermute | solution.py:21
  198.6 7.6 %collective-permute-done.37.refs_2_ = bf16[2,384,256]{2,1,0:T(8,128)(2,1)S(1)} collective-permute-done((bf16[2,384,256]{2,1,0:T(8,128)(2,1)S(1)}, bf16[2,384,256]{2,1,0:T(8,128)(2,1)S(1)}, u32[]{:S(2)}, u32[]{:S(2)}) %collective-permute-start.37) | collective-permute-done | bytes 393248 | tf_op jit(solution)/shard_map/ppermute | solution.py:21
  207.0 6.7 %shard_map.244 = (bf16[2,64,768]{2,1,0:T(8,128)(2,1)}, bf16[2,64,768]{2,1,0:T(8,128)(2,1)}, bf16[2,2,64,768]{3,2,1,0:T(8,128)(2,1)}, bf16[4,5,32,576]{3,2,1,0:T(8,128)(2,1)}, bf16[4,5,32,576]{3,2,1,0:T(8,128)(2,1)}) custom-call(s32[3]{0:T(128)} %pad_add_fusion.meta, bf16[2,384,256]{2,1,0:T(8,128)(2,1)} %get-tuple-element.161.refs_0_, ...), custom_call_target="tpu_custom_call" | custom-call | bytes 1048576 | tf_op jit(solution)/shard_map/pallas_call | solution.py:541
  217.9 2.3 collective-permute-start.43
  222.1 14.3 %collective-permute-done.39 = bf16[2,2,64,768]{3,2,1,0:T(8,128)(2,1)S(1)} collective-permute-done((bf16[2,2,64,768]{3,2,1,0:T(8,128)(2,1)}, bf16[2,2,64,768]{3,2,1,0:T(8,128)(2,1)S(1)}, u32[]{:S(2)}, u32[]{:S(2)}) %collective-permute-start.39) | collective-permute-done | bytes 393248 | tf_op jit(solution)/shard_map/ppermute | solution.py:21
  237.2 1.7 collective-permute-start.47
  238.9 2.7 collective-permute-start.45
  245.1 2.3 shard_map.246
  247.4 2.1 collective-permute-start.50
  252.3 1.6 fusion.51
  253.9 4.4 %fusion.49 = (f32[8,1,96,768]{3,2,1,0:T(8,128)}, f32[8,1,96,768]{3,2,1,0:T(8,128)}) fusion(bf16[8,2,96,768]{3,2,1,0:T(8,128)(2,1)} %bitcast.126), kind=kLoop, calls=%fused_computation.148 | loop fusion | bytes 9437184 | tf_op jit(solution)/shard_map/slice | solution.py:834
  260.2 2.9 %shard_map.245 = f32[128,768]{1,0:T(8,128)} custom-call(s32[3]{0:T(128)} %pad_add_fusion.meta, bf16[2,64,768]{2,1,0:T(8,128)(2,1)} %fusion.11.grad_ref, bf16[128,768]{1,0:T(8,128)(2,1)} %bitcast.134, f32[1,768]{1,0:T(1,128)} %reshape.206.gain_ref, f32[128,768]{1,0:T(8,128)} %get-tuple-element.176.resid_grad_ref), custom_call_target="tpu_custom_call" | custom-call | bytes 1048576 | tf_op jit(solution)/shard_map/pallas_call | solution.py:541
  264.5 3.5 %shard_map.247 = (f32[192,2304]{1,0:T(8,128)}, f32[192,768]{1,0:T(8,128)}) custom-call(s32[3]{0:T(128)} %pad_add_fusion.meta, bf16[24,3072]{1,0:T(8,128)(2,1)} %get-tuple-element.191.refs_0_, bf16[24,3072]{1,0:T(8,128)(2,1)} %copy-done.28, bf16[24,3072]{1,0:T(8,128)(2,1)} %copy-done.27, bf16[24,3072]{1,0:T(8,128)(2,1)} %copy-done.26, ...), custom_call_target="tpu_custom_call" | custom-call | bytes 1048576 | tf_op jit(solution)/shard_map/pallas_call | solution.py:541
  (292 shorter events, 56.1 us)
Async XLA Ops:
  7.2 47.7 %all-gather.7.cloned.1.call-start = ((), (), s32[]{:S(2)}) async-start(), calls=%async_computation.3 | async-start | bytes 1769472 | tf_op jit(solution)/shard_map/all_gather | solution.py:665
  7.9 83.5 %all-gather.5.cloned.1.call-start = ((), (), s32[]{:S(2)}) async-start(), calls=%async_computation.2 | async-start | bytes 1597440 | tf_op jit(solution)/shard_map/all_gather | solution.py:673
  9.9 5.7 %collective-permute-start = (bf16[64,576]{1,0:T(8,128)(2,1)S(1)}, bf16[64,576]{1,0:T(8,128)(2,1)S(1)}, u32[]{:S(2)}, u32[]{:S(2)}) collective-permute-start(bf16[64,576]{1,0:T(8,128)(2,1)S(1)} %get-tuple-element.226), channel_id=1, source_target_pairs={{0,1},{1,0},{2,3},{3,2},{4,5},{5,4},{6,7},{7,6},{8,9},{9,8},{10,11... | collective-permute-start | bytes 221192 | tf_op jit(solution)/shard_map/ppermute | solution.py:21
  13.0 9.2 %collective-permute-start.1 = (bf16[64,576]{1,0:T(8,128)(2,1)S(1)}, bf16[64,576]{1,0:T(8,128)(2,1)S(1)}, u32[]{:S(2)}, u32[]{:S(2)}) collective-permute-start(bf16[64,576]{1,0:T(8,128)(2,1)S(1)} %get-tuple-element.227), channel_id=1, source_target_pairs={{0,2},{1,3},{2,0},{3,1},{4,6},{5,7},{6,4},{7,5},{8,10},{9,11},{10,... | collective-permute-start | bytes 221192 | tf_op jit(solution)/shard_map/ppermute | solution.py:21
  15.6 6.6 %collective-permute-start.2 = (bf16[64,576]{1,0:T(8,128)(2,1)S(1)}, bf16[64,576]{1,0:T(8,128)(2,1)S(1)}, u32[]{:S(2)}, u32[]{:S(2)}) collective-permute-start(bf16[64,576]{1,0:T(8,128)(2,1)S(1)} %get-tuple-element.228), channel_id=1, source_target_pairs={{0,3},{1,2},{2,1},{3,0},{4,7},{5,6},{6,5},{7,4},{8,11},{9,10},{10,... | collective-permute-start | bytes 221192 | tf_op jit(solution)/shard_map/ppermute | solution.py:21
  22.3 9.6 %collective-permute-start.5 = (bf16[2,64,768]{2,1,0:T(8,128)(2,1)S(1)}, bf16[2,64,768]{2,1,0:T(8,128)(2,1)S(1)}, u32[]{:S(2)}, u32[]{:S(2)}) collective-permute-start(bf16[2,64,768]{2,1,0:T(8,128)(2,1)S(1)} %bitcast.135), channel_id=1, source_target_pairs={{0,3},{1,2},{2,1},{3,0},{4,7},{5,6},{6,5},{7,4},{8,11},{9,10},{10,... | collective-permute-start | bytes 589832 | tf_op jit(solution)/shard_map/ppermute | solution.py:21
  25.0 16.5 %collective-permute-start.4 = (bf16[2,64,768]{2,1,0:T(8,128)(2,1)S(1)}, bf16[2,64,768]{2,1,0:T(8,128)(2,1)S(1)}, u32[]{:S(2)}, u32[]{:S(2)}) collective-permute-start(bf16[2,64,768]{2,1,0:T(8,128)(2,1)S(1)} %bitcast.136), channel_id=1, source_target_pairs={{0,2},{1,3},{2,0},{3,1},{4,6},{5,7},{6,4},{7,5},{8,10},{9,11},{10,... | collective-permute-start | bytes 589832 | tf_op jit(solution)/shard_map/ppermute | solution.py:21
  25.5 16.0 %collective-permute-start.3 = (bf16[2,64,768]{2,1,0:T(8,128)(2,1)S(1)}, bf16[2,64,768]{2,1,0:T(8,128)(2,1)S(1)}, u32[]{:S(2)}, u32[]{:S(2)}) collective-permute-start(bf16[2,64,768]{2,1,0:T(8,128)(2,1)S(1)} %bitcast.137), channel_id=1, source_target_pairs={{0,1},{1,0},{2,3},{3,2},{4,5},{5,4},{6,7},{7,6},{8,9},{9,8},{10,11... | collective-permute-start | bytes 589832 | tf_op jit(solution)/shard_map/ppermute | solution.py:21
  27.0 14.5 %collective-permute-start.8 = (bf16[4,48,576]{2,1,0:T(8,128)(2,1)S(1)}, bf16[4,48,576]{2,1,0:T(8,128)(2,1)S(1)}, u32[]{:S(2)}, u32[]{:S(2)}) collective-permute-start(bf16[4,48,576]{2,1,0:T(8,128)(2,1)S(1)} %slice.254.refs_5_), channel_id=1, source_target_pairs={{0,24},{4,28},{8,16},{12,20},{16,8},{20,12},{24,0},{28,4},{1,25},{... | collective-permute-start | bytes 663560 | tf_op jit(solution)/shard_map/ppermute | solution.py:21
  29.4 12.8 %collective-permute-start.7 = (bf16[4,48,576]{2,1,0:T(8,128)(2,1)S(1)}, bf16[4,48,576]{2,1,0:T(8,128)(2,1)S(1)}, u32[]{:S(2)}, u32[]{:S(2)}) collective-permute-start(bf16[4,48,576]{2,1,0:T(8,128)(2,1)S(1)} %slice.254.refs_5_), channel_id=1, source_target_pairs={{0,16},{4,20},{8,24},{12,28},{16,0},{20,4},{24,8},{28,12},{1,17},{... | collective-permute-start | bytes 663560 | tf_op jit(solution)/shard_map/ppermute | solution.py:21
  31.9 10.5 %collective-permute-start.6 = (bf16[4,48,576]{2,1,0:T(8,128)(2,1)S(1)}, bf16[4,48,576]{2,1,0:T(8,128)(2,1)S(1)}, u32[]{:S(2)}, u32[]{:S(2)}) collective-permute-start(bf16[4,48,576]{2,1,0:T(8,128)(2,1)S(1)} %slice.254.refs_5_), channel_id=1, source_target_pairs={{0,8},{4,12},{8,0},{12,4},{16,24},{20,28},{24,16},{28,20},{1,9},{5... | collective-permute-start | bytes 663560 | tf_op jit(solution)/shard_map/ppermute | solution.py:21
  42.4 71.7 %all-gather.9.cloned.1.call-start = ((), (), s32[]{:S(2)}) async-start(), calls=%async_computation.4 | async-start | bytes 1474560 | tf_op jit(solution)/shard_map/all_gather | solution.py:693
  48.7 13.2 %collective-permute-start.11 = (bf16[2,256,384]{2,1,0:T(8,128)(2,1)}, bf16[2,256,384]{2,1,0:T(8,128)(2,1)S(1)}, u32[]{:S(2)}, u32[]{:S(2)}) collective-permute-start(bf16[2,256,384]{2,1,0:T(8,128)(2,1)} %get-tuple-element.116.refs_1_), channel_id=1, source_target_pairs={{0,24},{4,28},{8,16},{12,20},{16,8},{20,12},{24,0},{28,4},{1,25},{... | collective-permute-start | bytes 1179656 | tf_op jit(solution)/shard_map/ppermute | solution.py:21
  50.5 18.1 %collective-permute-start.10 = (bf16[2,256,384]{2,1,0:T(8,128)(2,1)}, bf16[2,256,384]{2,1,0:T(8,128)(2,1)S(1)}, u32[]{:S(2)}, u32[]{:S(2)}) collective-permute-start(bf16[2,256,384]{2,1,0:T(8,128)(2,1)} %get-tuple-element.116.refs_1_), channel_id=1, source_target_pairs={{0,16},{4,20},{8,24},{12,28},{16,0},{20,4},{24,8},{28,12},{1,17},{... | collective-permute-start | bytes 1179656 | tf_op jit(solution)/shard_map/ppermute | solution.py:21
  51.7 17.0 %collective-permute-start.9 = (bf16[2,256,384]{2,1,0:T(8,128)(2,1)}, bf16[2,256,384]{2,1,0:T(8,128)(2,1)S(1)}, u32[]{:S(2)}, u32[]{:S(2)}) collective-permute-start(bf16[2,256,384]{2,1,0:T(8,128)(2,1)} %get-tuple-element.116.refs_1_), channel_id=1, source_target_pairs={{0,8},{4,12},{8,0},{12,4},{16,24},{20,28},{24,16},{28,20},{1,9},{5... | collective-permute-start | bytes 1179656 | tf_op jit(solution)/shard_map/ppermute | solution.py:21
  69.9 119.5 %reduce-scatter.3.cloned.1.call-start = ((), (), s32[]{:S(2)}) async-start(), calls=%async_computation.5 | async-start | bytes 1769472 | tf_op jit(solution)/shard_map/reduce_scatter | solution.py:738
  85.6 10.7 %collective-permute-start.16 = (bf16[2,64,192]{2,1,0:T(8,128)(2,1)}, bf16[2,64,192]{2,1,0:T(8,128)(2,1)S(1)}, u32[]{:S(2)}, u32[]{:S(2)}) collective-permute-start(bf16[2,64,192]{2,1,0:T(8,128)(2,1)} %get-tuple-element.121.refs_11_), channel_id=1, source_target_pairs={{0,1},{1,0},{2,3},{3,2},{4,5},{5,4},{6,7},{7,6},{8,9},{9,8},{10,11... | collective-permute-start | bytes 147464 | tf_op jit(solution)/shard_map/ppermute | solution.py:21
  88.9 12.6 %collective-permute-start.17 = (bf16[2,64,192]{2,1,0:T(8,128)(2,1)}, bf16[2,64,192]{2,1,0:T(8,128)(2,1)S(1)}, u32[]{:S(2)}, u32[]{:S(2)}) collective-permute-start(bf16[2,64,192]{2,1,0:T(8,128)(2,1)} %get-tuple-element.122.refs_12_), channel_id=1, source_target_pairs={{0,2},{1,3},{2,0},{3,1},{4,6},{5,7},{6,4},{7,5},{8,10},{9,11},{10,... | collective-permute-start | bytes 147464 | tf_op jit(solution)/shard_map/ppermute | solution.py:21
  88.9 12.6 %collective-permute-start.18 = (bf16[2,64,192]{2,1,0:T(8,128)(2,1)}, bf16[2,64,192]{2,1,0:T(8,128)(2,1)S(1)}, u32[]{:S(2)}, u32[]{:S(2)}) collective-permute-start(bf16[2,64,192]{2,1,0:T(8,128)(2,1)} %get-tuple-element.123.refs_13_), channel_id=1, source_target_pairs={{0,3},{1,2},{2,1},{3,0},{4,7},{5,6},{6,5},{7,4},{8,11},{9,10},{10,... | collective-permute-start | bytes 147464 | tf_op jit(solution)/shard_map/ppermute | solution.py:21
  105.6 10.9 %collective-permute-start.21 = (bf16[128,768]{1,0:T(8,128)(2,1)}, bf16[128,768]{1,0:T(8,128)(2,1)S(1)}, u32[]{:S(2)}, u32[]{:S(2)}) collective-permute-start(bf16[128,768]{1,0:T(8,128)(2,1)} %get-tuple-element.133), channel_id=1, source_target_pairs={{0,24},{4,28},{8,16},{12,20},{16,8},{20,12},{24,0},{28,4},{1,25},{... | collective-permute-start | bytes 589832 | tf_op jit(solution)/shard_map/ppermute | solution.py:21
  108.0 8.4 %collective-permute-start.20 = (bf16[128,768]{1,0:T(8,128)(2,1)}, bf16[128,768]{1,0:T(8,128)(2,1)S(1)}, u32[]{:S(2)}, u32[]{:S(2)}) collective-permute-start(bf16[128,768]{1,0:T(8,128)(2,1)} %get-tuple-element.133), channel_id=1, source_target_pairs={{0,16},{4,20},{8,24},{12,28},{16,0},{20,4},{24,8},{28,12},{1,17},{... | collective-permute-start | bytes 589832 | tf_op jit(solution)/shard_map/ppermute | solution.py:21
  108.5 8.0 %collective-permute-start.19 = (bf16[128,768]{1,0:T(8,128)(2,1)}, bf16[128,768]{1,0:T(8,128)(2,1)S(1)}, u32[]{:S(2)}, u32[]{:S(2)}) collective-permute-start(bf16[128,768]{1,0:T(8,128)(2,1)} %get-tuple-element.133), channel_id=1, source_target_pairs={{0,8},{4,12},{8,0},{12,4},{16,24},{20,28},{24,16},{28,20},{1,9},{5... | collective-permute-start | bytes 589832 | tf_op jit(solution)/shard_map/ppermute | solution.py:21
  128.2 8.8 %collective-permute-start.29 = (bf16[128,768]{1,0:T(8,128)(2,1)S(1)}, bf16[128,768]{1,0:T(8,128)(2,1)S(1)}, u32[]{:S(2)}, u32[]{:S(2)}) collective-permute-start(bf16[128,768]{1,0:T(8,128)(2,1)S(1)} %get-tuple-element.215), channel_id=1, source_target_pairs={{0,24},{4,28},{8,16},{12,20},{16,8},{20,12},{24,0},{28,4},{1,25},{... | collective-permute-start | bytes 589832 | tf_op jit(solution)/shard_map/ppermute | solution.py:21
  130.6 9.8 %collective-permute-start.28 = (bf16[128,768]{1,0:T(8,128)(2,1)S(1)}, bf16[128,768]{1,0:T(8,128)(2,1)S(1)}, u32[]{:S(2)}, u32[]{:S(2)}) collective-permute-start(bf16[128,768]{1,0:T(8,128)(2,1)S(1)} %get-tuple-element.216), channel_id=1, source_target_pairs={{0,16},{4,20},{8,24},{12,28},{16,0},{20,4},{24,8},{28,12},{1,17},{... | collective-permute-start | bytes 589832 | tf_op jit(solution)/shard_map/ppermute | solution.py:21
  131.1 9.3 %collective-permute-start.27 = (bf16[128,768]{1,0:T(8,128)(2,1)S(1)}, bf16[128,768]{1,0:T(8,128)(2,1)S(1)}, u32[]{:S(2)}, u32[]{:S(2)}) collective-permute-start(bf16[128,768]{1,0:T(8,128)(2,1)S(1)} %get-tuple-element.217), channel_id=1, source_target_pairs={{0,8},{4,12},{8,0},{12,4},{16,24},{20,28},{24,16},{28,20},{1,9},{5... | collective-permute-start | bytes 589832 | tf_op jit(solution)/shard_map/ppermute | solution.py:21
  140.4 73.3 %reduce-scatter.5.cloned.1.call-start = ((), (), s32[]{:S(2)}) async-start(), calls=%async_computation.6 | async-start | bytes 1474560 | tf_op jit(solution)/shard_map/reduce_scatter | solution.py:767
  145.2 14.4 %collective-permute-start.30 = (bf16[1,128,768]{2,1,0:T(8,128)(2,1)}, bf16[1,128,768]{2,1,0:T(8,128)(2,1)S(1)}, u32[]{:S(2)}, u32[]{:S(2)}) collective-permute-start(bf16[1,128,768]{2,1,0:T(8,128)(2,1)} %bitcast.156), channel_id=1, source_target_pairs={{0,1},{1,0},{2,3},{3,2},{4,5},{5,4},{6,7},{7,6},{8,9},{9,8},{10,11... | collective-permute-start | bytes 589832 | tf_op jit(solution)/shard_map/ppermute | solution.py:21
  151.6 9.5 %collective-permute-start.31 = (bf16[2,64,192]{2,1,0:T(8,128)(2,1)}, bf16[2,64,192]{2,1,0:T(8,128)(2,1)S(1)}, u32[]{:S(2)}, u32[]{:S(2)}) collective-permute-start(bf16[2,64,192]{2,1,0:T(8,128)(2,1)} %get-tuple-element.147), channel_id=1, source_target_pairs={{0,1},{1,0},{2,3},{3,2},{4,5},{5,4},{6,7},{7,6},{8,9},{9,8},{10,11... | collective-permute-start | bytes 147464 | tf_op jit(solution)/shard_map/ppermute | solution.py:21
  151.7 9.4 %collective-permute-start.32 = (bf16[2,64,192]{2,1,0:T(8,128)(2,1)}, bf16[2,64,192]{2,1,0:T(8,128)(2,1)S(1)}, u32[]{:S(2)}, u32[]{:S(2)}) collective-permute-start(bf16[2,64,192]{2,1,0:T(8,128)(2,1)} %get-tuple-element.148), channel_id=1, source_target_pairs={{0,2},{1,3},{2,0},{3,1},{4,6},{5,7},{6,4},{7,5},{8,10},{9,11},{10,... | collective-permute-start | bytes 147464 | tf_op jit(solution)/shard_map/ppermute | solution.py:21
  151.7 9.4 %collective-permute-start.33 = (bf16[2,64,192]{2,1,0:T(8,128)(2,1)}, bf16[2,64,192]{2,1,0:T(8,128)(2,1)S(1)}, u32[]{:S(2)}, u32[]{:S(2)}) collective-permute-start(bf16[2,64,192]{2,1,0:T(8,128)(2,1)} %get-tuple-element.149), channel_id=1, source_target_pairs={{0,3},{1,2},{2,1},{3,0},{4,7},{5,6},{6,5},{7,4},{8,11},{9,10},{10,... | collective-permute-start | bytes 147464 | tf_op jit(solution)/shard_map/ppermute | solution.py:21
  161.1 19.2 %collective-permute-start.34 = (bf16[2,128,768]{2,1,0:T(8,128)(2,1)S(1)}, bf16[2,128,768]{2,1,0:T(8,128)(2,1)S(1)}, u32[]{:S(2)}, u32[]{:S(2)}) collective-permute-start(bf16[2,128,768]{2,1,0:T(8,128)(2,1)S(1)} %pad_maximum_fusion.1), channel_id=1, source_target_pairs={{0,2},{1,3},{2,0},{3,1},{4,6},{5,7},{6,4},{7,5},{8,10},{9,11},{10,... | collective-permute-start | bytes 1179656 | tf_op jit(solution)/shard_map/ppermute | solution.py:21
  180.4 73.5 %all-gather.11.cloned.1.call-start = ((), (), s32[]{:S(2)}) async-start(), calls=%async_computation.7 | async-start | bytes 2654208 | tf_op jit(solution)/shard_map/all_gather | solution.py:793
  185.5 13.1 %collective-permute-start.38 = (bf16[2,384,256]{2,1,0:T(8,128)(2,1)}, bf16[2,384,256]{2,1,0:T(8,128)(2,1)S(1)}, u32[]{:S(2)}, u32[]{:S(2)}) collective-permute-start(bf16[2,384,256]{2,1,0:T(8,128)(2,1)} %get-tuple-element.209), channel_id=1, source_target_pairs={{0,24},{4,28},{8,16},{12,20},{16,8},{20,12},{24,0},{28,4},{1,25},{... | collective-permute-start | bytes 1179656 | tf_op jit(solution)/shard_map/ppermute | solution.py:21
  187.7 18.5 %collective-permute-start.37 = (bf16[2,384,256]{2,1,0:T(8,128)(2,1)S(1)}, bf16[2,384,256]{2,1,0:T(8,128)(2,1)S(1)}, u32[]{:S(2)}, u32[]{:S(2)}) collective-permute-start(bf16[2,384,256]{2,1,0:T(8,128)(2,1)S(1)} %get-tuple-element.210), channel_id=1, source_target_pairs={{0,16},{4,20},{8,24},{12,28},{16,0},{20,4},{24,8},{28,12},{1,17},{... | collective-permute-start | bytes 1179656 | tf_op jit(solution)/shard_map/ppermute | solution.py:21
  189.1 17.1 %collective-permute-start.36 = (bf16[2,384,256]{2,1,0:T(8,128)(2,1)S(1)}, bf16[2,384,256]{2,1,0:T(8,128)(2,1)S(1)}, u32[]{:S(2)}, u32[]{:S(2)}) collective-permute-start(bf16[2,384,256]{2,1,0:T(8,128)(2,1)S(1)} %get-tuple-element.211), channel_id=1, source_target_pairs={{0,8},{4,12},{8,0},{12,4},{16,24},{20,28},{24,16},{28,20},{1,9},{5... | collective-permute-start | bytes 1179656 | tf_op jit(solution)/shard_map/ppermute | solution.py:21
  215.5 21.0 %collective-permute-start.39 = (bf16[2,2,64,768]{3,2,1,0:T(8,128)(2,1)}, bf16[2,2,64,768]{3,2,1,0:T(8,128)(2,1)S(1)}, u32[]{:S(2)}, u32[]{:S(2)}) collective-permute-start(bf16[2,2,64,768]{3,2,1,0:T(8,128)(2,1)} %get-tuple-element.171), channel_id=1, source_target_pairs={{0,2},{1,3},{2,0},{3,1},{4,6},{5,7},{6,4},{7,5},{8,10},{9,11},{10,... | collective-permute-start | bytes 1179656 | tf_op jit(solution)/shard_map/ppermute | solution.py:21
  217.9 18.6 %collective-permute-start.43 = (bf16[5,32,576]{2,1,0:T(8,128)(2,1)S(1)}, bf16[5,32,576]{2,1,0:T(8,128)(2,1)S(1)}, u32[]{:S(2)}, u32[]{:S(2)}) collective-permute-start(bf16[5,32,576]{2,1,0:T(8,128)(2,1)S(1)} %get-tuple-element.219), channel_id=1, source_target_pairs={{0,24},{4,28},{8,16},{12,20},{16,8},{20,12},{24,0},{28,4},{1,25},{... | collective-permute-start | bytes 552968 | tf_op jit(solution)/shard_map/ppermute | solution.py:21
  220.1 16.3 %collective-permute-start.42 = (bf16[5,32,576]{2,1,0:T(8,128)(2,1)S(1)}, bf16[5,32,576]{2,1,0:T(8,128)(2,1)S(1)}, u32[]{:S(2)}, u32[]{:S(2)}) collective-permute-start(bf16[5,32,576]{2,1,0:T(8,128)(2,1)S(1)} %get-tuple-element.220), channel_id=1, source_target_pairs={{0,16},{4,20},{8,24},{12,28},{16,0},{20,4},{24,8},{28,12},{1,17},{... | collective-permute-start | bytes 552968 | tf_op jit(solution)/shard_map/ppermute | solution.py:21
  220.9 15.6 %collective-permute-start.41 = (bf16[5,32,576]{2,1,0:T(8,128)(2,1)S(1)}, bf16[5,32,576]{2,1,0:T(8,128)(2,1)S(1)}, u32[]{:S(2)}, u32[]{:S(2)}) collective-permute-start(bf16[5,32,576]{2,1,0:T(8,128)(2,1)S(1)} %get-tuple-element.221), channel_id=1, source_target_pairs={{0,8},{4,12},{8,0},{12,4},{16,24},{20,28},{24,16},{28,20},{1,9},{5... | collective-permute-start | bytes 552968 | tf_op jit(solution)/shard_map/ppermute | solution.py:21
  237.2 5.9 %collective-permute-start.47 = (bf16[32,576]{1,0:T(8,128)(2,1)S(1)}, bf16[32,576]{1,0:T(8,128)(2,1)S(1)}, u32[]{:S(2)}, u32[]{:S(2)}) collective-permute-start(bf16[32,576]{1,0:T(8,128)(2,1)S(1)} %get-tuple-element.233), channel_id=1, source_target_pairs={{0,3},{1,2},{2,1},{3,0},{4,7},{5,6},{6,5},{7,4},{8,11},{9,10},{10,... | collective-permute-start | bytes 110600 | tf_op jit(solution)/shard_map/ppermute | solution.py:21
  238.9 5.1 %collective-permute-start.46 = (bf16[32,576]{1,0:T(8,128)(2,1)S(1)}, bf16[32,576]{1,0:T(8,128)(2,1)S(1)}, u32[]{:S(2)}, u32[]{:S(2)}) collective-permute-start(bf16[32,576]{1,0:T(8,128)(2,1)S(1)} %get-tuple-element.234), channel_id=1, source_target_pairs={{0,2},{1,3},{2,0},{3,1},{4,6},{5,7},{6,4},{7,5},{8,10},{9,11},{10,... | collective-permute-start | bytes 110600 | tf_op jit(solution)/shard_map/ppermute | solution.py:21
  238.9 5.5 %collective-permute-start.45 = (bf16[32,576]{1,0:T(8,128)(2,1)S(1)}, bf16[32,576]{1,0:T(8,128)(2,1)S(1)}, u32[]{:S(2)}, u32[]{:S(2)}) collective-permute-start(bf16[32,576]{1,0:T(8,128)(2,1)S(1)} %get-tuple-element.235), channel_id=1, source_target_pairs={{0,1},{1,0},{2,3},{3,2},{4,5},{5,4},{6,7},{7,6},{8,9},{9,8},{10,11... | collective-permute-start | bytes 110600 | tf_op jit(solution)/shard_map/ppermute | solution.py:21
  241.7 17.7 %collective-permute-start.44 = (bf16[1,2,64,768]{3,2,1,0:T(8,128)(2,1)S(1)}, bf16[1,2,64,768]{3,2,1,0:T(8,128)(2,1)S(1)}, u32[]{:S(2)}, u32[]{:S(2)}) collective-permute-start(bf16[1,2,64,768]{3,2,1,0:T(8,128)(2,1)S(1)} %fusion.22), channel_id=1, source_target_pairs={{0,1},{1,0},{2,3},{3,2},{4,5},{5,4},{6,7},{7,6},{8,9},{9,8},{10,11... | collective-permute-start | bytes 589832 | tf_op jit(solution)/shard_map/ppermute | solution.py:21
  247.4 10.9 %collective-permute-start.50 = (bf16[24,3072]{1,0:T(8,128)(2,1)}, bf16[24,3072]{1,0:T(8,128)(2,1)S(1)}, u32[]{:S(2)}, u32[]{:S(2)}) collective-permute-start(bf16[24,3072]{1,0:T(8,128)(2,1)} %get-tuple-element.191.refs_0_), channel_id=1, source_target_pairs={{0,24},{4,28},{8,16},{12,20},{16,8},{20,12},{24,0},{28,4},{1,25},{... | collective-permute-start | bytes 442376 | tf_op jit(solution)/shard_map/ppermute | solution.py:21
  249.6 8.7 %collective-permute-start.49 = (bf16[24,3072]{1,0:T(8,128)(2,1)}, bf16[24,3072]{1,0:T(8,128)(2,1)S(1)}, u32[]{:S(2)}, u32[]{:S(2)}) collective-permute-start(bf16[24,3072]{1,0:T(8,128)(2,1)} %get-tuple-element.191.refs_0_), channel_id=1, source_target_pairs={{0,16},{4,20},{8,24},{12,28},{16,0},{20,4},{24,8},{28,12},{1,17},{... | collective-permute-start | bytes 442376 | tf_op jit(solution)/shard_map/ppermute | solution.py:21
  250.4 7.9 %collective-permute-start.48 = (bf16[24,3072]{1,0:T(8,128)(2,1)}, bf16[24,3072]{1,0:T(8,128)(2,1)S(1)}, u32[]{:S(2)}, u32[]{:S(2)}) collective-permute-start(bf16[24,3072]{1,0:T(8,128)(2,1)} %get-tuple-element.191.refs_0_), channel_id=1, source_target_pairs={{0,8},{4,12},{8,0},{12,4},{16,24},{20,28},{24,16},{28,20},{1,9},{5... | collective-permute-start | bytes 442376 | tf_op jit(solution)/shard_map/ppermute | solution.py:21
  258.3 4.8 %collective-permute-start.51 = (bf16[24,3072]{1,0:T(8,128)(2,1)S(1)}, bf16[24,3072]{1,0:T(8,128)(2,1)S(1)}, u32[]{:S(2)}, u32[]{:S(2)}) collective-permute-start(bf16[24,3072]{1,0:T(8,128)(2,1)S(1)} %copy-done.25), channel_id=1, source_target_pairs={{0,4},{4,0},{8,12},{12,8},{16,20},{20,16},{24,28},{28,24},{1,5},{5... | collective-permute-start | bytes 442376 | tf_op jit(solution)/shard_map/ppermute | solution.py:21
  258.4 4.7 %collective-permute-start.52 = (bf16[24,3072]{1,0:T(8,128)(2,1)S(1)}, bf16[24,3072]{1,0:T(8,128)(2,1)S(1)}, u32[]{:S(2)}, u32[]{:S(2)}) collective-permute-start(bf16[24,3072]{1,0:T(8,128)(2,1)S(1)} %collective-permute-done.48.refs_1_), channel_id=1, source_target_pairs={{0,4},{4,0},{8,12},{12,8},{16,20},{20,16},{24,28},{28,24},{1,5},{5... | collective-permute-start | bytes 442376 | tf_op jit(solution)/shard_map/ppermute | solution.py:21
  (71 other events, 402.7 us)
Sparse Core Ops, SparseCore 0:
  9.9 33.3 all-gather.6
  45.5 31.6 all-gather.4
  78.7 35.3 all-gather.8
  140.6 41.4 reduce-scatter.2
  184.3 29.1 reduce-scatter.4
  215.2 32.0 all-gather.10

commit v4 on v3

--- a/solution.py
+++ b/solution.py
@@ -126,18 +126,18 @@
     return copies
 
 
-def in_pairs(start, stop, step):
-    def both(i, carry):
-        step((start + 2 * i, start + 2 * i + 1))
-        return carry
-
-    def one(n, carry):
-        step((n,))
-        return carry
-
-    half = (stop - start) // 2
-    lax.fori_loop(0, half, both, 0)
-    lax.fori_loop(start + 2 * half, stop, one, 0)
+def in_groups(start, stop, step, widest=4):
+    many = widest
+    while many:
+
+        def some(i, carry, many=many, start=start):
+            step(tuple(start + many * i + k for k in range(many)))
+            return carry
+
+        steps = (stop - start) // many
+        lax.fori_loop(0, steps, some, 0)
+        start = start + many * steps
+        many //= 2
 
 
 def attend_kernel(meta, *refs, heads, pieces, groups, rows):
@@ -193,13 +193,13 @@
             if j == 0 and tile == 0:
                 for copy in copies[1:]:
                     copy.wait()
-            in_pairs(0, block, scores)
+            in_groups(0, block, scores)
             top_ref[...] = jnp.broadcast_to(
                 jnp.max(top_ref[...], axis=1, keepdims=True), top_ref.shape
             )
             total_ref[...] = jnp.zeros_like(total_ref)
             acc_ref[...] = jnp.zeros_like(acc_ref)
-            in_pairs(0, block + 1, weights)
+            in_groups(0, block + 1, weights)
             total = jnp.sum(total_ref[...], axis=1, keepdims=True)
             lse = jnp.broadcast_to(top_ref[:, :1] + jnp.log(total), top_ref.shape)
             result = acc_ref[...] / total
@@ -281,7 +281,7 @@
             dq_acc[...] = dq
 
         visit((block,), True)
-        in_pairs(0, block, visit)
+        in_groups(0, block, visit)
         mine = lax.broadcasted_iota(jnp.int32, (size, wide), 1)
         whole = sum(
             jnp.where(

time: 276 us -> 275 us (level)
  transfers between devices with their start and end apart: 61 -> 61, of which waited for: 32 -> 30; matrix products, arithmetic and copies ran while one was open for 13% -> 13% of each run, Pallas kernels for 22% -> 21%
where the time goes in v4:
time: 275 us; the launch traced here: 273 us
  waiting for transfers between devices  89.4 us (33%)
  starting transfers between devices  62.2 us (23%)
  Pallas kernels  62 us (23%)
  local copies, waits for them, and re-layouts  24.5 us (9%)
  between operations  15 us (5%)
  other arithmetic  12.6 us (5%)
  matrix products  7.93 us (3%)
    ppermute x55, waiting for transfers between devices, swap(): lax.ppermute(x, axis, [(i, i ^ mask) for i in range(lax.axis_size(axis))])  82 us
    ppermute x55, starting transfers between devices, swap(): lax.ppermute(x, axis, [(i, i ^ mask) for i in range(lax.axis_size(axis))])  61.7 us
    pallas_call x9, Pallas kernels, in_vmem(): pl.pallas_call(kernel, grid_spec=pltpu.PrefetchScalarGridSpec(num_scalar_...  55.2 us
    pallas_call x2, Pallas kernels, shuffle(): pl.pallas_call(shuffle_kernel, grid_spec=pltpu.PrefetchScalarGridSpec(num...  6.76 us
    all_gather x1, waiting for transfers between devices, per_device(): lax.all_gather(after(ffn_cut, *group_tokens), 'fsdp', axis=0, tiled=True)  6.51 us
    unnamed x125, local copies, waits for them, and re-layouts  5.78 us
  transfers between devices with their start and end apart: 61, of which 30 were waited for; matrix products, arithmetic and copies ran while one was open for 13% of the time, Pallas kernels for 21%

profile of v4, /device:TPU:0, one launch (start us, length us, event | category | flops | bytes accessed | tf_op | source)
XLA Modules:
  0.0 273.5 jit_solution(8212081804713890107)
XLA Ops:
  9.9 3.1 %collective-permute-start = (bf16[64,576]{1,0:T(8,128)(2,1)S(1)}, bf16[64,576]{1,0:T(8,128)(2,1)S(1)}, u32[]{:S(2)}, u32[]{:S(2)}) collective-permute-start(bf16[64,576]{1,0:T(8,128)(2,1)S(1)} %get-tuple-element.226), channel_id=1, source_target_pairs={{0,1},{1,0},{2,3},{3,2},{4,5},{5,4},{6,7},{7,6},{8,9},{9,8},{10,11... | collective-permute-start | bytes 221192 | tf_op jit(solution)/shard_map/ppermute | solution.py:21
  13.0 2.6 collective-permute-start.1
  15.6 6.6 %collective-permute-done.1 = bf16[64,576]{1,0:T(8,128)(2,1)S(1)} collective-permute-done((bf16[64,576]{1,0:T(8,128)(2,1)S(1)}, bf16[64,576]{1,0:T(8,128)(2,1)S(1)}, u32[]{:S(2)}, u32[]{:S(2)}) %collective-permute-start.1) | collective-permute-done | bytes 73760 | tf_op jit(solution)/shard_map/ppermute | solution.py:21
  22.3 2.5 collective-permute-start.5
  25.5 1.5 collective-permute-start.3
  27.0 2.4 collective-permute-start.8
  29.9 2.0 collective-permute-done.5.refs_3_
  31.9 1.5 collective-permute-start.6
  34.2 7.3 %collective-permute-done.4.refs_2_ = bf16[2,64,768]{2,1,0:T(8,128)(2,1)S(1)} collective-permute-done((bf16[2,64,768]{2,1,0:T(8,128)(2,1)S(1)}, bf16[2,64,768]{2,1,0:T(8,128)(2,1)S(1)}, u32[]{:S(2)}, u32[]{:S(2)}) %collective-permute-start.4) | collective-permute-done | bytes 196640 | tf_op jit(solution)/shard_map/ppermute | solution.py:21
  43.7 5.0 %shard_map.237 = (bf16[2,256,384]{2,1,0:T(8,128)(2,1)}, bf16[2,256,256]{2,1,0:T(8,128)(2,1)}, bf16[2,256,768]{2,1,0:T(8,128)(2,1)}, f32[2,256,768]{2,1,0:T(8,128)}, bf16[768,576]{1,0:T(8,128)(2,1)}) custom-call(s32[3]{0:T(128)} %pad_add_fusion.meta, bf16[2,64,768]{2,1,0:T(8,128)(2,1)} %bitcast.132, bf16[2,64,768]{2,1,0:T(8,128)(2,1)} %copy-done.24, ...), custom_call_target="tpu_custom_call" | custom-call | bytes 1048576 | tf_op jit(solution)/shard_map/pallas_call | solution.py:541
  48.7 1.8 collective-permute-start.11
  54.9 3.4 %shard_map.238 = bf16[8,128,768]{2,1,0:T(8,128)(2,1)} custom-call(s32[8]{0:T(128)} %add_xor_fusion.table, bf16[8,128,768]{2,1,0:T(8,128)(2,1)} %bitcast.138), custom_call_target="tpu_custom_call" | custom-call | tf_op jit(solution)/shard_map/pallas_call | solution.py:70
  58.3 3.6 %collective-permute-done.11.refs_4_ = bf16[2,256,384]{2,1,0:T(8,128)(2,1)S(1)} collective-permute-done((bf16[2,256,384]{2,1,0:T(8,128)(2,1)}, bf16[2,256,384]{2,1,0:T(8,128)(2,1)S(1)}, u32[]{:S(2)}, u32[]{:S(2)}) %collective-permute-start.11) | collective-permute-done | bytes 393248 | tf_op jit(solution)/shard_map/ppermute | solution.py:21
  61.9 6.7 %collective-permute-done.10.refs_3_ = bf16[2,256,384]{2,1,0:T(8,128)(2,1)S(1)} collective-permute-done((bf16[2,256,384]{2,1,0:T(8,128)(2,1)}, bf16[2,256,384]{2,1,0:T(8,128)(2,1)S(1)}, u32[]{:S(2)}, u32[]{:S(2)}) %collective-permute-start.10) | collective-permute-done | bytes 393248 | tf_op jit(solution)/shard_map/ppermute | solution.py:21
  72.9 11.5 %shard_map.239 = (bf16[2,64,192]{2,1,0:T(8,128)(2,1)}, bf16[2,64,192]{2,1,0:T(8,128)(2,1)}, bf16[2,64,192]{2,1,0:T(8,128)(2,1)}, bf16[2,64,192]{2,1,0:T(8,128)(2...) custom-call(s32[19]{0:T(128)} %pad_add_fusion.1.meta, bf16[2,256,256]{2,1,0:T(8,128)(2,1)} %get-tuple-element.114.refs_0_, ...), custom_call_target="tpu_custom_call" | custom-call | flops 16106127360 | bytes 1048576 | tf_op jit(solution)/shard_map/pallas_call | solution.py:541
  84.3 3.3 %collective-permute-start.16 = (bf16[2,64,192]{2,1,0:T(8,128)(2,1)}, bf16[2,64,192]{2,1,0:T(8,128)(2,1)S(1)}, u32[]{:S(2)}, u32[]{:S(2)}) collective-permute-start(bf16[2,64,192]{2,1,0:T(8,128)(2,1)} %get-tuple-element.121.refs_11_), channel_id=1, source_target_pairs={{0,1},{1,0},{2,3},{3,2},{4,5},{5,4},{6,7},{7,6},{8,9},{9,8},{10,11... | collective-permute-start | bytes 147464 | tf_op jit(solution)/shard_map/ppermute | solution.py:21
  87.7 2.4 collective-permute-start.18
  91.0 2.4 slice.255.refs_5_.refs_6_
  94.4 5.7 %collective-permute-done.17.refs_2_ = bf16[2,64,192]{2,1,0:T(8,128)(2,1)S(1)} collective-permute-done((bf16[2,64,192]{2,1,0:T(8,128)(2,1)}, bf16[2,64,192]{2,1,0:T(8,128)(2,1)S(1)}, u32[]{:S(2)}, u32[]{:S(2)}) %collective-permute-start.17) | collective-permute-done | bytes 49184 | tf_op jit(solution)/shard_map/ppermute | solution.py:21
  100.7 3.3 %shard_map.240 = (f32[128,768]{1,0:T(8,128)}, bf16[128,768]{1,0:T(8,128)(2,1)}) custom-call(s32[3]{0:T(128)} %pad_add_fusion.meta, bf16[2,64,192]{2,1,0:T(8,128)(2,1)} %get-tuple-element.124.refs_0_.refs_10_, bf16[2,64,192]{2,1,0:T(8,128)(2,1)} %copy-done.33, bf16[2,64,192]{2,1,0:T(8,128)(2,1)} %copy-done.34, bf16[2,64,192]{2,1,0:T(8,128)(2,1)} %copy-done.35, ...), custom_call_target="tpu_custom_call" | custom-call | bytes 1048576 | tf_op jit(solution)/shard_map/pallas_call | solution.py:541
  104.1 1.6 collective-permute-start.21
  107.5 6.5 %all-gather.9.cloned.1.call-done = bf16[768,768]{1,0:T(8,128)(2,1)} async-done(((bf16[192,768]{1,0:T(8,128)(2,1)}), bf16[768,768]{1,0:T(8,128)(2,1)}) %all-gather.9.cloned.1.call-update) | async-done | bytes 1179664 | tf_op jit(solution)/shard_map/all_gather | solution.py:693
  120.2 1.8 convert_reduce_fusion
  123.9 2.3 convolution_convert_fusion.1
  128.2 2.4 collective-permute-start.29
  132.5 3.3 %shard_map.241 = bf16[8,128,768]{2,1,0:T(8,128)(2,1)} custom-call(s32[8]{0:T(128)} %fusion.47.table, bf16[8,128,768]{2,1,0:T(8,128)(2,1)} %bitcast.141), custom_call_target="tpu_custom_call" | custom-call | tf_op jit(solution)/shard_map/pallas_call | solution.py:70
  136.9 3.4 %collective-permute-done.28.refs_2_ = bf16[128,768]{1,0:T(8,128)(2,1)S(1)} collective-permute-done((bf16[128,768]{1,0:T(8,128)(2,1)S(1)}, bf16[128,768]{1,0:T(8,128)(2,1)S(1)}, u32[]{:S(2)}, u32[]{:S(2)}) %collective-permute-start.28) | collective-permute-done | bytes 196640 | tf_op jit(solution)/shard_map/ppermute | solution.py:21
  141.0 4.1 %shard_map.242 = (bf16[2,64,192]{2,1,0:T(8,128)(2,1)}, bf16[2,64,192]{2,1,0:T(8,128)(2,1)}, bf16[2,64,192]{2,1,0:T(8,128)(2,1)}, bf16[2,64,192]{2,1,0:T(8,128)(2...) custom-call(s32[3]{0:T(128)} %pad_add_fusion.meta, ...), custom_call_target="tpu_custom_call" | custom-call | bytes 1048576 | tf_op jit(solution)/shard_map/pallas_call | solution.py:541
  145.2 4.7 %collective-permute-start.30 = (bf16[1,128,768]{2,1,0:T(8,128)(2,1)}, bf16[1,128,768]{2,1,0:T(8,128)(2,1)S(1)}, u32[]{:S(2)}, u32[]{:S(2)}) collective-permute-start(bf16[1,128,768]{2,1,0:T(8,128)(2,1)} %bitcast.156), channel_id=1, source_target_pairs={{0,1},{1,0},{2,3},{3,2},{4,5},{5,4},{6,7},{7,6},{8,9},{9,8},{10,11... | collective-permute-start | bytes 589832 | tf_op jit(solution)/shard_map/ppermute | solution.py:21
  150.4 3.9 %collective-permute-start.33 = (bf16[2,64,192]{2,1,0:T(8,128)(2,1)}, bf16[2,64,192]{2,1,0:T(8,128)(2,1)S(1)}, u32[]{:S(2)}, u32[]{:S(2)}) collective-permute-start(bf16[2,64,192]{2,1,0:T(8,128)(2,1)} %get-tuple-element.149), channel_id=1, source_target_pairs={{0,3},{1,2},{2,1},{3,0},{4,7},{5,6},{6,5},{7,4},{8,11},{9,10},{10,... | collective-permute-start | bytes 147464 | tf_op jit(solution)/shard_map/ppermute | solution.py:21
  154.3 3.5 %collective-permute-done.30 = bf16[1,128,768]{2,1,0:T(8,128)(2,1)S(1)} collective-permute-done((bf16[1,128,768]{2,1,0:T(8,128)(2,1)}, bf16[1,128,768]{2,1,0:T(8,128)(2,1)S(1)}, u32[]{:S(2)}, u32[]{:S(2)}) %collective-permute-start.30) | collective-permute-done | bytes 196640 | tf_op jit(solution)/shard_map/ppermute | solution.py:21
  159.4 2.0 collective-permute-start.34
  161.4 15.9 %shard_map.243 = (bf16[2,256,192]{2,1,0:T(8,128)(2,1)}, bf16[4,2,384,256]{3,2,1,0:T(8,128)(2,1)}, bf16[4,2,384,256]{3,2,1,0:T(8,128)(2,1)}) custom-call(s32[19]{0:T(128)} %pad_add_fusion.1.meta, bf16[2,256,256]{2,1,0:T(8,128)(2,1)} %get-tuple-element.114.refs_0_, bf16[2,256,384]{2,1,0:T(8,128)(2,1)} %get-tuple-element.116.refs_1_, ...), custom_call_target="tpu_custom_call" | custom-call | flops 9663676416 | bytes 1048576 | tf_op jit(solution)/shard_map/pallas_call | solution.py:541
  179.1 3.6 %collective-permute-done.35 = bf16[4,2,384,256]{3,2,1,0:T(8,128)(2,1)S(1)} collective-permute-done((bf16[4,2,384,256]{3,2,1,0:T(8,128)(2,1)}, bf16[4,2,384,256]{3,2,1,0:T(8,128)(2,1)S(1)}, u32[]{:S(2)}, u32[]{:S(2)}) %collective-permute-start.35) | collective-permute-done | bytes 1572896 | tf_op jit(solution)/shard_map/ppermute | solution.py:21
  184.0 1.7 collective-permute-start.38
  187.7 9.4 %collective-permute-done.38.refs_3_ = bf16[2,384,256]{2,1,0:T(8,128)(2,1)S(1)} collective-permute-done((bf16[2,384,256]{2,1,0:T(8,128)(2,1)}, bf16[2,384,256]{2,1,0:T(8,128)(2,1)S(1)}, u32[]{:S(2)}, u32[]{:S(2)}) %collective-permute-start.38) | collective-permute-done | bytes 393248 | tf_op jit(solution)/shard_map/ppermute | solution.py:21
  197.1 7.6 %collective-permute-done.37.refs_2_ = bf16[2,384,256]{2,1,0:T(8,128)(2,1)S(1)} collective-permute-done((bf16[2,384,256]{2,1,0:T(8,128)(2,1)S(1)}, bf16[2,384,256]{2,1,0:T(8,128)(2,1)S(1)}, u32[]{:S(2)}, u32[]{:S(2)}) %collective-permute-start.37) | collective-permute-done | bytes 393248 | tf_op jit(solution)/shard_map/ppermute | solution.py:21
  205.6 6.7 %shard_map.244 = (bf16[2,64,768]{2,1,0:T(8,128)(2,1)}, bf16[2,64,768]{2,1,0:T(8,128)(2,1)}, bf16[2,2,64,768]{3,2,1,0:T(8,128)(2,1)}, bf16[4,5,32,576]{3,2,1,0:T(8,128)(2,1)}, bf16[4,5,32,576]{3,2,1,0:T(8,128)(2,1)}) custom-call(s32[3]{0:T(128)} %pad_add_fusion.meta, bf16[2,384,256]{2,1,0:T(8,128)(2,1)} %get-tuple-element.161.refs_0_, ...), custom_call_target="tpu_custom_call" | custom-call | bytes 1048576 | tf_op jit(solution)/shard_map/pallas_call | solution.py:541
  216.4 2.3 collective-permute-start.43
  220.7 14.3 %collective-permute-done.39 = bf16[2,2,64,768]{3,2,1,0:T(8,128)(2,1)S(1)} collective-permute-done((bf16[2,2,64,768]{3,2,1,0:T(8,128)(2,1)}, bf16[2,2,64,768]{3,2,1,0:T(8,128)(2,1)S(1)}, u32[]{:S(2)}, u32[]{:S(2)}) %collective-permute-start.39) | collective-permute-done | bytes 393248 | tf_op jit(solution)/shard_map/ppermute | solution.py:21
  235.8 1.8 collective-permute-start.47
  237.5 2.6 collective-permute-start.45
  243.7 2.3 shard_map.246
  246.0 1.8 collective-permute-start.50
  250.9 1.6 fusion.51
  252.5 4.4 %fusion.49 = (f32[8,1,96,768]{3,2,1,0:T(8,128)}, f32[8,1,96,768]{3,2,1,0:T(8,128)}) fusion(bf16[8,2,96,768]{3,2,1,0:T(8,128)(2,1)} %bitcast.126), kind=kLoop, calls=%fused_computation.148 | loop fusion | bytes 9437184 | tf_op jit(solution)/shard_map/slice | solution.py:834
  258.7 2.9 %shard_map.245 = f32[128,768]{1,0:T(8,128)} custom-call(s32[3]{0:T(128)} %pad_add_fusion.meta, bf16[2,64,768]{2,1,0:T(8,128)(2,1)} %fusion.11.grad_ref, bf16[128,768]{1,0:T(8,128)(2,1)} %bitcast.134, f32[1,768]{1,0:T(1,128)} %reshape.206.gain_ref, f32[128,768]{1,0:T(8,128)} %get-tuple-element.176.resid_grad_ref), custom_call_target="tpu_custom_call" | custom-call | bytes 1048576 | tf_op jit(solution)/shard_map/pallas_call | solution.py:541
  263.1 3.5 %shard_map.247 = (f32[192,2304]{1,0:T(8,128)}, f32[192,768]{1,0:T(8,128)}) custom-call(s32[3]{0:T(128)} %pad_add_fusion.meta, bf16[24,3072]{1,0:T(8,128)(2,1)} %get-tuple-element.191.refs_0_, bf16[24,3072]{1,0:T(8,128)(2,1)} %copy-done.28, bf16[24,3072]{1,0:T(8,128)(2,1)} %copy-done.27, bf16[24,3072]{1,0:T(8,128)(2,1)} %copy-done.26, ...), custom_call_target="tpu_custom_call" | custom-call | bytes 1048576 | tf_op jit(solution)/shard_map/pallas_call | solution.py:541
  (292 shorter events, 58.0 us)
Async XLA Ops:
  7.2 47.7 %all-gather.7.cloned.1.call-start = ((), (), s32[]{:S(2)}) async-start(), calls=%async_computation.3 | async-start | bytes 1769472 | tf_op jit(solution)/shard_map/all_gather | solution.py:665
  7.9 82.2 %all-gather.5.cloned.1.call-start = ((), (), s32[]{:S(2)}) async-start(), calls=%async_computation.2 | async-start | bytes 1597440 | tf_op jit(solution)/shard_map/all_gather | solution.py:673
  9.9 5.7 %collective-permute-start = (bf16[64,576]{1,0:T(8,128)(2,1)S(1)}, bf16[64,576]{1,0:T(8,128)(2,1)S(1)}, u32[]{:S(2)}, u32[]{:S(2)}) collective-permute-start(bf16[64,576]{1,0:T(8,128)(2,1)S(1)} %get-tuple-element.226), channel_id=1, source_target_pairs={{0,1},{1,0},{2,3},{3,2},{4,5},{5,4},{6,7},{7,6},{8,9},{9,8},{10,11... | collective-permute-start | bytes 221192 | tf_op jit(solution)/shard_map/ppermute | solution.py:21
  13.0 9.2 %collective-permute-start.1 = (bf16[64,576]{1,0:T(8,128)(2,1)S(1)}, bf16[64,576]{1,0:T(8,128)(2,1)S(1)}, u32[]{:S(2)}, u32[]{:S(2)}) collective-permute-start(bf16[64,576]{1,0:T(8,128)(2,1)S(1)} %get-tuple-element.227), channel_id=1, source_target_pairs={{0,2},{1,3},{2,0},{3,1},{4,6},{5,7},{6,4},{7,5},{8,10},{9,11},{10,... | collective-permute-start | bytes 221192 | tf_op jit(solution)/shard_map/ppermute | solution.py:21
  15.6 6.6 %collective-permute-start.2 = (bf16[64,576]{1,0:T(8,128)(2,1)S(1)}, bf16[64,576]{1,0:T(8,128)(2,1)S(1)}, u32[]{:S(2)}, u32[]{:S(2)}) collective-permute-start(bf16[64,576]{1,0:T(8,128)(2,1)S(1)} %get-tuple-element.228), channel_id=1, source_target_pairs={{0,3},{1,2},{2,1},{3,0},{4,7},{5,6},{6,5},{7,4},{8,11},{9,10},{10,... | collective-permute-start | bytes 221192 | tf_op jit(solution)/shard_map/ppermute | solution.py:21
  22.3 9.6 %collective-permute-start.5 = (bf16[2,64,768]{2,1,0:T(8,128)(2,1)S(1)}, bf16[2,64,768]{2,1,0:T(8,128)(2,1)S(1)}, u32[]{:S(2)}, u32[]{:S(2)}) collective-permute-start(bf16[2,64,768]{2,1,0:T(8,128)(2,1)S(1)} %bitcast.135), channel_id=1, source_target_pairs={{0,3},{1,2},{2,1},{3,0},{4,7},{5,6},{6,5},{7,4},{8,11},{9,10},{10,... | collective-permute-start | bytes 589832 | tf_op jit(solution)/shard_map/ppermute | solution.py:21
  25.0 16.5 %collective-permute-start.4 = (bf16[2,64,768]{2,1,0:T(8,128)(2,1)S(1)}, bf16[2,64,768]{2,1,0:T(8,128)(2,1)S(1)}, u32[]{:S(2)}, u32[]{:S(2)}) collective-permute-start(bf16[2,64,768]{2,1,0:T(8,128)(2,1)S(1)} %bitcast.136), channel_id=1, source_target_pairs={{0,2},{1,3},{2,0},{3,1},{4,6},{5,7},{6,4},{7,5},{8,10},{9,11},{10,... | collective-permute-start | bytes 589832 | tf_op jit(solution)/shard_map/ppermute | solution.py:21
  25.5 16.0 %collective-permute-start.3 = (bf16[2,64,768]{2,1,0:T(8,128)(2,1)S(1)}, bf16[2,64,768]{2,1,0:T(8,128)(2,1)S(1)}, u32[]{:S(2)}, u32[]{:S(2)}) collective-permute-start(bf16[2,64,768]{2,1,0:T(8,128)(2,1)S(1)} %bitcast.137), channel_id=1, source_target_pairs={{0,1},{1,0},{2,3},{3,2},{4,5},{5,4},{6,7},{7,6},{8,9},{9,8},{10,11... | collective-permute-start | bytes 589832 | tf_op jit(solution)/shard_map/ppermute | solution.py:21
  27.0 14.5 %collective-permute-start.8 = (bf16[4,48,576]{2,1,0:T(8,128)(2,1)S(1)}, bf16[4,48,576]{2,1,0:T(8,128)(2,1)S(1)}, u32[]{:S(2)}, u32[]{:S(2)}) collective-permute-start(bf16[4,48,576]{2,1,0:T(8,128)(2,1)S(1)} %slice.254.refs_5_), channel_id=1, source_target_pairs={{0,24},{4,28},{8,16},{12,20},{16,8},{20,12},{24,0},{28,4},{1,25},{... | collective-permute-start | bytes 663560 | tf_op jit(solution)/shard_map/ppermute | solution.py:21
  29.4 12.8 %collective-permute-start.7 = (bf16[4,48,576]{2,1,0:T(8,128)(2,1)S(1)}, bf16[4,48,576]{2,1,0:T(8,128)(2,1)S(1)}, u32[]{:S(2)}, u32[]{:S(2)}) collective-permute-start(bf16[4,48,576]{2,1,0:T(8,128)(2,1)S(1)} %slice.254.refs_5_), channel_id=1, source_target_pairs={{0,16},{4,20},{8,24},{12,28},{16,0},{20,4},{24,8},{28,12},{1,17},{... | collective-permute-start | bytes 663560 | tf_op jit(solution)/shard_map/ppermute | solution.py:21
  31.9 10.5 %collective-permute-start.6 = (bf16[4,48,576]{2,1,0:T(8,128)(2,1)S(1)}, bf16[4,48,576]{2,1,0:T(8,128)(2,1)S(1)}, u32[]{:S(2)}, u32[]{:S(2)}) collective-permute-start(bf16[4,48,576]{2,1,0:T(8,128)(2,1)S(1)} %slice.254.refs_5_), channel_id=1, source_target_pairs={{0,8},{4,12},{8,0},{12,4},{16,24},{20,28},{24,16},{28,20},{1,9},{5... | collective-permute-start | bytes 663560 | tf_op jit(solution)/shard_map/ppermute | solution.py:21
  42.4 71.7 %all-gather.9.cloned.1.call-start = ((), (), s32[]{:S(2)}) async-start(), calls=%async_computation.4 | async-start | bytes 1474560 | tf_op jit(solution)/shard_map/all_gather | solution.py:693
  48.7 13.2 %collective-permute-start.11 = (bf16[2,256,384]{2,1,0:T(8,128)(2,1)}, bf16[2,256,384]{2,1,0:T(8,128)(2,1)S(1)}, u32[]{:S(2)}, u32[]{:S(2)}) collective-permute-start(bf16[2,256,384]{2,1,0:T(8,128)(2,1)} %get-tuple-element.116.refs_1_), channel_id=1, source_target_pairs={{0,24},{4,28},{8,16},{12,20},{16,8},{20,12},{24,0},{28,4},{1,25},{... | collective-permute-start | bytes 1179656 | tf_op jit(solution)/shard_map/ppermute | solution.py:21
  50.5 18.1 %collective-permute-start.10 = (bf16[2,256,384]{2,1,0:T(8,128)(2,1)}, bf16[2,256,384]{2,1,0:T(8,128)(2,1)S(1)}, u32[]{:S(2)}, u32[]{:S(2)}) collective-permute-start(bf16[2,256,384]{2,1,0:T(8,128)(2,1)} %get-tuple-element.116.refs_1_), channel_id=1, source_target_pairs={{0,16},{4,20},{8,24},{12,28},{16,0},{20,4},{24,8},{28,12},{1,17},{... | collective-permute-start | bytes 1179656 | tf_op jit(solution)/shard_map/ppermute | solution.py:21
  51.7 17.0 %collective-permute-start.9 = (bf16[2,256,384]{2,1,0:T(8,128)(2,1)}, bf16[2,256,384]{2,1,0:T(8,128)(2,1)S(1)}, u32[]{:S(2)}, u32[]{:S(2)}) collective-permute-start(bf16[2,256,384]{2,1,0:T(8,128)(2,1)} %get-tuple-element.116.refs_1_), channel_id=1, source_target_pairs={{0,8},{4,12},{8,0},{12,4},{16,24},{20,28},{24,16},{28,20},{1,9},{5... | collective-permute-start | bytes 1179656 | tf_op jit(solution)/shard_map/ppermute | solution.py:21
  69.9 117.9 %reduce-scatter.3.cloned.1.call-start = ((), (), s32[]{:S(2)}) async-start(), calls=%async_computation.5 | async-start | bytes 1769472 | tf_op jit(solution)/shard_map/reduce_scatter | solution.py:738
  84.3 10.1 %collective-permute-start.16 = (bf16[2,64,192]{2,1,0:T(8,128)(2,1)}, bf16[2,64,192]{2,1,0:T(8,128)(2,1)S(1)}, u32[]{:S(2)}, u32[]{:S(2)}) collective-permute-start(bf16[2,64,192]{2,1,0:T(8,128)(2,1)} %get-tuple-element.121.refs_11_), channel_id=1, source_target_pairs={{0,1},{1,0},{2,3},{3,2},{4,5},{5,4},{6,7},{7,6},{8,9},{9,8},{10,11... | collective-permute-start | bytes 147464 | tf_op jit(solution)/shard_map/ppermute | solution.py:21
  87.7 12.4 %collective-permute-start.17 = (bf16[2,64,192]{2,1,0:T(8,128)(2,1)}, bf16[2,64,192]{2,1,0:T(8,128)(2,1)S(1)}, u32[]{:S(2)}, u32[]{:S(2)}) collective-permute-start(bf16[2,64,192]{2,1,0:T(8,128)(2,1)} %get-tuple-element.122.refs_12_), channel_id=1, source_target_pairs={{0,2},{1,3},{2,0},{3,1},{4,6},{5,7},{6,4},{7,5},{8,10},{9,11},{10,... | collective-permute-start | bytes 147464 | tf_op jit(solution)/shard_map/ppermute | solution.py:21
  87.7 12.4 %collective-permute-start.18 = (bf16[2,64,192]{2,1,0:T(8,128)(2,1)}, bf16[2,64,192]{2,1,0:T(8,128)(2,1)S(1)}, u32[]{:S(2)}, u32[]{:S(2)}) collective-permute-start(bf16[2,64,192]{2,1,0:T(8,128)(2,1)} %get-tuple-element.123.refs_13_), channel_id=1, source_target_pairs={{0,3},{1,2},{2,1},{3,0},{4,7},{5,6},{6,5},{7,4},{8,11},{9,10},{10,... | collective-permute-start | bytes 147464 | tf_op jit(solution)/shard_map/ppermute | solution.py:21
  104.1 12.3 %collective-permute-start.21 = (bf16[128,768]{1,0:T(8,128)(2,1)}, bf16[128,768]{1,0:T(8,128)(2,1)S(1)}, u32[]{:S(2)}, u32[]{:S(2)}) collective-permute-start(bf16[128,768]{1,0:T(8,128)(2,1)} %get-tuple-element.133), channel_id=1, source_target_pairs={{0,24},{4,28},{8,16},{12,20},{16,8},{20,12},{24,0},{28,4},{1,25},{... | collective-permute-start | bytes 589832 | tf_op jit(solution)/shard_map/ppermute | solution.py:21
  105.7 10.7 %collective-permute-start.20 = (bf16[128,768]{1,0:T(8,128)(2,1)}, bf16[128,768]{1,0:T(8,128)(2,1)S(1)}, u32[]{:S(2)}, u32[]{:S(2)}) collective-permute-start(bf16[128,768]{1,0:T(8,128)(2,1)} %get-tuple-element.133), channel_id=1, source_target_pairs={{0,16},{4,20},{8,24},{12,28},{16,0},{20,4},{24,8},{28,12},{1,17},{... | collective-permute-start | bytes 589832 | tf_op jit(solution)/shard_map/ppermute | solution.py:21
  107.0 9.4 %collective-permute-start.19 = (bf16[128,768]{1,0:T(8,128)(2,1)}, bf16[128,768]{1,0:T(8,128)(2,1)S(1)}, u32[]{:S(2)}, u32[]{:S(2)}) collective-permute-start(bf16[128,768]{1,0:T(8,128)(2,1)} %get-tuple-element.133), channel_id=1, source_target_pairs={{0,8},{4,12},{8,0},{12,4},{16,24},{20,28},{24,16},{28,20},{1,9},{5... | collective-permute-start | bytes 589832 | tf_op jit(solution)/shard_map/ppermute | solution.py:21
  128.2 8.8 %collective-permute-start.29 = (bf16[128,768]{1,0:T(8,128)(2,1)S(1)}, bf16[128,768]{1,0:T(8,128)(2,1)S(1)}, u32[]{:S(2)}, u32[]{:S(2)}) collective-permute-start(bf16[128,768]{1,0:T(8,128)(2,1)S(1)} %get-tuple-element.215), channel_id=1, source_target_pairs={{0,24},{4,28},{8,16},{12,20},{16,8},{20,12},{24,0},{28,4},{1,25},{... | collective-permute-start | bytes 589832 | tf_op jit(solution)/shard_map/ppermute | solution.py:21
  130.5 9.8 %collective-permute-start.28 = (bf16[128,768]{1,0:T(8,128)(2,1)S(1)}, bf16[128,768]{1,0:T(8,128)(2,1)S(1)}, u32[]{:S(2)}, u32[]{:S(2)}) collective-permute-start(bf16[128,768]{1,0:T(8,128)(2,1)S(1)} %get-tuple-element.216), channel_id=1, source_target_pairs={{0,16},{4,20},{8,24},{12,28},{16,0},{20,4},{24,8},{28,12},{1,17},{... | collective-permute-start | bytes 589832 | tf_op jit(solution)/shard_map/ppermute | solution.py:21
  131.1 9.3 %collective-permute-start.27 = (bf16[128,768]{1,0:T(8,128)(2,1)S(1)}, bf16[128,768]{1,0:T(8,128)(2,1)S(1)}, u32[]{:S(2)}, u32[]{:S(2)}) collective-permute-start(bf16[128,768]{1,0:T(8,128)(2,1)S(1)} %get-tuple-element.217), channel_id=1, source_target_pairs={{0,8},{4,12},{8,0},{12,4},{16,24},{20,28},{24,16},{28,20},{1,9},{5... | collective-permute-start | bytes 589832 | tf_op jit(solution)/shard_map/ppermute | solution.py:21
  140.4 71.9 %reduce-scatter.5.cloned.1.call-start = ((), (), s32[]{:S(2)}) async-start(), calls=%async_computation.6 | async-start | bytes 1474560 | tf_op jit(solution)/shard_map/reduce_scatter | solution.py:767
  145.2 12.6 %collective-permute-start.30 = (bf16[1,128,768]{2,1,0:T(8,128)(2,1)}, bf16[1,128,768]{2,1,0:T(8,128)(2,1)S(1)}, u32[]{:S(2)}, u32[]{:S(2)}) collective-permute-start(bf16[1,128,768]{2,1,0:T(8,128)(2,1)} %bitcast.156), channel_id=1, source_target_pairs={{0,1},{1,0},{2,3},{3,2},{4,5},{5,4},{6,7},{7,6},{8,9},{9,8},{10,11... | collective-permute-start | bytes 589832 | tf_op jit(solution)/shard_map/ppermute | solution.py:21
  149.9 9.5 %collective-permute-start.31 = (bf16[2,64,192]{2,1,0:T(8,128)(2,1)}, bf16[2,64,192]{2,1,0:T(8,128)(2,1)S(1)}, u32[]{:S(2)}, u32[]{:S(2)}) collective-permute-start(bf16[2,64,192]{2,1,0:T(8,128)(2,1)} %get-tuple-element.147), channel_id=1, source_target_pairs={{0,1},{1,0},{2,3},{3,2},{4,5},{5,4},{6,7},{7,6},{8,9},{9,8},{10,11... | collective-permute-start | bytes 147464 | tf_op jit(solution)/shard_map/ppermute | solution.py:21
  150.0 9.4 %collective-permute-start.32 = (bf16[2,64,192]{2,1,0:T(8,128)(2,1)}, bf16[2,64,192]{2,1,0:T(8,128)(2,1)S(1)}, u32[]{:S(2)}, u32[]{:S(2)}) collective-permute-start(bf16[2,64,192]{2,1,0:T(8,128)(2,1)} %get-tuple-element.148), channel_id=1, source_target_pairs={{0,2},{1,3},{2,0},{3,1},{4,6},{5,7},{6,4},{7,5},{8,10},{9,11},{10,... | collective-permute-start | bytes 147464 | tf_op jit(solution)/shard_map/ppermute | solution.py:21
  150.4 9.1 %collective-permute-start.33 = (bf16[2,64,192]{2,1,0:T(8,128)(2,1)}, bf16[2,64,192]{2,1,0:T(8,128)(2,1)S(1)}, u32[]{:S(2)}, u32[]{:S(2)}) collective-permute-start(bf16[2,64,192]{2,1,0:T(8,128)(2,1)} %get-tuple-element.149), channel_id=1, source_target_pairs={{0,3},{1,2},{2,1},{3,0},{4,7},{5,6},{6,5},{7,4},{8,11},{9,10},{10,... | collective-permute-start | bytes 147464 | tf_op jit(solution)/shard_map/ppermute | solution.py:21
  159.4 19.2 %collective-permute-start.34 = (bf16[2,128,768]{2,1,0:T(8,128)(2,1)S(1)}, bf16[2,128,768]{2,1,0:T(8,128)(2,1)S(1)}, u32[]{:S(2)}, u32[]{:S(2)}) collective-permute-start(bf16[2,128,768]{2,1,0:T(8,128)(2,1)S(1)} %pad_maximum_fusion.1), channel_id=1, source_target_pairs={{0,2},{1,3},{2,0},{3,1},{4,6},{5,7},{6,4},{7,5},{8,10},{9,11},{10,... | collective-permute-start | bytes 1179656 | tf_op jit(solution)/shard_map/ppermute | solution.py:21
  178.7 73.8 %all-gather.11.cloned.1.call-start = ((), (), s32[]{:S(2)}) async-start(), calls=%async_computation.7 | async-start | bytes 2654208 | tf_op jit(solution)/shard_map/all_gather | solution.py:793
  184.0 13.1 %collective-permute-start.38 = (bf16[2,384,256]{2,1,0:T(8,128)(2,1)}, bf16[2,384,256]{2,1,0:T(8,128)(2,1)S(1)}, u32[]{:S(2)}, u32[]{:S(2)}) collective-permute-start(bf16[2,384,256]{2,1,0:T(8,128)(2,1)} %get-tuple-element.209), channel_id=1, source_target_pairs={{0,24},{4,28},{8,16},{12,20},{16,8},{20,12},{24,0},{28,4},{1,25},{... | collective-permute-start | bytes 1179656 | tf_op jit(solution)/shard_map/ppermute | solution.py:21
  185.7 19.0 %collective-permute-start.37 = (bf16[2,384,256]{2,1,0:T(8,128)(2,1)S(1)}, bf16[2,384,256]{2,1,0:T(8,128)(2,1)S(1)}, u32[]{:S(2)}, u32[]{:S(2)}) collective-permute-start(bf16[2,384,256]{2,1,0:T(8,128)(2,1)S(1)} %get-tuple-element.210), channel_id=1, source_target_pairs={{0,16},{4,20},{8,24},{12,28},{16,0},{20,4},{24,8},{28,12},{1,17},{... | collective-permute-start | bytes 1179656 | tf_op jit(solution)/shard_map/ppermute | solution.py:21
  186.8 17.9 %collective-permute-start.36 = (bf16[2,384,256]{2,1,0:T(8,128)(2,1)S(1)}, bf16[2,384,256]{2,1,0:T(8,128)(2,1)S(1)}, u32[]{:S(2)}, u32[]{:S(2)}) collective-permute-start(bf16[2,384,256]{2,1,0:T(8,128)(2,1)S(1)} %get-tuple-element.211), channel_id=1, source_target_pairs={{0,8},{4,12},{8,0},{12,4},{16,24},{20,28},{24,16},{28,20},{1,9},{5... | collective-permute-start | bytes 1179656 | tf_op jit(solution)/shard_map/ppermute | solution.py:21
  214.0 21.0 %collective-permute-start.39 = (bf16[2,2,64,768]{3,2,1,0:T(8,128)(2,1)}, bf16[2,2,64,768]{3,2,1,0:T(8,128)(2,1)S(1)}, u32[]{:S(2)}, u32[]{:S(2)}) collective-permute-start(bf16[2,2,64,768]{3,2,1,0:T(8,128)(2,1)} %get-tuple-element.171), channel_id=1, source_target_pairs={{0,2},{1,3},{2,0},{3,1},{4,6},{5,7},{6,4},{7,5},{8,10},{9,11},{10,... | collective-permute-start | bytes 1179656 | tf_op jit(solution)/shard_map/ppermute | solution.py:21
  216.4 18.6 %collective-permute-start.43 = (bf16[5,32,576]{2,1,0:T(8,128)(2,1)S(1)}, bf16[5,32,576]{2,1,0:T(8,128)(2,1)S(1)}, u32[]{:S(2)}, u32[]{:S(2)}) collective-permute-start(bf16[5,32,576]{2,1,0:T(8,128)(2,1)S(1)} %get-tuple-element.219), channel_id=1, source_target_pairs={{0,24},{4,28},{8,16},{12,20},{16,8},{20,12},{24,0},{28,4},{1,25},{... | collective-permute-start | bytes 552968 | tf_op jit(solution)/shard_map/ppermute | solution.py:21
  218.7 16.3 %collective-permute-start.42 = (bf16[5,32,576]{2,1,0:T(8,128)(2,1)S(1)}, bf16[5,32,576]{2,1,0:T(8,128)(2,1)S(1)}, u32[]{:S(2)}, u32[]{:S(2)}) collective-permute-start(bf16[5,32,576]{2,1,0:T(8,128)(2,1)S(1)} %get-tuple-element.220), channel_id=1, source_target_pairs={{0,16},{4,20},{8,24},{12,28},{16,0},{20,4},{24,8},{28,12},{1,17},{... | collective-permute-start | bytes 552968 | tf_op jit(solution)/shard_map/ppermute | solution.py:21
  219.3 15.7 %collective-permute-start.41 = (bf16[5,32,576]{2,1,0:T(8,128)(2,1)S(1)}, bf16[5,32,576]{2,1,0:T(8,128)(2,1)S(1)}, u32[]{:S(2)}, u32[]{:S(2)}) collective-permute-start(bf16[5,32,576]{2,1,0:T(8,128)(2,1)S(1)} %get-tuple-element.221), channel_id=1, source_target_pairs={{0,8},{4,12},{8,0},{12,4},{16,24},{20,28},{24,16},{28,20},{1,9},{5... | collective-permute-start | bytes 552968 | tf_op jit(solution)/shard_map/ppermute | solution.py:21
  235.8 5.8 %collective-permute-start.47 = (bf16[32,576]{1,0:T(8,128)(2,1)S(1)}, bf16[32,576]{1,0:T(8,128)(2,1)S(1)}, u32[]{:S(2)}, u32[]{:S(2)}) collective-permute-start(bf16[32,576]{1,0:T(8,128)(2,1)S(1)} %get-tuple-element.233), channel_id=1, source_target_pairs={{0,3},{1,2},{2,1},{3,0},{4,7},{5,6},{6,5},{7,4},{8,11},{9,10},{10,... | collective-permute-start | bytes 110600 | tf_op jit(solution)/shard_map/ppermute | solution.py:21
  237.5 5.1 %collective-permute-start.46 = (bf16[32,576]{1,0:T(8,128)(2,1)S(1)}, bf16[32,576]{1,0:T(8,128)(2,1)S(1)}, u32[]{:S(2)}, u32[]{:S(2)}) collective-permute-start(bf16[32,576]{1,0:T(8,128)(2,1)S(1)} %get-tuple-element.234), channel_id=1, source_target_pairs={{0,2},{1,3},{2,0},{3,1},{4,6},{5,7},{6,4},{7,5},{8,10},{9,11},{10,... | collective-permute-start | bytes 110600 | tf_op jit(solution)/shard_map/ppermute | solution.py:21
  237.5 5.5 %collective-permute-start.45 = (bf16[32,576]{1,0:T(8,128)(2,1)S(1)}, bf16[32,576]{1,0:T(8,128)(2,1)S(1)}, u32[]{:S(2)}, u32[]{:S(2)}) collective-permute-start(bf16[32,576]{1,0:T(8,128)(2,1)S(1)} %get-tuple-element.235), channel_id=1, source_target_pairs={{0,1},{1,0},{2,3},{3,2},{4,5},{5,4},{6,7},{7,6},{8,9},{9,8},{10,11... | collective-permute-start | bytes 110600 | tf_op jit(solution)/shard_map/ppermute | solution.py:21
  240.2 17.8 %collective-permute-start.44 = (bf16[1,2,64,768]{3,2,1,0:T(8,128)(2,1)S(1)}, bf16[1,2,64,768]{3,2,1,0:T(8,128)(2,1)S(1)}, u32[]{:S(2)}, u32[]{:S(2)}) collective-permute-start(bf16[1,2,64,768]{3,2,1,0:T(8,128)(2,1)S(1)} %fusion.22), channel_id=1, source_target_pairs={{0,1},{1,0},{2,3},{3,2},{4,5},{5,4},{6,7},{7,6},{8,9},{9,8},{10,11... | collective-permute-start | bytes 589832 | tf_op jit(solution)/shard_map/ppermute | solution.py:21
  246.0 10.9 %collective-permute-start.50 = (bf16[24,3072]{1,0:T(8,128)(2,1)}, bf16[24,3072]{1,0:T(8,128)(2,1)S(1)}, u32[]{:S(2)}, u32[]{:S(2)}) collective-permute-start(bf16[24,3072]{1,0:T(8,128)(2,1)} %get-tuple-element.191.refs_0_), channel_id=1, source_target_pairs={{0,24},{4,28},{8,16},{12,20},{16,8},{20,12},{24,0},{28,4},{1,25},{... | collective-permute-start | bytes 442376 | tf_op jit(solution)/shard_map/ppermute | solution.py:21
  247.8 9.1 %collective-permute-start.49 = (bf16[24,3072]{1,0:T(8,128)(2,1)}, bf16[24,3072]{1,0:T(8,128)(2,1)S(1)}, u32[]{:S(2)}, u32[]{:S(2)}) collective-permute-start(bf16[24,3072]{1,0:T(8,128)(2,1)} %get-tuple-element.191.refs_0_), channel_id=1, source_target_pairs={{0,16},{4,20},{8,24},{12,28},{16,0},{20,4},{24,8},{28,12},{1,17},{... | collective-permute-start | bytes 442376 | tf_op jit(solution)/shard_map/ppermute | solution.py:21
  248.8 8.1 %collective-permute-start.48 = (bf16[24,3072]{1,0:T(8,128)(2,1)}, bf16[24,3072]{1,0:T(8,128)(2,1)S(1)}, u32[]{:S(2)}, u32[]{:S(2)}) collective-permute-start(bf16[24,3072]{1,0:T(8,128)(2,1)} %get-tuple-element.191.refs_0_), channel_id=1, source_target_pairs={{0,8},{4,12},{8,0},{12,4},{16,24},{20,28},{24,16},{28,20},{1,9},{5... | collective-permute-start | bytes 442376 | tf_op jit(solution)/shard_map/ppermute | solution.py:21
  256.9 4.8 %collective-permute-start.51 = (bf16[24,3072]{1,0:T(8,128)(2,1)S(1)}, bf16[24,3072]{1,0:T(8,128)(2,1)S(1)}, u32[]{:S(2)}, u32[]{:S(2)}) collective-permute-start(bf16[24,3072]{1,0:T(8,128)(2,1)S(1)} %copy-done.25), channel_id=1, source_target_pairs={{0,4},{4,0},{8,12},{12,8},{16,20},{20,16},{24,28},{28,24},{1,5},{5... | collective-permute-start | bytes 442376 | tf_op jit(solution)/shard_map/ppermute | solution.py:21
  257.0 4.7 %collective-permute-start.52 = (bf16[24,3072]{1,0:T(8,128)(2,1)S(1)}, bf16[24,3072]{1,0:T(8,128)(2,1)S(1)}, u32[]{:S(2)}, u32[]{:S(2)}) collective-permute-start(bf16[24,3072]{1,0:T(8,128)(2,1)S(1)} %collective-permute-done.48.refs_1_), channel_id=1, source_target_pairs={{0,4},{4,0},{8,12},{12,8},{16,20},{20,16},{24,28},{28,24},{1,5},{5... | collective-permute-start | bytes 442376 | tf_op jit(solution)/shard_map/ppermute | solution.py:21
  (71 other events, 405.6 us)
Sparse Core Ops, SparseCore 0:
  9.9 33.3 all-gather.6
  45.5 31.6 all-gather.4
  78.7 35.2 all-gather.8
  140.5 40.0 reduce-scatter.2
  182.8 29.2 reduce-scatter.4
  213.8 31.9 all-gather.10
